TPU v7x, 128 devices: a whole 4x4x4 slice. The times are simulated.
128 devices in a mesh: rows: 8 (over y, core), cols: 16 (over x, z).
Axes of the slice: x: 4, y: 4, z: 4, core: 2. Of those that a mesh axis runs over, the one named last changes fastest.
Arguments:
- lot_features: bfloat16 [16384, 512], P(('rows', 'cols')), may hold values from -60 to 60
- slot_features: bfloat16 [16384, 512], P(('cols', 'rows')), may hold values from -60 to 60
- lot_mass: float32 [16384], P('rows'), may hold values from 0.5 to 2
- slot_mass: float32 [16384], P('cols'), may hold values from 0.5 to 2
Outputs:
- lot_grad: float32 [16384, 512], P(('rows', 'cols'))
All inputs are finite; a program needn't handle non-finite values.
Results may differ from a plain program's by a relative error of at most 0.0034.
Values may be sent and summed in bfloat16 or wider, within the bound.
No kernel may reach another device: no remote copies, remote signals or barrier semaphores. Data moves between devices by JAX's collectives and lax.ppermute only.
A program may use at most 64 MiB of HBM per device.

v0:
```python
import jax
import jax.numpy as jnp
from jax import lax
from jax.sharding import PartitionSpec as P

ITERS = 3


EPS = 1.0


def combined_all(value, axis, join):
    pieces = jax.tree.map(lambda part: lax.all_gather(part, axis), value)
    head = jax.tree.map(lambda part: part[0], pieces)
    tail = jax.tree.map(lambda part: part[1:], pieces)
    total, _ = lax.scan(lambda total, share: (join(total, share), None), head, tail)
    return total


def combine(first, second):
    top = jnp.maximum(first[0], second[0])
    return (top, first[1] * jnp.exp(first[0] - top) + second[1] * jnp.exp(second[0] - top))


def local(lot_features, slot_features, lot_mass, slot_mass):
    lot_full = lax.all_gather(lot_features, "cols", axis=0, tiled=True)
    slot_full = lax.all_gather(slot_features, "rows", axis=0, tiled=True)
    width = lot_full.shape[1]
    lot_sq = jnp.sum(lot_full.astype(jnp.float32) ** 2, axis=1)
    slot_sq = jnp.sum(slot_full.astype(jnp.float32) ** 2, axis=1)
    cost_scale = 0.5 / width**0.5

    def make_tile():
        inner = lax.dot_general(
            lot_full, slot_full, (((1,), (1,)), ((), ())), preferred_element_type=jnp.float32
        )
        return (lot_sq[:, None] + slot_sq[None, :] - 2.0 * inner) * cost_scale

    def get_tile():
        return make_tile()

    log_lot = jnp.log(lot_mass)
    log_slot = jnp.log(slot_mass)
    slot_pot = jnp.zeros(slot_mass.shape, jnp.float32)
    lot_pot = jnp.zeros(lot_mass.shape, jnp.float32)
    for step in range(ITERS):
        scores = (slot_pot[None, :] - get_tile()) / EPS
        peaks = jnp.max(scores, axis=1)
        totals = jnp.sum(jnp.exp(scores - peaks[:, None]), axis=1)
        peaks, totals = combined_all((peaks, totals), "cols", combine)
        lot_pot = EPS * log_lot - EPS * (peaks + jnp.log(totals))
        scores = (lot_pot[:, None] - get_tile()) / EPS
        peaks = jnp.max(scores, axis=0)
        totals = jnp.sum(jnp.exp(scores - peaks[None, :]), axis=0)
        peaks, totals = combined_all((peaks, totals), "rows", combine)
        slot_pot = EPS * log_slot - EPS * (peaks + jnp.log(totals))
    plan = jnp.exp((lot_pot[:, None] + slot_pot[None, :] - get_tile()) / EPS)
    row_total = jnp.sum(plan, axis=1)
    moved = jnp.dot(plan.astype(jnp.bfloat16), slot_full, preferred_element_type=jnp.float32)
    own_rows = lot_features.shape[0]
    own_start = lax.axis_index("cols") * own_rows
    moved_sum, row_sum = lax.psum((moved, row_total), "cols")
    gradient = row_sum[:, None] * lot_full.astype(jnp.float32) - moved_sum
    return lax.dynamic_slice_in_dim(gradient, own_start, own_rows, 0)


def solution(mesh):
    placed = (P(("rows", "cols"), None), P(("cols", "rows"), None), P("rows"), P("cols"))
    return jax.shard_map(
        local, mesh=mesh, in_specs=placed, out_specs=P(("rows", "cols"), None), check_vma=False
    )
```

profile of v0, /device:TPU:1, one launch (start us, length us, event | category | flops | bytes accessed | tf_op | source)
XLA Modules:
  0.0 469.2 jit_solution(8574434106292164887)
XLA Ops:
  6.5 0.7 all-gather.17.cloned.1.call-update
  7.3 0.0 all-gather.15.cloned.1.call-start
  7.3 0.7 all-gather.15.cloned.1.call-update
  8.0 0.0 all-reduce.2.cloned.1.call-start
  8.1 28.1 %all-gather.17.cloned.1.call-done = bf16[1024,512]{1,0:T(8,128)(2,1)} async-done(((bf16[128,512]{1,0:T(8,128)(2,1)}), bf16[1024,512]{1,0:T(8,128)(2,1)}) %all-gather.17.cloned.1.call-update) | async-done | bytes 1048592 | tf_op jit(solution)/shard_map/all_gather | solution.py:27
  36.1 1.5 multiply_reduce_fusion.1
  37.6 44.3 %all-gather.15.cloned.1.call-done = bf16[2048,512]{1,0:T(8,128)(2,1)} async-done(((bf16[128,512]{1,0:T(8,128)(2,1)}), bf16[2048,512]{1,0:T(8,128)(2,1)}) %all-gather.15.cloned.1.call-update) | async-done | bytes 2097168 | tf_op jit(solution)/shard_map/all_gather | solution.py:26
  81.9 2.1 multiply_reduce_fusion
  84.0 4.4 subtract_reduce_fusion.5
  88.4 3.2 copy-done
  91.6 1.4 exponential_reduce_fusion.5
  93.0 17.5 %all-gather.1 = f32[32768]{0:T(1024)S(1)} all-gather(f32[2048]{0:T(1024)S(1)} %exponential_reduce_fusion.5), channel_id=3, replica_groups=mesh['rows'=8,'cols'=16] {'cols'}, dimensions={0}, use_global_device_ids=true | all-gather | bytes 139264 | tf_op jit(solution)/shard_map/all_gather | solution.py:13
  110.5 16.2 %all-gather = f32[32768]{0:T(1024)S(1)} all-gather(f32[2048]{0:T(1024)S(1)} %get-tuple-element.269), channel_id=2, replica_groups=mesh['rows'=8,'cols'=16] {'cols'}, dimensions={0}, use_global_device_ids=true | all-gather | bytes 139264 | tf_op jit(solution)/shard_map/all_gather | solution.py:13
  126.8 0.9 while.72
  127.8 4.2 subtract_reduce_fusion.4
  131.9 1.6 copy-done.1
  133.5 1.9 exponential_reduce_fusion.4
  135.4 25.5 %all-gather.2 = f32[8192]{0:T(1024)S(1)} all-gather(f32[1024]{0:T(1024)S(1)} %subtract_reduce_fusion.4), channel_id=4, replica_groups=mesh['rows'=8,'cols'=16] {'rows'}, dimensions={0}, use_global_device_ids=true | all-gather | bytes 36864 | tf_op jit(solution)/shard_map/all_gather | solution.py:13
  160.9 12.8 %all-gather.3 = f32[8192]{0:T(1024)S(1)} all-gather(f32[1024]{0:T(1024)S(1)} %exponential_reduce_fusion.4), channel_id=5, replica_groups=mesh['rows'=8,'cols'=16] {'rows'}, dimensions={0}, use_global_device_ids=true | all-gather | bytes 36864 | tf_op jit(solution)/shard_map/all_gather | solution.py:13
  173.7 0.4 while.73
  174.1 4.0 subtract_reduce_fusion.3
  178.1 4.3 exponential_reduce_fusion.3
  182.4 17.5 %all-gather.4 = f32[32768]{0:T(1024)S(1)} all-gather(f32[2048]{0:T(1024)S(1)} %subtract_reduce_fusion.3), channel_id=6, replica_groups=mesh['rows'=8,'cols'=16] {'cols'}, dimensions={0}, use_global_device_ids=true | all-gather | bytes 139264 | tf_op jit(solution)/shard_map/all_gather | solution.py:13
  199.9 16.3 %all-gather.5 = f32[32768]{0:T(1024)S(1)} all-gather(f32[2048]{0:T(1024)S(1)} %exponential_reduce_fusion.3), channel_id=7, replica_groups=mesh['rows'=8,'cols'=16] {'cols'}, dimensions={0}, use_global_device_ids=true | all-gather | bytes 139264 | tf_op jit(solution)/shard_map/all_gather | solution.py:13
  216.3 0.9 while.74
  217.3 4.0 subtract_reduce_fusion.2
  221.3 4.4 exponential_reduce_fusion.2
  225.6 23.7 %all-gather.6 = f32[8192]{0:T(1024)S(1)} all-gather(f32[1024]{0:T(1024)S(1)} %subtract_reduce_fusion.2), channel_id=8, replica_groups=mesh['rows'=8,'cols'=16] {'rows'}, dimensions={0}, use_global_device_ids=true | all-gather | bytes 36864 | tf_op jit(solution)/shard_map/all_gather | solution.py:13
  249.3 12.8 %all-gather.7 = f32[8192]{0:T(1024)S(1)} all-gather(f32[1024]{0:T(1024)S(1)} %exponential_reduce_fusion.2), channel_id=9, replica_groups=mesh['rows'=8,'cols'=16] {'rows'}, dimensions={0}, use_global_device_ids=true | all-gather | bytes 36864 | tf_op jit(solution)/shard_map/all_gather | solution.py:13
  262.1 0.4 while.75
  262.5 4.0 subtract_reduce_fusion.1
  266.5 4.3 exponential_reduce_fusion.1
  270.9 17.5 %all-gather.8 = f32[32768]{0:T(1024)S(1)} all-gather(f32[2048]{0:T(1024)S(1)} %subtract_reduce_fusion.1), channel_id=10, replica_groups=mesh['rows'=8,'cols'=16] {'cols'}, dimensions={0}, use_global_device_ids=true | all-gather | bytes 139264 | tf_op jit(solution)/shard_map/all_gather | solution.py:13
  288.3 16.1 %all-gather.9 = f32[32768]{0:T(1024)S(1)} all-gather(f32[2048]{0:T(1024)S(1)} %exponential_reduce_fusion.1), channel_id=11, replica_groups=mesh['rows'=8,'cols'=16] {'cols'}, dimensions={0}, use_global_device_ids=true | all-gather | bytes 139264 | tf_op jit(solution)/shard_map/all_gather | solution.py:13
  304.5 0.9 while.76
  305.5 4.1 subtract_reduce_fusion
  309.6 4.4 exponential_reduce_fusion
  313.9 23.7 %all-gather.10 = f32[8192]{0:T(1024)S(1)} all-gather(f32[1024]{0:T(1024)S(1)} %subtract_reduce_fusion), channel_id=12, replica_groups=mesh['rows'=8,'cols'=16] {'rows'}, dimensions={0}, use_global_device_ids=true | all-gather | bytes 36864 | tf_op jit(solution)/shard_map/all_gather | solution.py:13
  337.6 12.8 %all-gather.11 = f32[8192]{0:T(1024)S(1)} all-gather(f32[1024]{0:T(1024)S(1)} %exponential_reduce_fusion), channel_id=13, replica_groups=mesh['rows'=8,'cols'=16] {'rows'}, dimensions={0}, use_global_device_ids=true | all-gather | bytes 36864 | tf_op jit(solution)/shard_map/all_gather | solution.py:13
  350.5 0.4 while.77
  350.9 7.9 %fusion.2 = f32[2048,512]{1,0:T(8,128)} fusion(bf16[1024,512]{1,0:T(8,128)(2,1)S(1)} %copy-done.3, f32[2048,1024]{0,1:T(8,128)} %copy-done, f32[1024]{0:T(1024)S(1)} %add_subtract_fusion.3, f32[2048]{0:T(1024)S(1)} %add_subtract_fusion), kind=kOutput, calls=%fused_computation.34 | convolution fusion | flops 2153775104 | bytes 13643776 | tf_op jit(solution)/shard_map/dot_general | solution.py:59
  358.8 0.0 all-reduce.2.cloned.1.call-update
  358.8 4.4 fusion.1
  363.2 32.2 %psum.14 = f32[2048]{0:T(1024)S(1)} all-reduce(f32[2048]{0:T(1024)S(1)} %fusion.1), channel_id=1, replica_groups=mesh['rows'=8,'cols'=16] {'cols'}, use_global_device_ids=true, to_apply=%region_27.28 | all-reduce | flops 2048 | bytes 16384 | tf_op jit(solution)/shard_map/psum | solution.py:62
  395.4 0.1 dynamic-slice
  395.5 2.5 convert_element_type.10
  398.0 62.9 %all-reduce.2.cloned.1.call-done = f32[2048,512]{1,0:T(8,128)} async-done(((f32[2048,512]{1,0:T(8,128)}), f32[2048,512]{1,0:T(8,128)}) %all-reduce.2.cloned.1.call-update) | async-done | bytes 4194320 | tf_op jit(solution)/shard_map/psum | solution.py:62
  460.9 1.8 dynamic-slice_subtract_fusion
  (185 shorter events, 2.3 us)
Async XLA Ops:
  6.5 29.6 %all-gather.17.cloned.1.call-start = ((), (), s32[]{:S(2)}) async-start(), calls=%async_computation.1 | async-start | bytes 1179648 | tf_op jit(solution)/shard_map/all_gather | solution.py:27
  7.3 74.7 %all-gather.15.cloned.1.call-start = ((), (), s32[]{:S(2)}) async-start(), calls=%async_computation | async-start | bytes 2228224 | tf_op jit(solution)/shard_map/all_gather | solution.py:26
  8.0 452.9 %all-reduce.2.cloned.1.call-start = ((), (), s32[]{:S(2)}) async-start(), calls=%async_computation.2 | async-start | bytes 8388608 | tf_op jit(solution)/shard_map/psum | solution.py:62
  88.4 3.2 copy-start
  88.4 39.3 %copy-start.4 = (f32[2048]{0:T(1024)S(1)}, f32[2048]{0:T(1024)}, u32[]{:S(2)}) copy-start(f32[2048]{0:T(1024)} %param.18) | copy-start | bytes 24580
  127.7 5.8 %copy-start.1 = (f32[2048,1024]{0,1:T(8,128)S(1)}, f32[2048,1024]{0,1:T(8,128)}, u32[]{:S(2)}) copy-start(f32[2048,1024]{0,1:T(8,128)} %copy-done) | copy-start | bytes 25165828
  127.7 46.4 %copy-start.5 = (f32[1024]{0:T(1024)S(1)}, f32[1024]{0:T(1024)}, u32[]{:S(2)}) copy-start(f32[1024]{0:T(1024)} %param.19) | copy-start | bytes 12292
  305.5 45.4 %copy-start.3 = (bf16[1024,512]{1,0:T(8,128)(2,1)S(1)}, bf16[1024,512]{1,0:T(8,128)(2,1)}, u32[]{:S(2)}) copy-start(bf16[1024,512]{1,0:T(8,128)(2,1)} %all-gather.17.cloned.1.call-done) | copy-start | bytes 3145732
  358.8 36.7 %copy-start.2 = (bf16[2048,512]{1,0:T(8,128)(2,1)S(1)}, bf16[2048,512]{1,0:T(8,128)(2,1)}, u32[]{:S(2)}) copy-start(bf16[2048,512]{1,0:T(8,128)(2,1)} %all-gather.15.cloned.1.call-done) | copy-start | bytes 6291460
Sparse Core Ops, SparseCore 0:
  9.1 26.9 all-gather.16
  38.3 43.6 all-gather.14
  358.9 101.9 all-reduce.1
where the time goes:
time: 470 us; the launch traced here: 469 us
  blocking collectives  244 us (52%)
  waiting for transfers between devices  137 us (29%)
  other arithmetic  54.2 us (12%)
  between operations  13.6 us (3%)
  matrix products  12.3 us (3%)
  local copies, waits for them, and re-layouts  6.25 us (1%)
    all_gather x12, blocking collectives, combined_all(): pieces = jax.tree.map(lambda part: lax.all_gather(part, axis), value)  212 us
    psum x1, waiting for transfers between devices, local(): moved_sum, row_sum = lax.psum((moved, row_total), 'cols')  62.9 us
    all_gather x1, waiting for transfers between devices, local(): lot_full = lax.all_gather(lot_features, 'cols', axis=0, tiled=True)  44.3 us
    psum x1, blocking collectives, local(): moved_sum, row_sum = lax.psum((moved, row_total), 'cols')  32.2 us
    all_gather x1, waiting for transfers between devices, local(): slot_full = lax.all_gather(slot_features, 'rows', axis=0, tiled=True)  28.1 us
    reduce_max x3, other arithmetic, local(): peaks = jnp.max(scores, axis=0)  12.2 us
    reduce_sum x3, other arithmetic, local(): totals = jnp.sum(jnp.exp(scores - peaks[None, :]), axis=0)  10.7 us
    reduce_sum x3, other arithmetic, local(): totals = jnp.sum(jnp.exp(scores - peaks[:, None]), axis=1)  10 us
  transfers between devices with their start and end apart: 3, of which 3 were waited for; matrix products, arithmetic and copies ran while one was open for 2% of the time, Pallas kernels for 0%

commit v1 on v0

v1 whole, which is shorter than its diff:
```python
import math

import jax
import jax.numpy as jnp
from jax import lax
from jax.experimental import pallas as pl
from jax.experimental.pallas import tpu as pltpu
from jax.sharding import Mesh, PartitionSpec as P

ITERS = 3
LOG2E = math.log2(math.e)
LANES = 128

LOT_GROUP = ("x", "core")
SLOT_GROUP = ("y", "z")


def lane_sum(values):
    total = values[:, :LANES]
    for start in range(LANES, values.shape[1], LANES):
        total = total + values[:, start : start + LANES]
    return jnp.sum(total.T, axis=0, keepdims=True)


def square_row(block):
    wide = block.astype(jnp.float32)
    return lane_sum(wide * wide) * (0.5 * LOG2E / math.sqrt(block.shape[1]))


def joined(parts):
    top = parts[0]
    for part in parts[1:]:
        top = jnp.maximum(top, part)
    total = jnp.exp2(parts[0] - top)
    for part in parts[1:]:
        total = total + jnp.exp2(part - top)
    return top + jnp.log(total) * LOG2E


def row_pass(score, wide_g, peak, total):
    lots, slots = score.shape
    tiles = slots // LANES

    def step(i, carry):
        rows = pl.ds(pl.multiple_of(i * 8, 8), 8)
        terms = [
            score[rows, t * LANES : (t + 1) * LANES] + wide_g[t * 8 : (t + 1) * 8, :]
            for t in range(tiles)
        ]
        top = terms[0]
        for term in terms[1:]:
            top = jnp.maximum(top, term)
        whole = jnp.exp2(terms[0] - top)
        for term in terms[1:]:
            whole = whole + jnp.exp2(term - top)
        peak[rows, :] = top
        total[rows, :] = whole
        return carry

    lax.fori_loop(0, lots // 8, step, 0, unroll=4)


def row_result(peak, total):
    out = []
    for start in range(0, peak.shape[0], LANES):
        tops = peak[start : start + LANES, :].T
        sums = total[start : start + LANES, :].T
        top = jnp.max(tops, axis=0, keepdims=True)
        whole = jnp.sum(sums * jnp.exp2(tops - top), axis=0, keepdims=True)
        out.append(top + jnp.log(whole) * LOG2E)
    return jnp.concatenate(out, axis=0)


def column_pass(score, wide_f):
    lots, slots = score.shape
    out = []
    for t in range(slots // LANES):
        cols = slice(t * LANES, (t + 1) * LANES)

        def terms_of(start):
            return [
                score[pl.ds(start + k, 8), cols] + wide_f[pl.ds(start + k, 8), :]
                for k in range(0, LANES, 8)
            ]

        def fold(terms, top):
            whole = jnp.exp2(terms[0] - top)
            for term in terms[1:]:
                whole = whole + jnp.exp2(term - top)
            return whole

        def peak_of(terms):
            top = terms[0]
            for term in terms[1:]:
                top = jnp.maximum(top, term)
            return top

        terms = terms_of(0)
        top = peak_of(terms)
        whole = fold(terms, top)
        for start in range(LANES, lots, LANES):
            terms = terms_of(start)
            new = jnp.maximum(top, peak_of(terms))
            whole = whole * jnp.exp2(top - new) + fold(terms, new)
            top = new
        high = jnp.max(top, axis=0, keepdims=True)
        whole = jnp.sum(whole * jnp.exp2(top - high), axis=0, keepdims=True)
        out.append(high + jnp.log(whole) * LOG2E)
    return jnp.concatenate(out, axis=0)


def spread_rows(values, wide):
    for t in range(values.shape[0]):
        wide[t * 8 : (t + 1) * 8, :] = jnp.broadcast_to(values[t : t + 1, :], (8, LANES))


def spread_columns(values, wide):
    for r in range(values.shape[0]):
        wide[r * LANES : (r + 1) * LANES, :] = jnp.broadcast_to(values[r : r + 1, :], (LANES, LANES)).T


def send_out(out, values, copies):
    rows = values.shape[0]
    for n in range(copies):
        out[n * rows : (n + 1) * rows, :] = values


def padded(rows):
    have = jnp.concatenate(rows, axis=0)
    return jnp.concatenate([have, jnp.zeros((8 - have.shape[0], LANES), jnp.float32)], axis=0)


def score_kernel(peers, lots, slots, own_lots, own_mass, score, out, wide_g, peak, total):
    scale = LOG2E / math.sqrt(lots.shape[1])
    step = 256
    for start in range(0, slots.shape[0], step):
        inner = lax.dot_general(
            lots[...], slots[start : start + step, :], (((1,), (1,)), ((), ())), preferred_element_type=jnp.float32
        )
        score[:, start : start + step] = inner * scale
    norms = [square_row(slots[start : start + LANES, :]) for start in range(0, slots.shape[0], LANES)]
    spread_rows(-jnp.concatenate(norms, axis=0), wide_g)
    row_pass(score, wide_g, peak, total)
    own = padded([jnp.log(own_mass[...]) * LOG2E, square_row(own_lots[...])])
    send_out(out, jnp.concatenate([row_result(peak, total), own], axis=0), peers)


def lot_update(parts, first, shares, blocks):
    stride = parts.shape[0] // shares
    log_sum = joined([parts[n * stride : n * stride + blocks, :] for n in range(shares)])
    wide = first.shape[0] // shares
    logs = jnp.concatenate([first[n * wide + blocks : n * wide + blocks + 1, :] for n in range(shares)], axis=0)
    squares = jnp.concatenate([first[n * wide + blocks + 1 : n * wide + blocks + 2, :] for n in range(shares)], axis=0)
    pot = logs + squares - log_sum
    return pot - squares


def slot_update(parts, first, shares, blocks):
    stride = parts.shape[0] // shares
    log_sum = joined([parts[n * stride : n * stride + blocks, :] for n in range(shares)])
    wide = first.shape[0] // shares
    logs = jnp.concatenate([first[n * wide + blocks : n * wide + blocks + 1, :] for n in range(shares)], axis=0)
    return logs - log_sum


def column_kernel(shares, peers, score, parts, first, own_mass, out, f_out, wide_f):
    f = lot_update(parts, first, shares, score.shape[0] // LANES)
    f_out[...] = f
    spread_columns(f, wide_f)
    sums = column_pass(score, wide_f)
    if out.shape[0] // peers > sums.shape[0]:
        sums = jnp.concatenate([sums, padded([jnp.log(own_mass[...]) * LOG2E])], axis=0)
    send_out(out, sums, peers)


def row_kernel(shares, peers, score, parts, first, out, wide_g, peak, total):
    g = slot_update(parts, first, shares, score.shape[1] // LANES)
    spread_rows(g, wide_g)
    row_pass(score, wide_g, peak, total)
    send_out(out, row_result(peak, total), peers)


def final_kernel(shares, score, parts, first, f, lots, slots, out, wide_g, wide_f, plan, row_sum):
    g = slot_update(parts, first, shares, score.shape[1] // LANES)
    spread_rows(g, wide_g)
    spread_columns(f[...], wide_f)
    tiles = score.shape[1] // LANES

    def step(i, carry):
        rows = pl.ds(pl.multiple_of(i * 16, 16), 16)
        shift = wide_f[rows, :]
        whole = None
        for t in range(tiles):
            cols = slice(t * LANES, (t + 1) * LANES)
            both = jnp.concatenate([wide_g[t * 8 : (t + 1) * 8, :]] * 2, axis=0)
            term = jnp.exp2(score[rows, cols] + shift + both)
            plan[rows, cols] = term.astype(jnp.bfloat16)
            whole = term if whole is None else whole + term
        row_sum[rows, :] = jnp.broadcast_to(jnp.sum(whole, axis=1, keepdims=True), whole.shape)
        return carry

    lax.fori_loop(0, score.shape[0] // 16, step, 0, unroll=2)
    step_rows = 256
    for start in range(0, score.shape[0], step_rows):
        rows = slice(start, start + step_rows)
        moved = jnp.dot(plan[rows, :], slots[...], preferred_element_type=jnp.float32)
        sums = jnp.concatenate([row_sum[rows, :]] * (lots.shape[1] // LANES), axis=1)
        out[rows, :] = sums * lots[rows, :].astype(jnp.float32) - moved


def call(kernel, outs, scratch, cost, *args):
    vmem = pl.BlockSpec(memory_space=pltpu.VMEM)
    return pl.pallas_call(
        kernel,
        out_shape=outs,
        in_specs=[vmem] * len(args),
        out_specs=[vmem] * len(outs) if isinstance(outs, (list, tuple)) else vmem,
        scratch_shapes=[pltpu.VMEM(shape, dtype) for shape, dtype in scratch],
        compiler_params=pltpu.CompilerParams(vmem_limit_bytes=40 * 2**20),
        cost_estimate=pl.CostEstimate(flops=cost, bytes_accessed=0, transcendentals=cost // 1024),
    )(*args)


def spread(values, axes):
    return lax.all_to_all(values, axes, 0, 0, tiled=True)


def local(sizes, lot_features, slot_features, lot_mass, slot_mass):
    own_rows, width = lot_features.shape
    lot_share = sizes["x"] * sizes["core"]
    slot_share = sizes["y"] * sizes["z"]
    lot_at = lax.axis_index("x") * sizes["z"] + lax.axis_index("z")
    slot_at = lax.axis_index("y") * sizes["core"] + lax.axis_index("core")
    own_lot_mass = lax.dynamic_slice_in_dim(lot_mass, lot_at * own_rows, own_rows, 0).reshape(1, own_rows)
    own_slot_mass = lax.dynamic_slice_in_dim(slot_mass, slot_at * own_rows, own_rows, 0).reshape(1, own_rows)

    lots = lax.all_gather(lot_features, LOT_GROUP, axis=0, tiled=True)
    slots = spread(jnp.tile(slot_features, (slot_share, 1)), SLOT_GROUP)
    n, m = lots.shape[0], slots.shape[0]
    f32 = jnp.float32

    def shape(*dims):
        return jax.ShapeDtypeStruct(dims, f32)

    wide_g = ((m // LANES * 8, LANES), f32)
    wide_f = ((n, LANES), f32)
    lot_blocks, slot_blocks = n // LANES, m // LANES
    work = n * m * 4

    score, out = call(
        lambda *refs: score_kernel(lot_share, *refs),
        [shape(n, m), shape(lot_share * (lot_blocks + 8), LANES)],
        [wide_g, wide_f, wide_f],
        work,
        lots, slots, lot_features, own_lot_mass,
    )
    first_lot = lot_parts = spread(out, LOT_GROUP)
    first_slot = None
    for step in range(ITERS):
        extra = 8 if step == 0 else 0
        out, f = call(
            lambda *refs: column_kernel(lot_share, slot_share, *refs),
            [shape(slot_share * (slot_blocks + extra), LANES), shape(lot_blocks, LANES)],
            [wide_f],
            work,
            score, lot_parts, first_lot, own_slot_mass,
        )
        slot_parts = spread(out, SLOT_GROUP)
        if step == 0:
            first_slot = slot_parts
        if step < ITERS - 1:
            out = call(
                lambda *refs: row_kernel(slot_share, lot_share, *refs),
                shape(lot_share * lot_blocks, LANES),
                [wide_g, wide_f, wide_f],
                work,
                score, slot_parts, first_slot,
            )
            lot_parts = spread(out, LOT_GROUP)
    grad = call(
        lambda *refs: final_kernel(slot_share, *refs),
        shape(n, width),
        [wide_g, wide_f, ((n, m), jnp.bfloat16), wide_f],
        work,
        score, slot_parts, first_slot, f, lots, slots,
    )
    shares = spread(grad, LOT_GROUP)
    return jnp.sum(shares.reshape(lot_share, own_rows, width), axis=0)


def solution(mesh):
    sizes = {"y": 4, "core": 2, "x": 4, "z": 4}
    fine = Mesh(mesh.devices.reshape(tuple(sizes.values())), tuple(sizes))
    placed = (P(("y", "core", "x", "z"), None), P(("x", "z", "y", "core"), None), P(("y", "core")), P(("x", "z")))
    return jax.shard_map(
        lambda *args: local(sizes, *args), mesh=fine, in_specs=placed, out_specs=P(("y", "core", "x", "z"), None), check_vma=False
    )
```

time: 470 us -> 182 us (0.39)
  blocking collectives: 244 us -> 79.4 us
  waiting for transfers between devices: 137 us -> 32.1 us
  other arithmetic: 54.2 us -> 0.92 us
  Pallas kernels: 0 us -> 24.6 us
  starting transfers between devices: 0.08 us -> 16.2 us
  matrix products: 12.3 us -> 0 us
  local copies, waits for them, and re-layouts: 6.25 us -> 14.5 us
    all_gather x12 -> x0, blocking collectives: 212 us -> none  [combined_all(): pieces = jax.tree.map(lambda part: lax.all_gather(part, axis), value)]
    all_to_all x0 -> x6, blocking collectives: none -> 79.4 us  [spread(): return lax.all_to_all(values, axes, 0, 0, tiled=True)]
    psum x1 -> x0, waiting for transfers between devices: 62.9 us -> none  [local(): moved_sum, row_sum = lax.psum((moved, row_total), 'cols')]
    all_gather x2 -> x1, waiting for transfers between devices: 72.4 us -> 27.3 us  [local(): lots = lax.all_gather(lot_features, LOT_GROUP, axis=0, tiled=True)]
    psum x1 -> x0, blocking collectives: 32.2 us -> none  [local(): moved_sum, row_sum = lax.psum((moved, row_total), 'cols')]
    reduce_sum x9 -> x1, other arithmetic: 28.7 us -> 0.92 us  [local(): return jnp.sum(shares.reshape(lot_share, own_rows, width), axis=0)]
    pallas_call x0 -> x7, Pallas kernels: none -> 24.6 us  [call(): pl.pallas_call(kernel, out_shape=outs, in_specs=[vmem] * len(args), out_s...]
    reduce_max x5 -> x0, other arithmetic: 20.2 us -> none  [the longest x3 12.2 us: local(): peaks = jnp.max(scores, axis=0)]
  transfers between devices with their start and end apart: 3 -> 3, of which waited for: 3 -> 2; matrix products, arithmetic and copies ran while one was open for 2% -> 0% of each run, Pallas kernels for 0% -> 0%
where the time goes in v1:
time: 182 us; the launch traced here: 181 us
  blocking collectives  79.4 us (44%)
  waiting for transfers between devices  32.1 us (18%)
  Pallas kernels  24.6 us (14%)
  starting transfers between devices  16.2 us (9%)
  local copies, waits for them, and re-layouts  14.5 us (8%)
  between operations  13.5 us (7%)
    all_to_all x6, blocking collectives, spread(): return lax.all_to_all(values, axes, 0, 0, tiled=True)  79.4 us
    all_gather x1, waiting for transfers between devices, local(): lots = lax.all_gather(lot_features, LOT_GROUP, axis=0, tiled=True)  27.3 us
    pallas_call x7, Pallas kernels, call(): pl.pallas_call(kernel, out_shape=outs, in_specs=[vmem] * len(args), out_s...  24.6 us
    all_to_all x2, starting transfers between devices, spread(): return lax.all_to_all(values, axes, 0, 0, tiled=True)  16.2 us
    unnamed x14, local copies, waits for them, and re-layouts  11.2 us
    all_to_all x2, waiting for transfers between devices, spread(): return lax.all_to_all(values, axes, 0, 0, tiled=True)  4.09 us
  transfers between devices with their start and end apart: 3, of which 2 were waited for; matrix products, arithmetic and copies ran while one was open for 0% of the time, Pallas kernels for 0%

profile of v1, /device:TPU:1, one launch (start us, length us, event | category | flops | bytes accessed | tf_op | source)
XLA Modules:
  0.0 181.2 jit_solution(3202140371091032561)
XLA Ops:
  6.5 0.0 copy-start
  6.5 2.5 %tile.2 = bf16[16,128,512]{2,1,0:T(8,128)(2,1)} broadcast(bf16[128,512]{1,0:T(8,128)(2,1)} %param.5), dimensions={1,2} | broadcast | bytes 2228224 | tf_op jit(solution)/shard_map/tile | solution.py:238
  9.0 0.0 copy-start.6
  9.0 8.7 %all-to-all-start = ((bf16[16,128,512]{2,1,0:T(8,128)(2,1)}), bf16[16,128,512]{2,1,0:T(8,128)(2,1)S(1)}, u32[]{:S(2)}, u32[]{:S(2)}) async-start(bf16[16,128,512]{2,1,0:T(8,128)(2,1)} %tile.2), calls=%async_computation | async-start | bytes 4194304 | tf_op jit(solution)/shard_map/all_to_all | solution.py:225
  17.7 0.0 all-gather.2.cloned.1.call-start
  17.8 0.7 all-gather.2.cloned.1.call-update
  18.5 0.0 copy-done
  18.5 0.1 dynamic-slice_bitcast_fusion.1.refs_3_
  18.6 27.3 %all-gather.2.cloned.1.call-done.refs_0_.refs_4_ = bf16[1024,512]{1,0:T(8,128)(2,1)} async-done(((bf16[128,512]{1,0:T(8,128)(2,1)}), bf16[1024,512]{1,0:T(8,128)(2,1)}) %all-gather.2.cloned.1.call-update) | async-done | bytes 1048592 | tf_op jit(solution)/shard_map/all_gather | solution.py:237
  45.9 0.0 all-to-all-done
  45.9 0.0 copy-done.6
  45.9 0.0 copy-start.4
  45.9 1.2 copy-done.4
  47.1 5.7 %shard_map.46 = (f32[1024,2048]{1,0:T(8,128)S(1)}, f32[128,128]{1,0:T(8,128)}) custom-call(bf16[1024,512]{1,0:T(8,128)(2,1)S(1)} %copy-done.4, bf16[2048,512]{1,0:T(8,128)(2,1)S(1)} %bitcast.18, bf16[128,512]{1,0:T(8,128)(2,1)S(1)} %copy-done.6, f32[1,128]{1,0:T(1,128)S(1)} %dynamic-slice_bitcast_fusion.1.refs_3_), custom_call_target="tpu_custom_call" | custom-call | flops 8388608 | tf_op jit(solution)/shard_map/pallas_call | solution.py:213
  52.8 0.0 copy-start.1
  52.8 3.2 %copy-done.1 = f32[1024,2048]{1,0:T(8,128)} copy-done((f32[1024,2048]{1,0:T(8,128)}, f32[1024,2048]{1,0:T(8,128)S(1)}, u32[]{:S(2)}) %copy-start.1) | copy-done | bytes 8388632
  56.1 7.5 %all-to-all-start.1 = ((f32[8,16,128]{2,1,0:T(8,128)}), f32[8,16,128]{2,1,0:T(8,128)S(1)}, u32[]{:S(2)}, u32[]{:S(2)}) async-start(f32[8,16,128]{2,1,0:T(8,128)} %bitcast.2), calls=%async_computation.1 | async-start | bytes 131072 | tf_op jit(solution)/shard_map/all_to_all | solution.py:225
  63.5 0.8 dynamic-slice_bitcast_fusion.refs_3_
  64.3 4.1 %all-to-all-done.1 = f32[8,16,128]{2,1,0:T(8,128)S(1)} async-done(((f32[8,16,128]{2,1,0:T(8,128)}), f32[8,16,128]{2,1,0:T(8,128)S(1)}, u32[]{:S(2)}, u32[]{:S(2)}) %all-to-all-start.1) | async-done | bytes 65568 | tf_op jit(solution)/shard_map/all_to_all | solution.py:225
  68.4 0.0 copy-start.2
  68.4 3.4 %copy-done.2 = f32[1024,2048]{1,0:T(8,128)S(1)} copy-done((f32[1024,2048]{1,0:T(8,128)S(1)}, f32[1024,2048]{1,0:T(8,128)}, u32[]{:S(2)}) %copy-start.2) | copy-done | bytes 8388632
  71.8 2.5 %shard_map.47 = (f32[384,128]{1,0:T(8,128)S(1)}, f32[8,128]{1,0:T(8,128)}) custom-call(f32[1024,2048]{1,0:T(8,128)S(1)} %copy-done.2, f32[128,128]{1,0:T(8,128)S(1)} %bitcast.25, f32[128,128]{1,0:T(8,128)S(1)} %bitcast.26, f32[1,128]{1,0:T(1,128)S(1)} %dynamic-slice_bitcast_fusion.refs_3_), custom_call_target="tpu_custom_call" | custom-call | flops 8388608 | tf_op jit(solution)/shard_map/pallas_call | solution.py:213
  74.2 10.2 %all_to_all.83 = f32[16,24,128]{2,1,0:T(8,128)S(1)} all-to-all(f32[16,24,128]{2,1,0:T(8,128)S(1)} %bitcast.31), channel_id=1, replica_groups=mesh['y'=4,'core'=2,'x'=4,'z'=4] {'y','z'}, dimensions={0} | all-to-all | bytes 393216 | tf_op jit(solution)/shard_map/all_to_all | solution.py:225
  84.4 2.7 %shard_map.48 = f32[64,128]{1,0:T(8,128)S(1)} custom-call(f32[1024,2048]{1,0:T(8,128)S(1)} %copy-done.2, f32[384,128]{1,0:T(8,128)S(1)} %bitcast.21, f32[384,128]{1,0:T(8,128)S(1)} %bitcast.22), custom_call_target="tpu_custom_call" | custom-call | flops 8388608 | tf_op jit(solution)/shard_map/pallas_call | solution.py:213
  87.1 9.3 %all_to_all.84 = f32[8,8,128]{2,1,0:T(8,128)S(1)} all-to-all(f32[8,8,128]{2,1,0:T(8,128)S(1)} %bitcast.35), channel_id=1, replica_groups=mesh['y'=4,'core'=2,'x'=4,'z'=4] {'x','core'}, dimensions={0} | all-to-all | bytes 65536 | tf_op jit(solution)/shard_map/all_to_all | solution.py:225
  96.3 2.5 %shard_map.49 = (f32[256,128]{1,0:T(8,128)S(1)}, f32[8,128]{1,0:T(8,128)}) custom-call(f32[1024,2048]{1,0:T(8,128)S(1)} %copy-done.2, f32[64,128]{1,0:T(8,128)S(1)} %bitcast.33, f32[128,128]{1,0:T(8,128)S(1)} %bitcast.27, f32[1,128]{1,0:T(1,128)S(1)} %dynamic-slice_bitcast_fusion.refs_3_), custom_call_target="tpu_custom_call" | custom-call | flops 8388608 | tf_op jit(solution)/shard_map/pallas_call | solution.py:213
  98.8 9.9 %all_to_all.85 = f32[16,16,128]{2,1,0:T(8,128)S(1)} all-to-all(f32[16,16,128]{2,1,0:T(8,128)S(1)} %bitcast.37), channel_id=1, replica_groups=mesh['y'=4,'core'=2,'x'=4,'z'=4] {'y','z'}, dimensions={0} | all-to-all | bytes 262144 | tf_op jit(solution)/shard_map/all_to_all | solution.py:225
  108.7 2.7 %shard_map.50 = f32[64,128]{1,0:T(8,128)S(1)} custom-call(f32[1024,2048]{1,0:T(8,128)S(1)} %copy-done.2, f32[256,128]{1,0:T(8,128)S(1)} %bitcast.30, f32[384,128]{1,0:T(8,128)S(1)} %bitcast.23), custom_call_target="tpu_custom_call" | custom-call | flops 8388608 | tf_op jit(solution)/shard_map/pallas_call | solution.py:213
  111.4 9.1 %all_to_all.86 = f32[8,8,128]{2,1,0:T(8,128)S(1)} all-to-all(f32[8,8,128]{2,1,0:T(8,128)S(1)} %bitcast.34), channel_id=1, replica_groups=mesh['y'=4,'core'=2,'x'=4,'z'=4] {'x','core'}, dimensions={0} | all-to-all | bytes 65536 | tf_op jit(solution)/shard_map/all_to_all | solution.py:225
  120.6 0.0 copy-start.5
  120.6 2.0 %shard_map.51 = (f32[256,128]{1,0:T(8,128)S(1)}, f32[8,128]{1,0:T(8,128)S(1)}) custom-call(f32[1024,2048]{1,0:T(8,128)S(1)} %copy-done.2, f32[64,128]{1,0:T(8,128)S(1)} %bitcast.32, f32[128,128]{1,0:T(8,128)S(1)} %bitcast.28, f32[1,128]{1,0:T(1,128)S(1)} %dynamic-slice_bitcast_fusion.refs_3_), custom_call_target="tpu_custom_call" | custom-call | flops 8388608 | tf_op jit(solution)/shard_map/pallas_call | solution.py:213
  122.5 9.9 %all_to_all.87 = f32[16,16,128]{2,1,0:T(8,128)S(1)} all-to-all(f32[16,16,128]{2,1,0:T(8,128)S(1)} %bitcast.36), channel_id=1, replica_groups=mesh['y'=4,'core'=2,'x'=4,'z'=4] {'y','z'}, dimensions={0} | all-to-all | bytes 262144 | tf_op jit(solution)/shard_map/all_to_all | solution.py:225
  132.5 0.0 copy-done.5
  132.5 0.0 copy-start.3
  132.5 3.4 %copy-done.3 = f32[1024,2048]{1,0:T(8,128)S(1)} copy-done((f32[1024,2048]{1,0:T(8,128)S(1)}, f32[1024,2048]{1,0:T(8,128)}, u32[]{:S(2)}) %copy-start.3) | copy-done | bytes 8388632
  135.8 6.6 %shard_map.52 = f32[1024,512]{1,0:T(8,128)S(1)} custom-call(f32[1024,2048]{1,0:T(8,128)S(1)} %copy-done.3, f32[256,128]{1,0:T(8,128)S(1)} %bitcast.29, f32[384,128]{1,0:T(8,128)S(1)} %bitcast.24, f32[8,128]{1,0:T(8,128)S(1)} %get-tuple-element.16.refs_3_, bf16[1024,512]{1,0:T(8,128)(2,1)S(1)} %copy-done.5, bf16[2048,512]{1,0:T(8,128)(2,1)S(1)} %bitcast.19), custom_call_target="tpu_custom_call" | custom-call | flops 8388608 | tf_op jit(solution)/shard_map/pallas_call | solution.py:213
  142.5 31.0 %all_to_all.88 = f32[8,128,512]{2,1,0:T(8,128)S(1)} all-to-all(f32[8,128,512]{2,1,0:T(8,128)S(1)} %bitcast.20), channel_id=1, replica_groups=mesh['y'=4,'core'=2,'x'=4,'z'=4] {'x','core'}, dimensions={0} | all-to-all | bytes 4194304 | tf_op jit(solution)/shard_map/all_to_all | solution.py:225
  173.4 0.9 reduce_sum.9
Async XLA Ops:
  6.5 11.9 %copy-start = (f32[2048]{0:T(1024)S(1)}, f32[2048]{0:T(1024)}, u32[]{:S(2)}) copy-start(f32[2048]{0:T(1024)} %param.6) | copy-start | bytes 24580
  9.0 36.9 %copy-start.6 = (bf16[128,512]{1,0:T(8,128)(2,1)S(1)}, bf16[128,512]{1,0:T(8,128)(2,1)}, u32[]{:S(2)}) copy-start(bf16[128,512]{1,0:T(8,128)(2,1)} %refs_2_.1) | copy-start | bytes 393220
  9.0 36.9 %all-to-all-start = ((bf16[16,128,512]{2,1,0:T(8,128)(2,1)}), bf16[16,128,512]{2,1,0:T(8,128)(2,1)S(1)}, u32[]{:S(2)}, u32[]{:S(2)}) async-start(bf16[16,128,512]{2,1,0:T(8,128)(2,1)} %tile.2), calls=%async_computation | async-start | bytes 4194304 | tf_op jit(solution)/shard_map/all_to_all | solution.py:225
  17.7 28.2 %all-gather.2.cloned.1.call-start = ((), (), s32[]{:S(2)}) async-start(), calls=%async_computation.8 | async-start | bytes 1179648 | tf_op jit(solution)/shard_map/all_gather | solution.py:237
  45.9 1.2 copy-start.4
  52.8 3.2 %copy-start.1 = (f32[1024,2048]{1,0:T(8,128)}, f32[1024,2048]{1,0:T(8,128)S(1)}, u32[]{:S(2)}) copy-start(f32[1024,2048]{1,0:T(8,128)S(1)} %get-tuple-element.11.refs_0_) | copy-start | bytes 25165828
  56.1 12.3 %all-to-all-start.1 = ((f32[8,16,128]{2,1,0:T(8,128)}), f32[8,16,128]{2,1,0:T(8,128)S(1)}, u32[]{:S(2)}, u32[]{:S(2)}) async-start(f32[8,16,128]{2,1,0:T(8,128)} %bitcast.2), calls=%async_computation.1 | async-start | bytes 131072 | tf_op jit(solution)/shard_map/all_to_all | solution.py:225
  68.4 3.4 %copy-start.2 = (f32[1024,2048]{1,0:T(8,128)S(1)}, f32[1024,2048]{1,0:T(8,128)}, u32[]{:S(2)}) copy-start(f32[1024,2048]{1,0:T(8,128)} %copy-done.1) | copy-start | bytes 25165828
  120.6 11.9 %copy-start.5 = (bf16[1024,512]{1,0:T(8,128)(2,1)S(1)}, bf16[1024,512]{1,0:T(8,128)(2,1)}, u32[]{:S(2)}) copy-start(bf16[1024,512]{1,0:T(8,128)(2,1)} %all-gather.2.cloned.1.call-done.refs_0_.refs_4_) | copy-start | bytes 3145732
  132.5 3.4 %copy-start.3 = (f32[1024,2048]{1,0:T(8,128)S(1)}, f32[1024,2048]{1,0:T(8,128)}, u32[]{:S(2)}) copy-start(f32[1024,2048]{1,0:T(8,128)} %copy-done.1) | copy-start | bytes 25165828
Sparse Core Ops, SparseCore 0:
  20.3 25.5 all-gather.1

commit v2 on v0

v2 whole, which is shorter than its diff:
```python
import math

import jax
import jax.numpy as jnp
from jax import lax
from jax.experimental import pallas as pl
from jax.experimental.pallas import tpu as pltpu
from jax.sharding import Mesh, PartitionSpec as P

ITERS = 3
LOG2E = math.log2(math.e)
LANES = 128

SIZES = {"y": 4, "core": 2, "x": 4, "z": 4}
ALL = tuple(SIZES)
FULL, PAIRS, ACROSS, EACH = [(0, 1, 2, 3)], [(0, 1), (2, 3)], [(1, 2), (3, 0)], [(0,), (1,), (2,), (3,)]


def groups(ys, cores, xs, zs):
    return [
        [((y * 2 + core) * 4 + x) * 4 + z for core in cs for x in px for y in py for z in pz]
        for px in xs
        for py in ys
        for pz in zs
        for cs in cores
    ]


LOT_GROUPS = groups(EACH, [(0,), (1,)], FULL, ACROSS)
SLOT_GROUPS = groups(FULL, [(0, 1)], EACH, PAIRS)
CORE_SLOT_GROUPS = groups(FULL, [(0,), (1,)], EACH, PAIRS)
LOT_SHARE, SLOT_SHARE = 8, 16


def place_in_lots():
    return lax.axis_index("x") * 2 + (lax.axis_index("z") + 1) % 2


def lane_sum(values):
    total = values[:, :LANES]
    for start in range(LANES, values.shape[1], LANES):
        total = total + values[:, start : start + LANES]
    return jnp.sum(total.T, axis=0, keepdims=True)


def square_row(block):
    wide = block.astype(jnp.float32)
    return lane_sum(wide * wide) * (0.5 * LOG2E / math.sqrt(block.shape[1]))


def square_rows(features):
    return jnp.concatenate([square_row(features[start : start + LANES, :]) for start in range(0, features.shape[0], LANES)], axis=0)


def joined(parts):
    top = parts[0]
    for part in parts[1:]:
        top = jnp.maximum(top, part)
    total = jnp.exp2(parts[0] - top)
    for part in parts[1:]:
        total = total + jnp.exp2(part - top)
    return top + jnp.log(total) * LOG2E


def in_pairs(join, terms):
    while len(terms) > 1:
        terms = [join(*terms[i : i + 2]) if i + 1 < len(terms) else terms[i] for i in range(0, len(terms), 2)]
    return terms[0]


def peak_of(terms):
    return in_pairs(jnp.maximum, terms)


def fold(terms, top):
    return in_pairs(jnp.add, [jnp.exp2(term - top) for term in terms])


def onward(state, terms):
    top = peak_of(terms)
    if state is None:
        return top, fold(terms, top)
    top = jnp.maximum(top, state[0])
    return top, state[1] * jnp.exp2(state[0] - top) + fold(terms, top)


def row_pass(scores, wide_g, peak, total, before=None):
    groups_of, tiles_of = 8, 8

    def step(i, carry):
        rows = [pl.ds(pl.multiple_of(i * 8 * groups_of + 8 * r, 8), 8) for r in range(groups_of)]
        states = [None if before is None else (before[0][row, :], before[1][row, :]) for row in rows]
        n = 0
        for score in scores:
            for start in range(0, score.shape[1] // LANES, tiles_of):
                gs = [wide_g[(n + k) * 8 : (n + k + 1) * 8, :] for k in range(tiles_of)]
                n += tiles_of
                for r, row in enumerate(rows):
                    terms = [score[row, (start + k) * LANES : (start + k + 1) * LANES] + g for k, g in enumerate(gs)]
                    states[r] = onward(states[r], terms)
        for row, (top, whole) in zip(rows, states, strict=True):
            peak[row, :] = top
            total[row, :] = whole
        return carry

    lax.fori_loop(0, scores[0].shape[0] // (8 * groups_of), step, 0)


def row_result(peak, total):
    out = []
    for start in range(0, peak.shape[0], LANES):
        tops = peak[start : start + LANES, :].T
        sums = total[start : start + LANES, :].T
        top = jnp.max(tops, axis=0, keepdims=True)
        whole = jnp.sum(sums * jnp.exp2(tops - top), axis=0, keepdims=True)
        out.append(top + jnp.log(whole) * LOG2E)
    return jnp.concatenate(out, axis=0)


def column_pass(score, wide_f, sums, first):
    rows, tiles_of = 64, 8

    def step(i, carry):
        cols = [pl.ds(pl.multiple_of((i * tiles_of + k) * LANES, LANES), LANES) for k in range(tiles_of)]
        states = [None] * tiles_of
        for start in range(0, score.shape[0], rows):
            fs = [wide_f[start + k : start + k + 8, :] for k in range(0, rows, 8)]
            for k, col in enumerate(cols):
                terms = [score[start + 8 * n : start + 8 * n + 8, col] + f for n, f in enumerate(fs)]
                states[k] = onward(states[k], terms)
        for k, (top, whole) in enumerate(states):
            high = jnp.max(top, axis=0, keepdims=True)
            whole = jnp.sum(whole * jnp.exp2(top - high), axis=0, keepdims=True)
            sums[pl.ds(first + i * tiles_of + k, 1), :] = high + jnp.log(whole) * LOG2E
        return carry

    lax.fori_loop(0, score.shape[1] // (LANES * tiles_of), step, 0)


def spread_rows(values, wide):
    for t in range(values.shape[0]):
        wide[t * 8 : (t + 1) * 8, :] = jnp.broadcast_to(values[t : t + 1, :], (8, LANES))


def spread_columns(values, wide):
    for r in range(values.shape[0]):
        wide[r * LANES : (r + 1) * LANES, :] = jnp.broadcast_to(values[r : r + 1, :], (LANES, LANES)).T


def padded(rows):
    have = jnp.concatenate(rows, axis=0)
    return jnp.concatenate([have, jnp.zeros((8 - have.shape[0], LANES), jnp.float32)], axis=0)


def fill_scores(lots, slots, score):
    scale = LOG2E / math.sqrt(lots.shape[1])
    step = 256
    for start in range(0, slots.shape[0], step):
        inner = lax.dot_general(
            lots[...], slots[start : start + step, :], (((1,), (1,)), ((), ())), preferred_element_type=jnp.float32
        )
        score[:, start : start + step] = inner * scale


def own_score_kernel(slots, *refs):
    blocks, (lots, score, peak, total, wide_g, sems) = refs[:2], refs[2:]
    own_rows = lots.shape[0] // LOT_SHARE
    me = place_in_lots()
    copies = []
    for d in range(LOT_SHARE):
        rows = pl.ds(pl.multiple_of((me ^ d) * own_rows, own_rows), own_rows)
        block = blocks[d % 2].at[pl.ds((d // 2) * own_rows, own_rows), :]
        copies.append(pltpu.make_async_copy(block, lots.at[rows, :], sems.at[d]))
    for copy in copies:
        copy.start()
    spread_rows(-square_rows(slots), wide_g)
    for copy in copies:
        copy.wait()
    fill_scores(lots, slots, score)
    row_pass([score], wide_g, peak, total)


def other_score_kernel(slots, lots, peak_before, total_before, own_mass, score, out, wide_g, peak, total):
    spread_rows(-square_rows(slots), wide_g)
    fill_scores(lots, slots, score)
    row_pass([score], wide_g, peak, total, (peak_before, total_before))
    own_rows = own_mass.shape[1]
    own_lots = lots[pl.ds(pl.multiple_of(place_in_lots() * own_rows, own_rows), own_rows), :]
    own = padded([jnp.log(own_mass[...]) * LOG2E, square_row(own_lots)])
    sums = jnp.concatenate([row_result(peak, total), own], axis=0)
    for n in range(LOT_SHARE):
        out[n * sums.shape[0] : (n + 1) * sums.shape[0], :] = sums


def row_of_each(gathered, shares, row):
    stride = gathered.shape[0] // shares
    return [gathered[n * stride + row : n * stride + row + 1, :] for n in range(shares)]


def log_sum_of(parts, shares, blocks):
    stride = parts.shape[0] // shares
    return joined([parts[n * stride : n * stride + blocks, :] for n in range(shares)])


def lot_update(parts, first, blocks):
    logs = jnp.concatenate(row_of_each(first, LOT_SHARE, blocks), axis=0)
    squares = jnp.concatenate(row_of_each(first, LOT_SHARE, blocks + 1), axis=0)
    pot = logs + squares - log_sum_of(parts, LOT_SHARE, blocks)
    return pot - squares


def own_core_first(halves):
    mine, other = halves if isinstance(halves, tuple) else (halves[:8, :], halves[8:, :])
    ahead = lax.axis_index("core") == 0
    return jnp.concatenate([jnp.where(ahead, mine, other), jnp.where(ahead, other, mine)], axis=0)


def slot_update(parts, first, blocks):
    logs = own_core_first(jnp.concatenate(row_of_each(first, SLOT_SHARE, blocks), axis=0))
    return logs - log_sum_of(parts, SLOT_SHARE, blocks)


def column_kernel(score_a, score_b, parts, first, own_mass, out, wide_f, sums):
    spread_columns(lot_update(parts, first, score_a.shape[0] // LANES), wide_f)
    column_pass(score_a, wide_f, sums, 0)
    column_pass(score_b, wide_f, sums, score_a.shape[1] // LANES)
    half = sums.shape[0] // 2
    mine, other = sums[:half, :], sums[half:, :]
    ahead = lax.axis_index("core") == 0
    extra = [padded([jnp.log(own_mass[...]) * LOG2E])] if out.shape[0] // SLOT_SHARE > sums.shape[0] else []
    same = jnp.concatenate([mine, other, *extra], axis=0)
    turned = jnp.concatenate([other, mine, *extra], axis=0)
    rows = same.shape[0]
    for n in range(SLOT_SHARE):
        low = n < SLOT_SHARE // 2
        out[n * rows : (n + 1) * rows, :] = jnp.where(ahead, same if low else turned, turned if low else same)


def row_kernel(score_a, score_b, parts, first, out, wide_g, peak, total):
    spread_rows(slot_update(parts, first, sum_tiles(score_a, score_b)), wide_g)
    row_pass([score_a, score_b], wide_g, peak, total)
    sums = row_result(peak, total)
    for n in range(LOT_SHARE):
        out[n * sums.shape[0] : (n + 1) * sums.shape[0], :] = sums


def sum_tiles(score_a, score_b):
    return (score_a.shape[1] + score_b.shape[1]) // LANES


def final_kernel(score_a, score_b, parts, first, wide_f, lots, slots_a, slots_b, out, wide_g, plan, row_sum):
    spread_rows(slot_update(parts, first, sum_tiles(score_a, score_b)), wide_g)

    def step(i, carry):
        rows = pl.ds(pl.multiple_of(i * 16, 16), 16)
        shift = wide_f[rows, :]
        whole = None
        n = 0
        for score in (score_a, score_b):
            for t in range(score.shape[1] // LANES):
                both = jnp.concatenate([wide_g[n * 8 : (n + 1) * 8, :]] * 2, axis=0)
                term = jnp.exp2(score[rows, t * LANES : (t + 1) * LANES] + shift + both)
                plan[rows, n * LANES : (n + 1) * LANES] = term.astype(jnp.bfloat16)
                whole = term if whole is None else whole + term
                n += 1
        row_sum[rows, :] = jnp.broadcast_to(jnp.sum(whole, axis=1, keepdims=True), whole.shape)
        return carry

    lax.fori_loop(0, plan.shape[0] // 16, step, 0, unroll=2)
    half = score_a.shape[1]
    step_cols = 256
    for start in range(0, lots.shape[1], step_cols):
        cols = slice(start, start + step_cols)
        moved = jnp.dot(plan[:, :half], slots_a[:, cols], preferred_element_type=jnp.float32)
        moved = moved + jnp.dot(plan[:, half:], slots_b[:, cols], preferred_element_type=jnp.float32)
        sums = jnp.concatenate([row_sum[...]] * (step_cols // LANES), axis=1)
        out[:, cols] = (sums * lots[:, cols].astype(jnp.float32) - moved).astype(out.dtype)


def call(kernel, outs, scratch, cost, *args, grant=12, far_args=0):
    near, far = pl.BlockSpec(memory_space=pltpu.VMEM), pl.BlockSpec(memory_space=pltpu.HBM)
    return pl.pallas_call(
        kernel,
        out_shape=outs,
        in_specs=[near] * (len(args) - far_args) + [far] * far_args,
        out_specs=[near] * len(outs),
        scratch_shapes=[pltpu.VMEM(*item) if isinstance(item, tuple) else item for item in scratch],
        compiler_params=pltpu.CompilerParams(vmem_limit_bytes=grant * 2**20),
        cost_estimate=pl.CostEstimate(flops=cost, bytes_accessed=0, transcendentals=cost // 1024),
    )(*args)


def exchange(values, members):
    return lax.all_to_all(values, ALL, 0, 0, tiled=True, axis_index_groups=members)


def to_place(values, d):
    return lax.ppermute(values, ALL, [(group[i], group[i ^ d]) for group in LOT_GROUPS for i in range(LOT_SHARE)])


def local(lot_features, slot_features, lot_mass, slot_mass):
    own_rows, width = lot_features.shape
    lot_at = lax.axis_index("x") * SIZES["z"] + lax.axis_index("z")
    slot_at = lax.axis_index("y") * SIZES["core"] + lax.axis_index("core")
    own_lot_mass = lax.dynamic_slice_in_dim(lot_mass, lot_at * own_rows, own_rows, 0).reshape(1, own_rows)
    own_slot_mass = lax.dynamic_slice_in_dim(slot_mass, slot_at * own_rows, own_rows, 0).reshape(1, own_rows)

    core_share = SLOT_SHARE // 2
    slots_a = exchange(jnp.tile(slot_features, (core_share, 1)), CORE_SLOT_GROUPS)
    near = jnp.concatenate([lot_features] + [to_place(lot_features, d) for d in range(2, LOT_SHARE, 2)], axis=0)
    blocks = [near, to_place(near, 1)]
    slots_a, blocks = lax.optimization_barrier((slots_a, blocks))
    slots_b = lax.ppermute(slots_a, "core", [(0, 1), (1, 0)])

    n, half = LOT_SHARE * own_rows, core_share * own_rows
    lot_blocks, slot_blocks = n // LANES, 2 * half // LANES
    f32 = jnp.float32

    def shape(*dims, dtype=f32):
        return jax.ShapeDtypeStruct(dims, dtype)

    wide_g, half_g = ((slot_blocks * 8, LANES), f32), ((slot_blocks * 4, LANES), f32)
    wide_f = ((n, LANES), f32)
    work = n * half * 8

    lots, score_a, peak, total = call(
        own_score_kernel,
        [shape(n, width, dtype=lot_features.dtype), shape(n, half), shape(n, LANES), shape(n, LANES)],
        [half_g, pltpu.SemaphoreType.DMA((LOT_SHARE,))],
        work,
        slots_a, *blocks, far_args=2,
    )
    score_b, out = call(
        other_score_kernel,
        [shape(n, half), shape(LOT_SHARE * (lot_blocks + 8), LANES)],
        [half_g, wide_f, wide_f],
        work,
        slots_b, lots, peak, total, own_lot_mass,
    )
    out, own_slot_mass = lax.optimization_barrier((out, own_slot_mass))
    first_lot = lot_parts = exchange(out, LOT_GROUPS)
    first_slot = None
    for step in range(ITERS):
        extra = 8 if step == 0 else 0
        out, f = call(
            column_kernel,
            [shape(SLOT_SHARE * (slot_blocks + extra), LANES), shape(n, LANES)],
            [((slot_blocks, LANES), f32)],
            work,
            score_a, score_b, lot_parts, first_lot, own_slot_mass,
        )
        slot_parts = exchange(out, SLOT_GROUPS)
        if step == 0:
            first_slot = slot_parts
        if step < ITERS - 1:
            (out,) = call(
                row_kernel,
                [shape(LOT_SHARE * lot_blocks, LANES)],
                [wide_g, wide_f, wide_f],
                work,
                score_a, score_b, slot_parts, first_slot,
            )
            lot_parts = exchange(out, LOT_GROUPS)

    (partial,) = call(
        final_kernel,
        [shape(n, width, dtype=jnp.bfloat16)],
        [wide_g, ((n, 2 * half), jnp.bfloat16), wide_f],
        work,
        score_a, score_b, slot_parts, first_slot, f, lots, slots_a, slots_b,
    )
    shares = exchange(partial, LOT_GROUPS).astype(f32)
    return jnp.sum(shares.reshape(LOT_SHARE, own_rows, width), axis=0)


def solution(mesh):
    fine = Mesh(mesh.devices.reshape(tuple(SIZES.values())), ALL)
    placed = (P(ALL, None), P(("x", "z", "y", "core"), None), P(("y", "core")), P(("x", "z")))
    return jax.shard_map(local, mesh=fine, in_specs=placed, out_specs=P(ALL, None), check_vma=False)
```

time: 470 us -> 138 us (0.29)
  blocking collectives: 244 us -> 80.8 us
  waiting for transfers between devices: 137 us -> 10.2 us
  other arithmetic: 54.2 us -> 0.85 us
  Pallas kernels: 0 us -> 24.5 us
  starting transfers between devices: 0.08 us -> 16.6 us
  between operations: 13.6 us -> 0.1 us
  matrix products: 12.3 us -> 0 us
    all_gather x12 -> x0, blocking collectives: 212 us -> none  [combined_all(): pieces = jax.tree.map(lambda part: lax.all_gather(part, axis), value)]
    all_to_all x0 -> x7, blocking collectives: none -> 80.8 us  [exchange(): lax.all_to_all(values, ALL, 0, 0, tiled=True, axis_index_groups=members)]
    all_gather x2 -> x0, waiting for transfers between devices: 72.4 us -> none  [the longest x1 44.3 us: local(): lot_full = lax.all_gather(lot_features, 'cols', axis=0, tiled=True)]
    psum x1 -> x0, waiting for transfers between devices: 62.9 us -> none  [local(): moved_sum, row_sum = lax.psum((moved, row_total), 'cols')]
    psum x1 -> x0, blocking collectives: 32.2 us -> none  [local(): moved_sum, row_sum = lax.psum((moved, row_total), 'cols')]
    reduce_sum x9 -> x1, other arithmetic: 28.7 us -> 0.85 us  [local(): return jnp.sum(shares.reshape(LOT_SHARE, own_rows, width), axis=0)]
    pallas_call x0 -> x8, Pallas kernels: none -> 24.5 us  [call(): pl.pallas_call(kernel, out_shape=outs, in_specs=[near] * (len(args) - far...]
    reduce_max x5 -> x0, other arithmetic: 20.2 us -> none  [the longest x3 12.2 us: local(): peaks = jnp.max(scores, axis=0)]
  transfers between devices with their start and end apart: 3 -> 6, of which waited for: 3 -> 1; matrix products, arithmetic and copies ran while one was open for 2% -> 3% of each run, Pallas kernels for 0% -> 3%
where the time goes in v2:
time: 138 us; the launch traced here: 137 us
  blocking collectives  80.8 us (59%)
  Pallas kernels  24.5 us (18%)
  starting transfers between devices  16.6 us (12%)
  waiting for transfers between devices  10.2 us (7%)
  local copies, waits for them, and re-layouts  3.75 us (3%)
    all_to_all x7, blocking collectives, exchange(): lax.all_to_all(values, ALL, 0, 0, tiled=True, axis_index_groups=members)  80.8 us
    pallas_call x8, Pallas kernels, call(): pl.pallas_call(kernel, out_shape=outs, in_specs=[near] * (len(args) - far...  24.5 us
    ppermute x4, waiting for transfers between devices, to_place(): lax.ppermute(values, ALL, [(group[i], group[i ^ d]) for group in LOT_GROU...  10.2 us
    ppermute x4, starting transfers between devices, to_place(): lax.ppermute(values, ALL, [(group[i], group[i ^ d]) for group in LOT_GROU...  8.18 us
    all_to_all x1, starting transfers between devices, exchange(): lax.all_to_all(values, ALL, 0, 0, tiled=True, axis_index_groups=members)  5.71 us
  transfers between devices with their start and end apart: 6, of which 1 were waited for; matrix products, arithmetic and copies ran while one was open for 3% of the time, Pallas kernels for 3%

profile of v2, /device:TPU:1, one launch (start us, length us, event | category | flops | bytes accessed | tf_op | source)
XLA Modules:
  0.0 136.7 jit_solution(7240603661483034142)
XLA Ops:
  0.0 0.0 copy-start
  0.0 2.0 %collective-permute-start = (bf16[128,512]{1,0:T(8,128)(2,1)}, bf16[128,512]{1,0:T(8,128)(2,1)S(1)}, u32[]{:S(2)}, u32[]{:S(2)}) collective-permute-start(bf16[128,512]{1,0:T(8,128)(2,1)} %param.4), channel_id=1, source_target_pairs={{1,5},{2,6},{5,1},{6,2},{9,13},{10,14},{13,9},{14,10},{17,21},{18,... | collective-permute-start | bytes 393224 | tf_op jit(solution)/shard_map/ppermute | solution.py:298
  2.0 2.5 %collective-permute-start.1 = (bf16[128,512]{1,0:T(8,128)(2,1)}, bf16[128,512]{1,0:T(8,128)(2,1)S(1)}, u32[]{:S(2)}, u32[]{:S(2)}) collective-permute-start(bf16[128,512]{1,0:T(8,128)(2,1)} %param.4), channel_id=1, source_target_pairs={{1,9},{2,10},{5,13},{6,14},{9,1},{10,2},{13,5},{14,6},{17,25},{18,... | collective-permute-start | bytes 393224 | tf_op jit(solution)/shard_map/ppermute | solution.py:298
  4.5 0.0 collective-permute-start.2
  4.5 2.0 %tile.2 = bf16[8,128,512]{2,1,0:T(8,128)(2,1)} broadcast(bf16[128,512]{1,0:T(8,128)(2,1)} %param.5), dimensions={1,2} | broadcast | bytes 1179648 | tf_op jit(solution)/shard_map/tile | solution.py:309
  6.5 5.7 %all-to-all-start = ((bf16[8,128,512]{2,1,0:T(8,128)(2,1)}), bf16[8,128,512]{2,1,0:T(8,128)(2,1)S(1)}, u32[]{:S(2)}, u32[]{:S(2)}) async-start(bf16[8,128,512]{2,1,0:T(8,128)(2,1)} %tile.2), calls=%async_computation | async-start | bytes 2097152 | tf_op jit(solution)/shard_map/all_to_all | solution.py:294
  12.2 0.9 constant_dynamic-update-slice_fusion.3
  13.1 0.0 collective-permute-done
  13.2 0.0 collective-permute-done.1
  13.2 0.0 collective-permute-done.2
  13.2 3.7 %collective-permute-start.3 = (bf16[512,512]{1,0:T(8,128)(2,1)S(1)}, bf16[512,512]{1,0:T(8,128)(2,1)S(1)}, u32[]{:S(2)}, u32[]{:S(2)}) collective-permute-start(bf16[512,512]{1,0:T(8,128)(2,1)S(1)} %constant_dynamic-update-slice_fusion.refs_0_), channel_id=1, source_target_pairs={{1,2},{2,1},{5,6},{6,5},{9,10},{10,9},{13,14},{14,13},{17,18},{18,... | collective-permute-start | bytes 1572872 | tf_op jit(solution)/shard_map/ppermute | solution.py:298
  16.9 10.2 %collective-permute-done.3.refs_1_ = bf16[512,512]{1,0:T(8,128)(2,1)S(1)} collective-permute-done((bf16[512,512]{1,0:T(8,128)(2,1)S(1)}, bf16[512,512]{1,0:T(8,128)(2,1)S(1)}, u32[]{:S(2)}, u32[]{:S(2)}) %collective-permute-start.3) | collective-permute-done | bytes 524320 | tf_op jit(solution)/shard_map/ppermute | solution.py:298
  27.0 0.0 all-to-all-done
  27.0 2.7 %collective-permute-start.4 = (bf16[1024,512]{1,0:T(8,128)(2,1)S(1)}, bf16[1024,512]{1,0:T(8,128)(2,1)S(1)}, u32[]{:S(2)}, u32[]{:S(2)}) collective-permute-start(bf16[1024,512]{1,0:T(8,128)(2,1)S(1)} %bitcast.18), channel_id=1, source_target_pairs={{0,16},{16,0},{1,17},{17,1},{2,18},{18,2},{3,19},{19,3},{4,20},{20... | collective-permute-start | bytes 3145736 | tf_op jit(solution)/shard_map/ppermute | solution.py:313
  29.8 0.8 dynamic-slice_bitcast_fusion.own_mass
  30.5 0.0 copy-done
  30.5 0.1 dynamic-slice_bitcast_fusion.1.own_mass
  30.6 3.8 %shard_map.46 = (bf16[1024,512]{1,0:T(8,128)(2,1)S(1)}, f32[1024,1024]{1,0:T(8,128)S(1)}, f32[1024,128]{1,0:T(8,128)S(1)}, f32[1024,128]{1,0:T(8,128)S(1)}) custom-call(bf16[1024,512]{1,0:T(8,128)(2,1)S(1)} %bitcast.19, bf16[512,512]{1,0:T(8,128)(2,1)S(1)} %constant_dynamic-update-slice_fusion.refs_0_, bf16[512,512]{1,0:T(8,128)(2,1)S(1)} %collective-permute-done.3.refs_1_), custom_call_target="tpu_custom_call" | custom-call | flops 8388608 | tf_op jit(solution)/shard_map/pallas_call | solution.py:282
  34.4 0.0 collective-permute-done.4.slots.slots_b
  34.4 2.7 %shard_map.47 = (f32[1024,1024]{1,0:T(8,128)S(1)}, f32[128,128]{1,0:T(8,128)S(1)}) custom-call(bf16[1024,512]{1,0:T(8,128)(2,1)S(1)} %collective-permute-done.4.slots.slots_b, bf16[1024,512]{1,0:T(8,128)(2,1)S(1)} %get-tuple-element.24.lots, f32[1024,128]{1,0:T(8,128)S(1)} %get-tuple-element.25.peak_before, f32[1024,128]{1,0:T(8,128)S(1)} %get-tuple-element.26.total_before, ...), custom_call_target="tpu_custom_call" | custom-call | flops 8388608 | tf_op jit(solution)/shard_map/pallas_call | solution.py:282
  37.1 10.7 %all_to_all.84 = f32[8,16,128]{2,1,0:T(8,128)S(1)} all-to-all(f32[8,16,128]{2,1,0:T(8,128)S(1)} %bitcast.39), channel_id=1, replica_groups={{1,2,5,6,9,10,13,14},{17,18,21,22,25,26,29,30},{3,0,7,4,11,8,15,12},{19..., dimensions={0} | all-to-all | bytes 131072 | tf_op jit(solution)/shard_map/all_to_all | solution.py:294
  47.8 2.6 %shard_map.48 = (f32[384,128]{1,0:T(8,128)S(1)}, f32[1024,128]{1,0:T(8,128)}) custom-call(f32[1024,1024]{1,0:T(8,128)S(1)} %get-tuple-element.23.score_a, f32[1024,1024]{1,0:T(8,128)S(1)} %get-tuple-element.27.score_b, f32[128,128]{1,0:T(8,128)S(1)} %bitcast.26, f32[128,128]{1,0:T(8,128)S(1)} %bitcast.27, f32[1,128]{1,0:T(1,128)S(1)} %dynamic-slice_bitcast_fusion.own_mass), custom_call_target="tpu_custom_call" | custom-call | flops 8388608 | tf_op jit(solution)/shard_map/pallas_call | solution.py:282
  50.4 11.8 %all_to_all.85 = f32[16,24,128]{2,1,0:T(8,128)S(1)} all-to-all(f32[16,24,128]{2,1,0:T(8,128)S(1)} %bitcast.32), channel_id=1, replica_groups={{0,1,32,33,64,65,96,97,16,17,48,49,80,81,112,113},{2,3,34,35,66,67,98,9..., dimensions={0} | all-to-all | bytes 393216 | tf_op jit(solution)/shard_map/all_to_all | solution.py:294
  62.2 2.2 %shard_map.49 = f32[64,128]{1,0:T(8,128)S(1)} custom-call(f32[1024,1024]{1,0:T(8,128)S(1)} %get-tuple-element.23.score_a, f32[1024,1024]{1,0:T(8,128)S(1)} %get-tuple-element.27.score_b, f32[384,128]{1,0:T(8,128)S(1)} %bitcast.21, f32[384,128]{1,0:T(8,128)S(1)} %bitcast.22), custom_call_target="tpu_custom_call" | custom-call | flops 8388608 | tf_op jit(solution)/shard_map/pallas_call | solution.py:282
  64.4 8.7 %all_to_all.86 = f32[8,8,128]{2,1,0:T(8,128)S(1)} all-to-all(f32[8,8,128]{2,1,0:T(8,128)S(1)} %bitcast.36), channel_id=1, replica_groups={{1,2,5,6,9,10,13,14},{17,18,21,22,25,26,29,30},{3,0,7,4,11,8,15,12},{19..., dimensions={0} | all-to-all | bytes 65536 | tf_op jit(solution)/shard_map/all_to_all | solution.py:294
  73.1 2.6 %shard_map.50 = (f32[256,128]{1,0:T(8,128)S(1)}, f32[1024,128]{1,0:T(8,128)}) custom-call(f32[1024,1024]{1,0:T(8,128)S(1)} %get-tuple-element.23.score_a, f32[1024,1024]{1,0:T(8,128)S(1)} %get-tuple-element.27.score_b, f32[64,128]{1,0:T(8,128)S(1)} %bitcast.34, f32[128,128]{1,0:T(8,128)S(1)} %bitcast.28, f32[1,128]{1,0:T(1,128)S(1)} %dynamic-slice_bitcast_fusion.own_mass), custom_call_target="tpu_custom_call" | custom-call | flops 8388608 | tf_op jit(solution)/shard_map/pallas_call | solution.py:282
  75.8 11.5 %all_to_all.87 = f32[16,16,128]{2,1,0:T(8,128)S(1)} all-to-all(f32[16,16,128]{2,1,0:T(8,128)S(1)} %bitcast.38), channel_id=1, replica_groups={{0,1,32,33,64,65,96,97,16,17,48,49,80,81,112,113},{2,3,34,35,66,67,98,9..., dimensions={0} | all-to-all | bytes 262144 | tf_op jit(solution)/shard_map/all_to_all | solution.py:294
  87.2 2.2 %shard_map.51 = f32[64,128]{1,0:T(8,128)S(1)} custom-call(f32[1024,1024]{1,0:T(8,128)S(1)} %get-tuple-element.23.score_a, f32[1024,1024]{1,0:T(8,128)S(1)} %get-tuple-element.27.score_b, f32[256,128]{1,0:T(8,128)S(1)} %bitcast.31, f32[384,128]{1,0:T(8,128)S(1)} %bitcast.23), custom_call_target="tpu_custom_call" | custom-call | flops 8388608 | tf_op jit(solution)/shard_map/pallas_call | solution.py:282
  89.4 8.7 %all_to_all.88 = f32[8,8,128]{2,1,0:T(8,128)S(1)} all-to-all(f32[8,8,128]{2,1,0:T(8,128)S(1)} %bitcast.35), channel_id=1, replica_groups={{1,2,5,6,9,10,13,14},{17,18,21,22,25,26,29,30},{3,0,7,4,11,8,15,12},{19..., dimensions={0} | all-to-all | bytes 65536 | tf_op jit(solution)/shard_map/all_to_all | solution.py:294
  98.1 2.0 %shard_map.52 = (f32[256,128]{1,0:T(8,128)S(1)}, f32[1024,128]{1,0:T(8,128)S(1)}) custom-call(f32[1024,1024]{1,0:T(8,128)S(1)} %get-tuple-element.23.score_a, f32[1024,1024]{1,0:T(8,128)S(1)} %get-tuple-element.27.score_b, f32[64,128]{1,0:T(8,128)S(1)} %bitcast.33, f32[128,128]{1,0:T(8,128)S(1)} %bitcast.29, f32[1,128]{1,0:T(1,128)S(1)} %dynamic-slice_bitcast_fusion.own_mass), custom_call_target="tpu_custom_call" | custom-call | flops 8388608 | tf_op jit(solution)/shard_map/pallas_call | solution.py:282
  100.1 10.6 %all_to_all.89 = f32[16,16,128]{2,1,0:T(8,128)S(1)} all-to-all(f32[16,16,128]{2,1,0:T(8,128)S(1)} %bitcast.37), channel_id=1, replica_groups={{0,1,32,33,64,65,96,97,16,17,48,49,80,81,112,113},{2,3,34,35,66,67,98,9..., dimensions={0} | all-to-all | bytes 262144 | tf_op jit(solution)/shard_map/all_to_all | solution.py:294
  110.7 6.5 %shard_map.53 = bf16[1024,512]{1,0:T(8,128)(2,1)S(1)} custom-call(f32[1024,1024]{1,0:T(8,128)S(1)} %get-tuple-element.23.score_a, f32[1024,1024]{1,0:T(8,128)S(1)} %get-tuple-element.27.score_b, f32[256,128]{1,0:T(8,128)S(1)} %bitcast.30, f32[384,128]{1,0:T(8,128)S(1)} %bitcast.24, f32[1024,128]{1,0:T(8,128)S(1)} %get-tuple-element.34.wide_f, ...), custom_call_target="tpu_custom_call" | custom-call | flops 8388608 | tf_op jit(solution)/shard_map/pallas_call | solution.py:282
  117.1 18.8 %all_to_all.90 = bf16[8,128,512]{2,1,0:T(8,128)(2,1)S(1)} all-to-all(bf16[8,128,512]{2,1,0:T(8,128)(2,1)S(1)} %bitcast.25), channel_id=1, replica_groups={{1,2,5,6,9,10,13,14},{17,18,21,22,25,26,29,30},{3,0,7,4,11,8,15,12},{19..., dimensions={0} | all-to-all | bytes 2097152 | tf_op jit(solution)/shard_map/all_to_all | solution.py:294
  135.9 0.8 convert_reduce_fusion
  (3 shorter events, 0.0 us)
Async XLA Ops:
  0.0 30.5 %copy-start = (f32[2048]{0:T(1024)S(1)}, f32[2048]{0:T(1024)}, u32[]{:S(2)}) copy-start(f32[2048]{0:T(1024)} %param.6) | copy-start | bytes 24580
  0.0 13.1 %collective-permute-start = (bf16[128,512]{1,0:T(8,128)(2,1)}, bf16[128,512]{1,0:T(8,128)(2,1)S(1)}, u32[]{:S(2)}, u32[]{:S(2)}) collective-permute-start(bf16[128,512]{1,0:T(8,128)(2,1)} %param.4), channel_id=1, source_target_pairs={{1,5},{2,6},{5,1},{6,2},{9,13},{10,14},{13,9},{14,10},{17,21},{18,... | collective-permute-start | bytes 393224 | tf_op jit(solution)/shard_map/ppermute | solution.py:298
  2.0 11.1 %collective-permute-start.1 = (bf16[128,512]{1,0:T(8,128)(2,1)}, bf16[128,512]{1,0:T(8,128)(2,1)S(1)}, u32[]{:S(2)}, u32[]{:S(2)}) collective-permute-start(bf16[128,512]{1,0:T(8,128)(2,1)} %param.4), channel_id=1, source_target_pairs={{1,9},{2,10},{5,13},{6,14},{9,1},{10,2},{13,5},{14,6},{17,25},{18,... | collective-permute-start | bytes 393224 | tf_op jit(solution)/shard_map/ppermute | solution.py:298
  4.5 8.7 %collective-permute-start.2 = (bf16[128,512]{1,0:T(8,128)(2,1)}, bf16[128,512]{1,0:T(8,128)(2,1)S(1)}, u32[]{:S(2)}, u32[]{:S(2)}) collective-permute-start(bf16[128,512]{1,0:T(8,128)(2,1)} %param.4), channel_id=1, source_target_pairs={{1,13},{2,14},{5,9},{6,10},{9,5},{10,6},{13,1},{14,2},{17,29},{18,... | collective-permute-start | bytes 393224 | tf_op jit(solution)/shard_map/ppermute | solution.py:298
  6.5 20.5 %all-to-all-start = ((bf16[8,128,512]{2,1,0:T(8,128)(2,1)}), bf16[8,128,512]{2,1,0:T(8,128)(2,1)S(1)}, u32[]{:S(2)}, u32[]{:S(2)}) async-start(bf16[8,128,512]{2,1,0:T(8,128)(2,1)} %tile.2), calls=%async_computation | async-start | bytes 2097152 | tf_op jit(solution)/shard_map/all_to_all | solution.py:294
  13.2 13.8 %collective-permute-start.3 = (bf16[512,512]{1,0:T(8,128)(2,1)S(1)}, bf16[512,512]{1,0:T(8,128)(2,1)S(1)}, u32[]{:S(2)}, u32[]{:S(2)}) collective-permute-start(bf16[512,512]{1,0:T(8,128)(2,1)S(1)} %constant_dynamic-update-slice_fusion.refs_0_), channel_id=1, source_target_pairs={{1,2},{2,1},{5,6},{6,5},{9,10},{10,9},{13,14},{14,13},{17,18},{18,... | collective-permute-start | bytes 1572872 | tf_op jit(solution)/shard_map/ppermute | solution.py:298
  27.0 7.4 %collective-permute-start.4 = (bf16[1024,512]{1,0:T(8,128)(2,1)S(1)}, bf16[1024,512]{1,0:T(8,128)(2,1)S(1)}, u32[]{:S(2)}, u32[]{:S(2)}) collective-permute-start(bf16[1024,512]{1,0:T(8,128)(2,1)S(1)} %bitcast.18), channel_id=1, source_target_pairs={{0,16},{16,0},{1,17},{17,1},{2,18},{18,2},{3,19},{19,3},{4,20},{20... | collective-permute-start | bytes 3145736 | tf_op jit(solution)/shard_map/ppermute | solution.py:313

commit v3 on v2

v3 whole, which is shorter than its diff:
```python
import math

import jax
import jax.numpy as jnp
from jax import lax
from jax.experimental import pallas as pl
from jax.experimental.pallas import tpu as pltpu
from jax.sharding import Mesh, PartitionSpec as P

ITERS = 3
LOG2E = math.log2(math.e)
LANES = 128

SIZES = {"y": 4, "core": 2, "x": 4, "z": 4}
ALL = tuple(SIZES)
FULL, PAIRS, ACROSS, EACH = [(0, 1, 2, 3)], [(0, 1), (2, 3)], [(1, 2), (3, 0)], [(0,), (1,), (2,), (3,)]


def groups(ys, cores, xs, zs):
    return [
        [((y * 2 + core) * 4 + x) * 4 + z for core in cs for x in px for y in py for z in pz]
        for px in xs
        for py in ys
        for pz in zs
        for cs in cores
    ]


LOT_GROUPS = groups(EACH, [(0,), (1,)], FULL, PAIRS)
SLOT_GROUPS = groups(FULL, [(0, 1)], EACH, ACROSS)
CORE_SLOT_GROUPS = groups(FULL, [(0,), (1,)], EACH, ACROSS)
LOT_SHARE, SLOT_SHARE = 8, 16
CHUNKS = 2


def place_in_lots():
    return lax.axis_index("x") * 2 + lax.axis_index("z") % 2


def lane_sum(values):
    total = values[:, :LANES]
    for start in range(LANES, values.shape[1], LANES):
        total = total + values[:, start : start + LANES]
    return jnp.sum(total.T, axis=0, keepdims=True)


def square_row(block):
    wide = block.astype(jnp.float32)
    return lane_sum(wide * wide) * (0.5 * LOG2E / math.sqrt(block.shape[1]))


def square_rows(features):
    return jnp.concatenate([square_row(features[start : start + LANES, :]) for start in range(0, features.shape[0], LANES)], axis=0)


def joined(parts):
    top = parts[0]
    for part in parts[1:]:
        top = jnp.maximum(top, part)
    total = jnp.exp2(parts[0] - top)
    for part in parts[1:]:
        total = total + jnp.exp2(part - top)
    return top + jnp.log(total) * LOG2E


def in_pairs(join, terms):
    while len(terms) > 1:
        terms = [join(*terms[i : i + 2]) if i + 1 < len(terms) else terms[i] for i in range(0, len(terms), 2)]
    return terms[0]


def peak_of(terms):
    return in_pairs(jnp.maximum, terms)


def fold(terms, top):
    return in_pairs(jnp.add, [jnp.exp2(term - top) for term in terms])


def onward(state, terms):
    top = peak_of(terms)
    if state is None:
        return top, fold(terms, top)
    top = jnp.maximum(top, state[0])
    return top, state[1] * jnp.exp2(state[0] - top) + fold(terms, top)


def row_pass(score, wide_g, peak, total, first):
    groups_of, tiles_of = 8, 8

    def step(i, carry):
        rows = [pl.multiple_of(i * 8 * groups_of + 8 * r, 8) for r in range(groups_of)]
        states = [None] * groups_of
        for start in range(0, score.shape[1] // LANES, tiles_of):
            gs = [wide_g[(start + k) * 8 : (start + k + 1) * 8, :] for k in range(tiles_of)]
            for r, row in enumerate(rows):
                terms = [score[pl.ds(row, 8), (start + k) * LANES : (start + k + 1) * LANES] + g for k, g in enumerate(gs)]
                states[r] = onward(states[r], terms)
        for row, (top, whole) in zip(rows, states, strict=True):
            peak[pl.ds(first + row, 8), :] = top
            total[pl.ds(first + row, 8), :] = whole
        return carry

    lax.fori_loop(0, score.shape[0] // (8 * groups_of), step, 0)


def row_result(peak, total):
    out = []
    for start in range(0, peak.shape[0], LANES):
        tops = peak[start : start + LANES, :].T
        sums = total[start : start + LANES, :].T
        top = jnp.max(tops, axis=0, keepdims=True)
        whole = jnp.sum(sums * jnp.exp2(tops - top), axis=0, keepdims=True)
        out.append(top + jnp.log(whole) * LOG2E)
    return jnp.concatenate(out, axis=0)


def column_pass(scores, wide_f, sums):
    rows, tiles_of = 64, 8
    below = scores[0].shape[0]

    def step(i, carry):
        cols = [pl.ds(pl.multiple_of((i * tiles_of + k) * LANES, LANES), LANES) for k in range(tiles_of)]
        states = [None] * tiles_of
        for start in range(0, wide_f.shape[0], rows):
            score, at = scores[start // below], start % below
            fs = [wide_f[start + k : start + k + 8, :] for k in range(0, rows, 8)]
            for k, col in enumerate(cols):
                terms = [score[at + 8 * n : at + 8 * n + 8, col] + f for n, f in enumerate(fs)]
                states[k] = onward(states[k], terms)
        for k, (top, whole) in enumerate(states):
            high = jnp.max(top, axis=0, keepdims=True)
            whole = jnp.sum(whole * jnp.exp2(top - high), axis=0, keepdims=True)
            sums[pl.ds(i * tiles_of + k, 1), :] = high + jnp.log(whole) * LOG2E
        return carry

    lax.fori_loop(0, sums.shape[0] // tiles_of, step, 0)


def spread_rows(values, wide):
    for t in range(values.shape[0]):
        wide[t * 8 : (t + 1) * 8, :] = jnp.broadcast_to(values[t : t + 1, :], (8, LANES))


def padded(rows):
    have = jnp.concatenate(rows, axis=0)
    return jnp.concatenate([have, jnp.zeros((8 - have.shape[0], LANES), jnp.float32)], axis=0)


def fill_scores(lots, slots, score, first):
    scale = LOG2E / math.sqrt(lots.shape[1])
    step = 256
    for start in range(0, slots.shape[0], step):
        inner = lax.dot_general(
            lots[...], slots[start : start + step, :], (((1,), (1,)), ((), ())), preferred_element_type=jnp.float32
        )
        score[:, first + start : first + start + step] = inner * scale


STEPS = (0, 2, 4, 6, 1, 3, 5, 7)


def to_places(rows, placed, blocks):
    me = place_in_lots()
    for n, b in enumerate(blocks):
        placed[pl.ds(me ^ STEPS[b], 1), :] = rows[n : n + 1, :]


def send_to_lots(values, out):
    rows = values.shape[0]
    for n in range(LOT_SHARE):
        out[n * rows : (n + 1) * rows, :] = values


def gather_rows(parts, lots):
    rows = parts[0].shape[0]
    for n, part in enumerate(parts):
        lots[n * rows : (n + 1) * rows, :] = part[...]


def own_kernel(lots, lot_mass, slot_mass, own_lots, lot_rows, slot_rows):
    own_lots[...] = lots[...]
    masses = lot_mass[pl.ds(lax.axis_index("x") * SIZES["z"] + lax.axis_index("z"), 1), :]
    lot_rows[...] = padded([jnp.log(masses) * LOG2E, square_row(lots[...])])
    masses = slot_mass[pl.ds(lax.axis_index("y") * SIZES["core"] + lax.axis_index("core"), 1), :]
    slot_rows[...] = padded([jnp.log(masses) * LOG2E])


def near_score_kernel(slots_a, slots_b, lot_rows, *refs):
    parts, (score, near, wide_g, placed, peak, total) = refs[: LOT_SHARE // 2], refs[LOT_SHARE // 2 :]
    gather_rows(parts, near)
    half = slots_a.shape[0]
    spread_rows(-jnp.concatenate([square_rows(slots_a), square_rows(slots_b)], axis=0), wide_g)
    fill_scores(near, slots_a, score, 0)
    fill_scores(near, slots_b, score, half)
    row_pass(score, wide_g, peak, total, 0)
    to_places(row_result(peak, total), placed, range(LOT_SHARE // 2))
    placed[LOT_SHARE:, :] = lot_rows[...]


def far_score_kernel(slots_a, slots_b, wide_g, placed_before, *refs):
    parts, (score, far, out, placed, peak, total) = refs[: LOT_SHARE // 2], refs[LOT_SHARE // 2 :]
    gather_rows(parts, far)
    half = slots_a.shape[0]
    fill_scores(far, slots_a, score, 0)
    fill_scores(far, slots_b, score, half)
    row_pass(score, wide_g, peak, total, 0)
    placed[...] = placed_before[...]
    to_places(row_result(peak, total), placed, range(LOT_SHARE // 2, LOT_SHARE))
    send_to_lots(placed[...], out)


def row_of_each(gathered, shares, row):
    stride = gathered.shape[0] // shares
    return [gathered[n * stride + row : n * stride + row + 1, :] for n in range(shares)]


def log_sum_of(parts, shares, blocks):
    stride = parts.shape[0] // shares
    return joined([parts[n * stride : n * stride + blocks, :] for n in range(shares)])


def lot_update(parts, first, blocks):
    logs = jnp.concatenate(row_of_each(first, LOT_SHARE, blocks), axis=0)
    squares = jnp.concatenate(row_of_each(first, LOT_SHARE, blocks + 1), axis=0)
    pot = logs + squares - log_sum_of(parts, LOT_SHARE, blocks)
    return pot - squares


def own_core_first(rows):
    half = rows.shape[0] // 2
    low, high = rows[:half, :], rows[half:, :]
    ahead = lax.axis_index("core") == 0
    return jnp.concatenate([jnp.where(ahead, low, high), jnp.where(ahead, high, low)], axis=0)


def slot_update(parts, first, blocks):
    logs = own_core_first(jnp.concatenate(row_of_each(first, SLOT_SHARE, blocks), axis=0))
    return logs - log_sum_of(parts, SLOT_SHARE, blocks)


def column_kernel(score_n, score_f, parts, first, slot_rows, out, wide_f, placed, sums):
    placed[...] = lot_update(parts, first, LOT_SHARE)
    me = place_in_lots()
    for b, step in enumerate(STEPS):
        row = placed[pl.ds(me ^ step, 1), :]
        wide_f[b * LANES : (b + 1) * LANES, :] = jnp.broadcast_to(row, (LANES, LANES)).T
    column_pass([score_n, score_f], wide_f, sums)
    half = sums.shape[0] // 2
    mine, other = sums[:half, :], sums[half:, :]
    ahead = lax.axis_index("core") == 0
    extra = [slot_rows[...]] if out.shape[0] // SLOT_SHARE > sums.shape[0] else []
    same = jnp.concatenate([mine, other, *extra], axis=0)
    turned = jnp.concatenate([other, mine, *extra], axis=0)
    rows = same.shape[0]
    for n in range(SLOT_SHARE):
        low = n < SLOT_SHARE // 2
        out[n * rows : (n + 1) * rows, :] = jnp.where(ahead, same if low else turned, turned if low else same)


def row_kernel(score_n, score_f, parts, first, out, wide_g, placed, peak, total):
    spread_rows(slot_update(parts, first, score_n.shape[1] // LANES), wide_g)
    row_pass(score_n, wide_g, peak, total, 0)
    row_pass(score_f, wide_g, peak, total, score_n.shape[0])
    to_places(row_result(peak, total), placed, range(LOT_SHARE))
    send_to_lots(placed[...], out)


def final_kernel(score_n, score_f, parts, first, wide_f, near, far, slots_a, slots_b, out, wide_g, *work):
    tiles = score_n.shape[1] // LANES
    spread_rows(slot_update(parts, first, tiles), wide_g)
    half, below, rows_of = slots_a.shape[0], score_n.shape[0], work[0].shape[0]
    plans, row_sums = work[: len(work) // 2], work[len(work) // 2 :]
    me = place_in_lots()

    def fill_plan(c):
        score, base = (score_n, 0) if c * rows_of < below else (score_f, below)
        for start in range(0, rows_of, 16):
            at = c * rows_of + start
            shift = wide_f[at : at + 16, :]
            wholes = []
            for t in range(tiles):
                cols = slice(t * LANES, (t + 1) * LANES)
                both = jnp.concatenate([wide_g[t * 8 : (t + 1) * 8, :]] * 2, axis=0)
                term = jnp.exp2(score[at - base : at - base + 16, cols] + (shift + both))
                plans[c][start : start + 16, cols] = term.astype(jnp.bfloat16)
                wholes.append(term)
            whole = jnp.sum(in_pairs(jnp.add, wholes), axis=1, keepdims=True)
            row_sums[c][start : start + 16, :] = jnp.broadcast_to(whole, (16, LANES))

    def finish(c):
        lots, base = (near, 0) if c * rows_of < below else (far, below)
        at = c * rows_of
        step_cols = 256
        for start in range(0, lots.shape[1], step_cols):
            cols = slice(start, start + step_cols)
            moved = jnp.dot(plans[c][:, :half], slots_a[:, cols], preferred_element_type=jnp.float32)
            moved = moved + jnp.dot(plans[c][:, half:], slots_b[:, cols], preferred_element_type=jnp.float32)
            sums = jnp.concatenate([row_sums[c][...]] * (step_cols // LANES), axis=1)
            grad = sums * lots[at - base : at - base + rows_of, cols].astype(jnp.float32) - moved
            for n in range(rows_of // LANES):
                to = pl.ds(pl.multiple_of((me ^ STEPS[at // LANES + n]) * LANES, LANES), LANES)
                out[to, cols] = grad[n * LANES : (n + 1) * LANES, :].astype(out.dtype)

    fill_plan(0)
    for c in range(len(plans)):
        if c + 1 < len(plans):
            fill_plan(c + 1)
        finish(c)


def call(kernel, outs, scratch, cost, *args, grant=12):
    near = pl.BlockSpec(memory_space=pltpu.VMEM)
    return pl.pallas_call(
        kernel,
        out_shape=outs,
        in_specs=[near] * len(args),
        out_specs=[near] * len(outs),
        scratch_shapes=[pltpu.VMEM(*item) for item in scratch],
        compiler_params=pltpu.CompilerParams(vmem_limit_bytes=grant * 2**20),
        cost_estimate=pl.CostEstimate(flops=cost, bytes_accessed=0, transcendentals=cost // 1024),
    )(*args)


def exchange(values, members):
    return lax.all_to_all(values, ALL, 0, 0, tiled=True, axis_index_groups=members)


def to_place(values, d):
    return lax.ppermute(values, ALL, [(group[i], group[i ^ d]) for group in LOT_GROUPS for i in range(LOT_SHARE)])


def local(lot_features, slot_features, lot_mass, slot_mass):
    own_rows, width = lot_features.shape
    lot_mass = lot_mass.reshape(-1, LANES)
    slot_mass = slot_mass.reshape(-1, LANES)

    slots_a = exchange(jnp.tile(slot_features, (SLOT_SHARE // 2, 1)), CORE_SLOT_GROUPS)
    near = [lot_features] + [to_place(lot_features, d) for d in range(2, LOT_SHARE, 2)]
    far = [to_place(part, 1) for part in near]
    n, m = LOT_SHARE * own_rows, SLOT_SHARE * own_rows
    slot_blocks = m // LANES
    f32 = jnp.float32

    def shape(*dims, dtype=f32):
        return jax.ShapeDtypeStruct(dims, dtype)

    own_lots, lot_rows, slot_rows = call(
        own_kernel,
        [shape(own_rows, width, dtype=lot_features.dtype), shape(8, LANES), shape(8, LANES)],
        [],
        own_rows * width,
        lot_features, lot_mass, slot_mass,
    )
    slots_a, near[1], near[2], near[3], far[0], far[1], far[2], own_lots, lot_rows, slot_rows = lax.optimization_barrier(
        (slots_a, *near[1:], *far[:3], own_lots, lot_rows, slot_rows)
    )
    slots_b = lax.ppermute(slots_a, "core", [(0, 1), (1, 0)])

    wide_g, placed, wide_f, half_f = ((slot_blocks * 8, LANES), (LOT_SHARE, LANES), (n, LANES), (n // 2, LANES))
    work = n * m * 4

    half_lots = shape(n // 2, width, dtype=lot_features.dtype)
    score_n, near, g, placed_n = call(
        near_score_kernel,
        [shape(n // 2, m), half_lots, shape(*wide_g), shape(LOT_SHARE + 8, LANES)],
        [(half_f, f32), (half_f, f32)],
        work // 2,
        slots_a, slots_b, lot_rows, own_lots, *near[1:],
    )
    score_f, far, out = call(
        far_score_kernel,
        [shape(n // 2, m), half_lots, shape(LOT_SHARE * (LOT_SHARE + 8), LANES)],
        [((LOT_SHARE + 8, LANES), f32), (half_f, f32), (half_f, f32)],
        work // 2,
        slots_a, slots_b, g, placed_n, *far,
    )
    first_lot = lot_parts = exchange(out, LOT_GROUPS)
    first_slot = None
    for step in range(ITERS):
        extra = 8 if step == 0 else 0
        out, f = call(
            column_kernel,
            [shape(SLOT_SHARE * (slot_blocks + extra), LANES), shape(*wide_f)],
            [(placed, f32), ((slot_blocks, LANES), f32)],
            work,
            score_n, score_f, lot_parts, first_lot, slot_rows,
        )
        slot_parts = exchange(out, SLOT_GROUPS)
        if step == 0:
            first_slot = slot_parts
        if step < ITERS - 1:
            (out,) = call(
                row_kernel,
                [shape(LOT_SHARE * LOT_SHARE, LANES)],
                [(wide_g, f32), (placed, f32), (wide_f, f32), (wide_f, f32)],
                work,
                score_n, score_f, slot_parts, first_slot,
            )
            lot_parts = exchange(out, LOT_GROUPS)
    (partial,) = call(
        final_kernel,
        [shape(n, width, dtype=jnp.bfloat16)],
        [(wide_g, f32)] + [((n // CHUNKS, m), jnp.bfloat16)] * CHUNKS + [((n // CHUNKS, LANES), f32)] * CHUNKS,
        work,
        score_n, score_f, slot_parts, first_slot, f, near, far, slots_a, slots_b,
    )
    shares = exchange(partial, LOT_GROUPS).astype(f32)
    return jnp.sum(shares.reshape(LOT_SHARE, own_rows, width), axis=0)


def solution(mesh):
    fine = Mesh(mesh.devices.reshape(tuple(SIZES.values())), ALL)
    placed = (P(ALL, None), P(("x", "z", "y", "core"), None), P(("y", "core")), P(("x", "z")))
    return jax.shard_map(local, mesh=fine, in_specs=placed, out_specs=P(ALL, None), check_vma=False)
```

time: 138 us -> 129 us (0.935)
  Pallas kernels: 24.5 us -> 18.5 us
  starting transfers between devices: 16.6 us -> 14.4 us
  blocking collectives: 80.8 us -> 79.3 us
    pallas_call x8 -> x9, Pallas kernels: 24.5 us -> 18.5 us  [call(): pl.pallas_call(kernel, out_shape=outs, in_specs=[near] * len(args), out_s...]
    ppermute x4 -> x7, starting transfers between devices: 8.18 us -> 3.7 us  [to_place(): lax.ppermute(values, ALL, [(group[i], group[i ^ d]) for group in LOT_GROU...]
    all_to_all x1, starting transfers between devices: 5.71 us -> 8.77 us  [exchange(): lax.all_to_all(values, ALL, 0, 0, tiled=True, axis_index_groups=members)]
    ppermute x4 -> x7, waiting for transfers between devices: 10.2 us -> 7.43 us  [to_place(): lax.ppermute(values, ALL, [(group[i], group[i ^ d]) for group in LOT_GROU...]
    ppermute x1, waiting for transfers between devices: 0.01 us -> 2.2 us  [local(): slots_b = lax.ppermute(slots_a, 'core', [(0, 1), (1, 0)])]
    all_to_all x7, blocking collectives: 80.8 us -> 79.3 us  [exchange(): lax.all_to_all(values, ALL, 0, 0, tiled=True, axis_index_groups=members)]
  transfers between devices with their start and end apart: 6 -> 9, of which waited for: 1 -> 7; matrix products, arithmetic and copies ran while one was open for 3% -> 0% of each run, Pallas kernels for 3% -> 2%
where the time goes in v3:
time: 129 us; the launch traced here: 128 us
  blocking collectives  79.3 us (61%)
  Pallas kernels  18.5 us (14%)
  starting transfers between devices  14.4 us (11%)
  waiting for transfers between devices  10.6 us (8%)
  local copies, waits for them, and re-layouts  4.25 us (3%)
    all_to_all x7, blocking collectives, exchange(): lax.all_to_all(values, ALL, 0, 0, tiled=True, axis_index_groups=members)  79.3 us
    pallas_call x9, Pallas kernels, call(): pl.pallas_call(kernel, out_shape=outs, in_specs=[near] * len(args), out_s...  18.5 us
    all_to_all x1, starting transfers between devices, exchange(): lax.all_to_all(values, ALL, 0, 0, tiled=True, axis_index_groups=members)  8.77 us
    ppermute x7, waiting for transfers between devices, to_place(): lax.ppermute(values, ALL, [(group[i], group[i ^ d]) for group in LOT_GROU...  7.43 us
    ppermute x7, starting transfers between devices, to_place(): lax.ppermute(values, ALL, [(group[i], group[i ^ d]) for group in LOT_GROU...  3.7 us
  transfers between devices with their start and end apart: 9, of which 7 were waited for; matrix products, arithmetic and copies ran while one was open for 0% of the time, Pallas kernels for 2%

profile of v3, /device:TPU:1, one launch (start us, length us, event | category | flops | bytes accessed | tf_op | source)
XLA Modules:
  0.0 128.0 jit_solution(3394597855091757598)
XLA Ops:
  0.0 2.0 %tile.2 = bf16[8,128,512]{2,1,0:T(8,128)(2,1)} broadcast(bf16[128,512]{1,0:T(8,128)(2,1)} %param.5), dimensions={1,2} | broadcast | bytes 1179648 | tf_op jit(solution)/shard_map/tile | solution.py:338
  2.0 8.8 %all-to-all-start = ((bf16[8,128,512]{2,1,0:T(8,128)(2,1)}), bf16[8,128,512]{2,1,0:T(8,128)(2,1)S(1)}, u32[]{:S(2)}, u32[]{:S(2)}) async-start(bf16[8,128,512]{2,1,0:T(8,128)(2,1)} %tile.2), calls=%async_computation | async-start | bytes 2097152 | tf_op jit(solution)/shard_map/all_to_all | solution.py:326
  10.7 2.7 %collective-permute-start.1 = (bf16[128,512]{1,0:T(8,128)(2,1)}, bf16[128,512]{1,0:T(8,128)(2,1)S(1)}, u32[]{:S(2)}, u32[]{:S(2)}) collective-permute-start(bf16[128,512]{1,0:T(8,128)(2,1)} %lots.1), channel_id=1, source_target_pairs={{0,8},{1,9},{4,12},{5,13},{8,0},{9,1},{12,4},{13,5},{16,24},{17,25... | collective-permute-start | bytes 393224 | tf_op jit(solution)/shard_map/ppermute | solution.py:330
  13.5 0.3 collective-permute-start
  13.8 0.6 collective-permute-start.2
  14.3 0.0 collective-permute-start.3
  14.4 2.2 %collective-permute-done.1.refs_2_ = bf16[128,512]{1,0:T(8,128)(2,1)S(1)} collective-permute-done((bf16[128,512]{1,0:T(8,128)(2,1)}, bf16[128,512]{1,0:T(8,128)(2,1)S(1)}, u32[]{:S(2)}, u32[]{:S(2)}) %collective-permute-start.1) | collective-permute-done | bytes 131104 | tf_op jit(solution)/shard_map/ppermute | solution.py:330
  16.6 0.0 collective-permute-start.5
  16.6 2.5 %collective-permute-done.refs_1_ = bf16[128,512]{1,0:T(8,128)(2,1)S(1)} collective-permute-done((bf16[128,512]{1,0:T(8,128)(2,1)}, bf16[128,512]{1,0:T(8,128)(2,1)S(1)}, u32[]{:S(2)}, u32[]{:S(2)}) %collective-permute-start) | collective-permute-done | bytes 131104 | tf_op jit(solution)/shard_map/ppermute | solution.py:330
  19.1 0.0 collective-permute-start.4
  19.1 0.0 copy-start
  19.1 0.9 copy-done
  20.0 0.0 copy-start.1
  20.0 0.7 copy-done.1
  20.7 0.0 copy-start.2
  20.7 0.7 copy-done.2
  21.4 0.1 shard_map.46
  21.5 0.0 collective-permute-done.2.refs_3_
  21.5 0.0 collective-permute-done.3.refs_0_
  21.5 0.3 collective-permute-done.5.refs_2_
  21.8 2.0 %collective-permute-done.4.refs_1_ = bf16[128,512]{1,0:T(8,128)(2,1)S(1)} collective-permute-done((bf16[128,512]{1,0:T(8,128)(2,1)S(1)}, bf16[128,512]{1,0:T(8,128)(2,1)S(1)}, u32[]{:S(2)}, u32[]{:S(2)}) %collective-permute-start.4) | collective-permute-done | bytes 131104 | tf_op jit(solution)/shard_map/ppermute | solution.py:330
  23.8 0.9 all-to-all-done
  24.7 2.0 %collective-permute-start.6 = (bf16[1024,512]{1,0:T(8,128)(2,1)S(1)}, bf16[1024,512]{1,0:T(8,128)(2,1)S(1)}, u32[]{:S(2)}, u32[]{:S(2)}) collective-permute-start(bf16[1024,512]{1,0:T(8,128)(2,1)S(1)} %bitcast.16), channel_id=1, source_target_pairs={{0,16},{16,0},{1,17},{17,1},{2,18},{18,2},{3,19},{19,3},{4,20},{20... | collective-permute-start | bytes 3145736 | tf_op jit(solution)/shard_map/ppermute | solution.py:358
  26.7 0.1 collective-permute-start.7
  26.8 2.2 %collective-permute-done.6.slots_b = bf16[1024,512]{1,0:T(8,128)(2,1)S(1)} collective-permute-done((bf16[1024,512]{1,0:T(8,128)(2,1)S(1)}, bf16[1024,512]{1,0:T(8,128)(2,1)S(1)}, u32[]{:S(2)}, u32[]{:S(2)}) %collective-permute-start.6) | collective-permute-done | bytes 1048608 | tf_op jit(solution)/shard_map/ppermute | solution.py:358
  29.0 2.4 %shard_map.47 = (f32[512,2048]{1,0:T(8,128)S(1)}, bf16[512,512]{1,0:T(8,128)(2,1)S(1)}, f32[128,128]{1,0:T(8,128)S(1)}, f32[16,128]{1,0:T(8,128)S(1)}) custom-call(bf16[1024,512]{1,0:T(8,128)(2,1)S(1)} %bitcast.17, bf16[1024,512]{1,0:T(8,128)(2,1)S(1)} %collective-permute-done.6.slots_b, f32[8,128]{1,0:T(8,128)S(1)} %get-tuple-element.33.lot_rows, ...), custom_call_target="tpu_custom_call" | custom-call | flops 4194304 | tf_op jit(solution)/shard_map/pallas_call | solution.py:314
  31.4 0.4 collective-permute-done.7.refs_3_
  31.8 2.3 %shard_map.48 = (f32[512,2048]{1,0:T(8,128)S(1)}, bf16[512,512]{1,0:T(8,128)(2,1)S(1)}, f32[128,128]{1,0:T(8,128)S(1)}) custom-call(bf16[1024,512]{1,0:T(8,128)(2,1)S(1)} %bitcast.18, bf16[1024,512]{1,0:T(8,128)(2,1)S(1)} %collective-permute-done.6.slots_b, f32[128,128]{1,0:T(8,128)S(1)} %get-tuple-element.39.wide_g, ...), custom_call_target="tpu_custom_call" | custom-call | flops 4194304 | tf_op jit(solution)/shard_map/pallas_call | solution.py:314
  34.2 8.9 %all_to_all.84 = f32[8,16,128]{2,1,0:T(8,128)S(1)} all-to-all(f32[8,16,128]{2,1,0:T(8,128)S(1)} %bitcast.38), channel_id=1, replica_groups={{0,1,4,5,8,9,12,13},{16,17,20,21,24,25,28,29},{2,3,6,7,10,11,14,15},{18..., dimensions={0} | all-to-all | bytes 131072 | tf_op jit(solution)/shard_map/all_to_all | solution.py:326
  43.1 2.3 %shard_map.49 = (f32[384,128]{1,0:T(8,128)S(1)}, f32[1024,128]{1,0:T(8,128)}) custom-call(f32[512,2048]{1,0:T(8,128)S(1)} %get-tuple-element.38.score_n, f32[512,2048]{1,0:T(8,128)S(1)} %get-tuple-element.44.score_f, f32[128,128]{1,0:T(8,128)S(1)} %bitcast.25, f32[128,128]{1,0:T(8,128)S(1)} %bitcast.26, f32[8,128]{1,0:T(8,128)S(1)} %get-tuple-element.46.slot_rows), custom_call_target="tpu_custom_call" | custom-call | flops 8388608 | tf_op jit(solution)/shard_map/pallas_call | solution.py:314
  45.4 14.3 %all_to_all.85 = f32[16,24,128]{2,1,0:T(8,128)S(1)} all-to-all(f32[16,24,128]{2,1,0:T(8,128)S(1)} %bitcast.31), channel_id=1, replica_groups={{1,2,33,34,65,66,97,98,17,18,49,50,81,82,113,114},{3,0,35,32,67,64,99,9..., dimensions={0} | all-to-all | bytes 393216 | tf_op jit(solution)/shard_map/all_to_all | solution.py:326
  59.7 2.0 %shard_map.50 = f32[64,128]{1,0:T(8,128)S(1)} custom-call(f32[512,2048]{1,0:T(8,128)S(1)} %get-tuple-element.38.score_n, f32[512,2048]{1,0:T(8,128)S(1)} %get-tuple-element.44.score_f, f32[384,128]{1,0:T(8,128)S(1)} %bitcast.20, f32[384,128]{1,0:T(8,128)S(1)} %bitcast.21), custom_call_target="tpu_custom_call" | custom-call | flops 8388608 | tf_op jit(solution)/shard_map/pallas_call | solution.py:314
  61.7 7.4 %all_to_all.86 = f32[8,8,128]{2,1,0:T(8,128)S(1)} all-to-all(f32[8,8,128]{2,1,0:T(8,128)S(1)} %bitcast.35), channel_id=1, replica_groups={{0,1,4,5,8,9,12,13},{16,17,20,21,24,25,28,29},{2,3,6,7,10,11,14,15},{18..., dimensions={0} | all-to-all | bytes 65536 | tf_op jit(solution)/shard_map/all_to_all | solution.py:326
  69.1 2.3 %shard_map.51 = (f32[256,128]{1,0:T(8,128)S(1)}, f32[1024,128]{1,0:T(8,128)}) custom-call(f32[512,2048]{1,0:T(8,128)S(1)} %get-tuple-element.38.score_n, f32[512,2048]{1,0:T(8,128)S(1)} %get-tuple-element.44.score_f, f32[64,128]{1,0:T(8,128)S(1)} %bitcast.33, f32[128,128]{1,0:T(8,128)S(1)} %bitcast.27, f32[8,128]{1,0:T(8,128)S(1)} %get-tuple-element.46.slot_rows), custom_call_target="tpu_custom_call" | custom-call | flops 8388608 | tf_op jit(solution)/shard_map/pallas_call | solution.py:314
  71.4 12.0 %all_to_all.87 = f32[16,16,128]{2,1,0:T(8,128)S(1)} all-to-all(f32[16,16,128]{2,1,0:T(8,128)S(1)} %bitcast.37), channel_id=1, replica_groups={{1,2,33,34,65,66,97,98,17,18,49,50,81,82,113,114},{3,0,35,32,67,64,99,9..., dimensions={0} | all-to-all | bytes 262144 | tf_op jit(solution)/shard_map/all_to_all | solution.py:326
  83.4 2.0 %shard_map.52 = f32[64,128]{1,0:T(8,128)S(1)} custom-call(f32[512,2048]{1,0:T(8,128)S(1)} %get-tuple-element.38.score_n, f32[512,2048]{1,0:T(8,128)S(1)} %get-tuple-element.44.score_f, f32[256,128]{1,0:T(8,128)S(1)} %bitcast.30, f32[384,128]{1,0:T(8,128)S(1)} %bitcast.22), custom_call_target="tpu_custom_call" | custom-call | flops 8388608 | tf_op jit(solution)/shard_map/pallas_call | solution.py:314
  85.4 8.0 %all_to_all.88 = f32[8,8,128]{2,1,0:T(8,128)S(1)} all-to-all(f32[8,8,128]{2,1,0:T(8,128)S(1)} %bitcast.34), channel_id=1, replica_groups={{0,1,4,5,8,9,12,13},{16,17,20,21,24,25,28,29},{2,3,6,7,10,11,14,15},{18..., dimensions={0} | all-to-all | bytes 65536 | tf_op jit(solution)/shard_map/all_to_all | solution.py:326
  93.4 1.9 %shard_map.53 = (f32[256,128]{1,0:T(8,128)S(1)}, f32[1024,128]{1,0:T(8,128)S(1)}) custom-call(f32[512,2048]{1,0:T(8,128)S(1)} %get-tuple-element.38.score_n, f32[512,2048]{1,0:T(8,128)S(1)} %get-tuple-element.44.score_f, f32[64,128]{1,0:T(8,128)S(1)} %bitcast.32, f32[128,128]{1,0:T(8,128)S(1)} %bitcast.28, f32[8,128]{1,0:T(8,128)S(1)} %get-tuple-element.46.slot_rows), custom_call_target="tpu_custom_call" | custom-call | flops 8388608 | tf_op jit(solution)/shard_map/pallas_call | solution.py:314
  95.4 12.0 %all_to_all.89 = f32[16,16,128]{2,1,0:T(8,128)S(1)} all-to-all(f32[16,16,128]{2,1,0:T(8,128)S(1)} %bitcast.36), channel_id=1, replica_groups={{1,2,33,34,65,66,97,98,17,18,49,50,81,82,113,114},{3,0,35,32,67,64,99,9..., dimensions={0} | all-to-all | bytes 262144 | tf_op jit(solution)/shard_map/all_to_all | solution.py:326
  107.4 3.0 %shard_map.54 = bf16[1024,512]{1,0:T(8,128)(2,1)S(1)} custom-call(f32[512,2048]{1,0:T(8,128)S(1)} %get-tuple-element.38.score_n, f32[512,2048]{1,0:T(8,128)S(1)} %get-tuple-element.44.score_f, f32[256,128]{1,0:T(8,128)S(1)} %bitcast.29, f32[384,128]{1,0:T(8,128)S(1)} %bitcast.23, f32[1024,128]{1,0:T(8,128)S(1)} %get-tuple-element.50.wide_f, ...), custom_call_target="tpu_custom_call" | custom-call | flops 8388608 | tf_op jit(solution)/shard_map/pallas_call | solution.py:314
  110.4 16.7 %all_to_all.90 = bf16[8,128,512]{2,1,0:T(8,128)(2,1)S(1)} all-to-all(bf16[8,128,512]{2,1,0:T(8,128)(2,1)S(1)} %bitcast.24), channel_id=1, replica_groups={{0,1,4,5,8,9,12,13},{16,17,20,21,24,25,28,29},{2,3,6,7,10,11,14,15},{18..., dimensions={0} | all-to-all | bytes 2097152 | tf_op jit(solution)/shard_map/all_to_all | solution.py:326
  127.1 0.8 convert_reduce_fusion
Async XLA Ops:
  2.0 22.8 %all-to-all-start = ((bf16[8,128,512]{2,1,0:T(8,128)(2,1)}), bf16[8,128,512]{2,1,0:T(8,128)(2,1)S(1)}, u32[]{:S(2)}, u32[]{:S(2)}) async-start(bf16[8,128,512]{2,1,0:T(8,128)(2,1)} %tile.2), calls=%async_computation | async-start | bytes 2097152 | tf_op jit(solution)/shard_map/all_to_all | solution.py:326
  10.7 5.8 %collective-permute-start.1 = (bf16[128,512]{1,0:T(8,128)(2,1)}, bf16[128,512]{1,0:T(8,128)(2,1)S(1)}, u32[]{:S(2)}, u32[]{:S(2)}) collective-permute-start(bf16[128,512]{1,0:T(8,128)(2,1)} %lots.1), channel_id=1, source_target_pairs={{0,8},{1,9},{4,12},{5,13},{8,0},{9,1},{12,4},{13,5},{16,24},{17,25... | collective-permute-start | bytes 393224 | tf_op jit(solution)/shard_map/ppermute | solution.py:330
  13.5 5.6 %collective-permute-start = (bf16[128,512]{1,0:T(8,128)(2,1)}, bf16[128,512]{1,0:T(8,128)(2,1)S(1)}, u32[]{:S(2)}, u32[]{:S(2)}) collective-permute-start(bf16[128,512]{1,0:T(8,128)(2,1)} %lots.1), channel_id=1, source_target_pairs={{0,4},{1,5},{4,0},{5,1},{8,12},{9,13},{12,8},{13,9},{16,20},{17,21... | collective-permute-start | bytes 393224 | tf_op jit(solution)/shard_map/ppermute | solution.py:330
  13.8 7.7 %collective-permute-start.2 = (bf16[128,512]{1,0:T(8,128)(2,1)}, bf16[128,512]{1,0:T(8,128)(2,1)S(1)}, u32[]{:S(2)}, u32[]{:S(2)}) collective-permute-start(bf16[128,512]{1,0:T(8,128)(2,1)} %lots.1), channel_id=1, source_target_pairs={{0,12},{1,13},{4,8},{5,9},{8,4},{9,5},{12,0},{13,1},{16,28},{17,29... | collective-permute-start | bytes 393224 | tf_op jit(solution)/shard_map/ppermute | solution.py:330
  14.3 7.2 %collective-permute-start.3 = (bf16[128,512]{1,0:T(8,128)(2,1)}, bf16[128,512]{1,0:T(8,128)(2,1)S(1)}, u32[]{:S(2)}, u32[]{:S(2)}) collective-permute-start(bf16[128,512]{1,0:T(8,128)(2,1)} %lots.1), channel_id=1, source_target_pairs={{0,1},{1,0},{4,5},{5,4},{8,9},{9,8},{12,13},{13,12},{16,17},{17,16... | collective-permute-start | bytes 393224 | tf_op jit(solution)/shard_map/ppermute | solution.py:330
  16.6 5.3 %collective-permute-start.5 = (bf16[128,512]{1,0:T(8,128)(2,1)S(1)}, bf16[128,512]{1,0:T(8,128)(2,1)S(1)}, u32[]{:S(2)}, u32[]{:S(2)}) collective-permute-start(bf16[128,512]{1,0:T(8,128)(2,1)S(1)} %collective-permute-done.1.refs_2_), channel_id=1, source_target_pairs={{0,1},{1,0},{4,5},{5,4},{8,9},{9,8},{12,13},{13,12},{16,17},{17,16... | collective-permute-start | bytes 393224 | tf_op jit(solution)/shard_map/ppermute | solution.py:330
  19.1 4.7 %collective-permute-start.4 = (bf16[128,512]{1,0:T(8,128)(2,1)S(1)}, bf16[128,512]{1,0:T(8,128)(2,1)S(1)}, u32[]{:S(2)}, u32[]{:S(2)}) collective-permute-start(bf16[128,512]{1,0:T(8,128)(2,1)S(1)} %collective-permute-done.refs_1_), channel_id=1, source_target_pairs={{0,1},{1,0},{4,5},{5,4},{8,9},{9,8},{12,13},{13,12},{16,17},{17,16... | collective-permute-start | bytes 393224 | tf_op jit(solution)/shard_map/ppermute | solution.py:330
  19.1 0.9 copy-start
  20.0 0.7 copy-start.1
  20.7 0.7 copy-start.2
  24.7 4.2 %collective-permute-start.6 = (bf16[1024,512]{1,0:T(8,128)(2,1)S(1)}, bf16[1024,512]{1,0:T(8,128)(2,1)S(1)}, u32[]{:S(2)}, u32[]{:S(2)}) collective-permute-start(bf16[1024,512]{1,0:T(8,128)(2,1)S(1)} %bitcast.16), channel_id=1, source_target_pairs={{0,16},{16,0},{1,17},{17,1},{2,18},{18,2},{3,19},{19,3},{4,20},{20... | collective-permute-start | bytes 3145736 | tf_op jit(solution)/shard_map/ppermute | solution.py:358
  26.7 5.1 %collective-permute-start.7 = (bf16[128,512]{1,0:T(8,128)(2,1)S(1)}, bf16[128,512]{1,0:T(8,128)(2,1)S(1)}, u32[]{:S(2)}, u32[]{:S(2)}) collective-permute-start(bf16[128,512]{1,0:T(8,128)(2,1)S(1)} %collective-permute-done.2.refs_3_), channel_id=1, source_target_pairs={{0,1},{1,0},{4,5},{5,4},{8,9},{9,8},{12,13},{13,12},{16,17},{17,16... | collective-permute-start | bytes 393224 | tf_op jit(solution)/shard_map/ppermute | solution.py:330

commit v4 on v3

--- a/solution.py
+++ b/solution.py
@@ -31,6 +31,7 @@
 CORE_SLOT_GROUPS = groups(FULL, [(0,), (1,)], EACH, ACROSS)
 LOT_SHARE, SLOT_SHARE = 8, 16
 CHUNKS = 2
+ORDER = (1, 5, 3, 7, 4, 2, 6)
 
 
 def place_in_lots():
@@ -115,16 +116,16 @@
     return jnp.concatenate(out, axis=0)
 
 
-def column_pass(scores, wide_f, sums):
+def column_pass(scores, wides, sums):
     rows, tiles_of = 64, 8
     below = scores[0].shape[0]
 
     def step(i, carry):
         cols = [pl.ds(pl.multiple_of((i * tiles_of + k) * LANES, LANES), LANES) for k in range(tiles_of)]
         states = [None] * tiles_of
-        for start in range(0, wide_f.shape[0], rows):
-            score, at = scores[start // below], start % below
-            fs = [wide_f[start + k : start + k + 8, :] for k in range(0, rows, 8)]
+        for start in range(0, below * len(scores), rows):
+            score, wide_f, at = scores[start // below], wides[start // below], start % below
+            fs = [wide_f[at + k : at + k + 8, :] for k in range(0, rows, 8)]
             for k, col in enumerate(cols):
                 terms = [score[at + 8 * n : at + 8 * n + 8, col] + f for n, f in enumerate(fs)]
                 states[k] = onward(states[k], terms)
@@ -178,12 +179,21 @@
         lots[n * rows : (n + 1) * rows, :] = part[...]
 
 
-def own_kernel(lots, lot_mass, slot_mass, own_lots, lot_rows, slot_rows):
+def own_kernel(lots, lot_mass, slot_mass, own_lots, lot_rows, near_logs):
     own_lots[...] = lots[...]
     masses = lot_mass[pl.ds(lax.axis_index("x") * SIZES["z"] + lax.axis_index("z"), 1), :]
     lot_rows[...] = padded([jnp.log(masses) * LOG2E, square_row(lots[...])])
-    masses = slot_mass[pl.ds(lax.axis_index("y") * SIZES["core"] + lax.axis_index("core"), 1), :]
-    slot_rows[...] = padded([jnp.log(masses) * LOG2E])
+    near_logs[...] = jnp.log(slot_mass[...]) * LOG2E
+
+
+def all_slot_logs(near_logs, across_logs):
+    core, place = lax.axis_index("core"), (lax.axis_index("z") + 1) % 2
+    rows = []
+    for at in (core, 1 - core):
+        for y in range(SIZES["y"]):
+            row = pl.ds(y * SIZES["core"] + at, 1)
+            rows += [jnp.where(place == z, near_logs[row, :], across_logs[row, :]) for z in range(2)]
+    return jnp.concatenate(rows, axis=0)
 
 
 def near_score_kernel(slots_a, slots_b, lot_rows, *refs):
@@ -198,9 +208,10 @@
     placed[LOT_SHARE:, :] = lot_rows[...]
 
 
-def far_score_kernel(slots_a, slots_b, wide_g, placed_before, *refs):
-    parts, (score, far, out, placed, peak, total) = refs[: LOT_SHARE // 2], refs[LOT_SHARE // 2 :]
+def far_score_kernel(slots_a, slots_b, near_logs, across_logs, wide_g, placed_before, *refs):
+    parts, (score, far, slot_logs, out, placed, peak, total) = refs[: LOT_SHARE // 2], refs[LOT_SHARE // 2 :]
     gather_rows(parts, far)
+    slot_logs[...] = all_slot_logs(near_logs, across_logs)
     half = slots_a.shape[0]
     fill_scores(far, slots_a, score, 0)
     fill_scores(far, slots_b, score, half)
@@ -227,69 +238,59 @@
     return pot - squares
 
 
-def own_core_first(rows):
-    half = rows.shape[0] // 2
-    low, high = rows[:half, :], rows[half:, :]
-    ahead = lax.axis_index("core") == 0
-    return jnp.concatenate([jnp.where(ahead, low, high), jnp.where(ahead, high, low)], axis=0)
-
-
-def slot_update(parts, first, blocks):
-    logs = own_core_first(jnp.concatenate(row_of_each(first, SLOT_SHARE, blocks), axis=0))
-    return logs - log_sum_of(parts, SLOT_SHARE, blocks)
-
-
-def column_kernel(score_n, score_f, parts, first, slot_rows, out, wide_f, placed, sums):
+def slot_update(parts, slot_logs):
+    return slot_logs[...] - log_sum_of(parts, SLOT_SHARE, slot_logs.shape[0])
+
+
+def column_kernel(score_n, score_f, parts, first, out, wide_n, wide_far, placed, sums):
     placed[...] = lot_update(parts, first, LOT_SHARE)
     me = place_in_lots()
     for b, step in enumerate(STEPS):
         row = placed[pl.ds(me ^ step, 1), :]
-        wide_f[b * LANES : (b + 1) * LANES, :] = jnp.broadcast_to(row, (LANES, LANES)).T
-    column_pass([score_n, score_f], wide_f, sums)
+        wide, at = (wide_n, b) if b < LOT_SHARE // 2 else (wide_far, b - LOT_SHARE // 2)
+        wide[at * LANES : (at + 1) * LANES, :] = jnp.broadcast_to(row, (LANES, LANES)).T
+    column_pass([score_n, score_f], [wide_n, wide_far], sums)
     half = sums.shape[0] // 2
     mine, other = sums[:half, :], sums[half:, :]
     ahead = lax.axis_index("core") == 0
-    extra = [slot_rows[...]] if out.shape[0] // SLOT_SHARE > sums.shape[0] else []
-    same = jnp.concatenate([mine, other, *extra], axis=0)
-    turned = jnp.concatenate([other, mine, *extra], axis=0)
+    same, turned = sums[...], jnp.concatenate([other, mine], axis=0)
     rows = same.shape[0]
     for n in range(SLOT_SHARE):
         low = n < SLOT_SHARE // 2
         out[n * rows : (n + 1) * rows, :] = jnp.where(ahead, same if low else turned, turned if low else same)
 
 
-def row_kernel(score_n, score_f, parts, first, out, wide_g, placed, peak, total):
-    spread_rows(slot_update(parts, first, score_n.shape[1] // LANES), wide_g)
+def row_kernel(score_n, score_f, parts, slot_logs, out, wide_g, placed, peak, total):
+    spread_rows(slot_update(parts, slot_logs), wide_g)
     row_pass(score_n, wide_g, peak, total, 0)
     row_pass(score_f, wide_g, peak, total, score_n.shape[0])
     to_places(row_result(peak, total), placed, range(LOT_SHARE))
     send_to_lots(placed[...], out)
 
 
-def final_kernel(score_n, score_f, parts, first, wide_f, near, far, slots_a, slots_b, out, wide_g, *work):
-    tiles = score_n.shape[1] // LANES
-    spread_rows(slot_update(parts, first, tiles), wide_g)
-    half, below, rows_of = slots_a.shape[0], score_n.shape[0], work[0].shape[0]
+def final_kernel(score, parts, slot_logs, wide_f, lots, slots_a, slots_b, *refs):
+    blocks = score.shape[0] // LANES
+    outs, wide_g, work = refs[:blocks], refs[blocks], refs[blocks + 1 :]
+    tiles = score.shape[1] // LANES
+    spread_rows(slot_update(parts, slot_logs), wide_g)
+    half, rows_of = slots_a.shape[0], work[0].shape[0]
     plans, row_sums = work[: len(work) // 2], work[len(work) // 2 :]
-    me = place_in_lots()
 
     def fill_plan(c):
-        score, base = (score_n, 0) if c * rows_of < below else (score_f, below)
         for start in range(0, rows_of, 16):
-            at = c * rows_of + start
-            shift = wide_f[at : at + 16, :]
+            rows = slice(c * rows_of + start, c * rows_of + start + 16)
+            shift = wide_f[rows, :]
             wholes = []
             for t in range(tiles):
                 cols = slice(t * LANES, (t + 1) * LANES)
                 both = jnp.concatenate([wide_g[t * 8 : (t + 1) * 8, :]] * 2, axis=0)
-                term = jnp.exp2(score[at - base : at - base + 16, cols] + (shift + both))
+                term = jnp.exp2(score[rows, cols] + (shift + both))
                 plans[c][start : start + 16, cols] = term.astype(jnp.bfloat16)
                 wholes.append(term)
             whole = jnp.sum(in_pairs(jnp.add, wholes), axis=1, keepdims=True)
             row_sums[c][start : start + 16, :] = jnp.broadcast_to(whole, (16, LANES))
 
     def finish(c):
-        lots, base = (near, 0) if c * rows_of < below else (far, below)
         at = c * rows_of
         step_cols = 256
         for start in range(0, lots.shape[1], step_cols):
@@ -297,10 +298,10 @@
             moved = jnp.dot(plans[c][:, :half], slots_a[:, cols], preferred_element_type=jnp.float32)
             moved = moved + jnp.dot(plans[c][:, half:], slots_b[:, cols], preferred_element_type=jnp.float32)
             sums = jnp.concatenate([row_sums[c][...]] * (step_cols // LANES), axis=1)
-            grad = sums * lots[at - base : at - base + rows_of, cols].astype(jnp.float32) - moved
+            grad = sums * lots[at : at + rows_of, cols].astype(jnp.float32) - moved
             for n in range(rows_of // LANES):
-                to = pl.ds(pl.multiple_of((me ^ STEPS[at // LANES + n]) * LANES, LANES), LANES)
-                out[to, cols] = grad[n * LANES : (n + 1) * LANES, :].astype(out.dtype)
+                out = outs[at // LANES + n]
+                out[:, cols] = grad[n * LANES : (n + 1) * LANES, :].astype(out.dtype)
 
     fill_plan(0)
     for c in range(len(plans)):
@@ -345,17 +346,18 @@
     def shape(*dims, dtype=f32):
         return jax.ShapeDtypeStruct(dims, dtype)
 
-    own_lots, lot_rows, slot_rows = call(
+    own_lots, lot_rows, near_logs = call(
         own_kernel,
-        [shape(own_rows, width, dtype=lot_features.dtype), shape(8, LANES), shape(8, LANES)],
+        [shape(own_rows, width, dtype=lot_features.dtype), shape(8, LANES), shape(slot_blocks // 2, LANES)],
         [],
         own_rows * width,
         lot_features, lot_mass, slot_mass,
     )
-    slots_a, near[1], near[2], near[3], far[0], far[1], far[2], own_lots, lot_rows, slot_rows = lax.optimization_barrier(
-        (slots_a, *near[1:], *far[:3], own_lots, lot_rows, slot_rows)
+    slots_a, near[1], near[2], near[3], far[0], far[1], far[2], own_lots, lot_rows, near_logs = lax.optimization_barrier(
+        (slots_a, *near[1:], *far[:3], own_lots, lot_rows, near_logs)
     )
     slots_b = lax.ppermute(slots_a, "core", [(0, 1), (1, 0)])
+    across_logs = lax.ppermute(near_logs, "z", [(a, b) for pair in ACROSS for a, b in (pair, pair[::-1])])
 
     wide_g, placed, wide_f, half_f = ((slot_blocks * 8, LANES), (LOT_SHARE, LANES), (n, LANES), (n // 2, LANES))
     work = n * m * 4
@@ -368,45 +370,47 @@
         work // 2,
         slots_a, slots_b, lot_rows, own_lots, *near[1:],
     )
-    score_f, far, out = call(
+    score_f, far, slot_logs, out = call(
         far_score_kernel,
-        [shape(n // 2, m), half_lots, shape(LOT_SHARE * (LOT_SHARE + 8), LANES)],
+        [shape(n // 2, m), half_lots, shape(slot_blocks, LANES), shape(LOT_SHARE * (LOT_SHARE + 8), LANES)],
         [((LOT_SHARE + 8, LANES), f32), (half_f, f32), (half_f, f32)],
         work // 2,
-        slots_a, slots_b, g, placed_n, *far,
+        slots_a, slots_b, near_logs, across_logs, g, placed_n, *far,
     )
     first_lot = lot_parts = exchange(out, LOT_GROUPS)
-    first_slot = None
     for step in range(ITERS):
-        extra = 8 if step == 0 else 0
-        out, f = call(
+        last = step == ITERS - 1
+        halves = [half_f, half_f]
+        out, *f_halves = call(
             column_kernel,
-            [shape(SLOT_SHARE * (slot_blocks + extra), LANES), shape(*wide_f)],
-            [(placed, f32), ((slot_blocks, LANES), f32)],
+            [shape(SLOT_SHARE * slot_blocks, LANES)] + [shape(*dims) for dims in halves if last],
+            [(dims, f32) for dims in halves if not last] + [(placed, f32), ((slot_blocks, LANES), f32)],
             work,
-            score_n, score_f, lot_parts, first_lot, slot_rows,
+            score_n, score_f, lot_parts, first_lot,
         )
         slot_parts = exchange(out, SLOT_GROUPS)
-        if step == 0:
-            first_slot = slot_parts
-        if step < ITERS - 1:
+        if not last:
             (out,) = call(
                 row_kernel,
                 [shape(LOT_SHARE * LOT_SHARE, LANES)],
                 [(wide_g, f32), (placed, f32), (wide_f, f32), (wide_f, f32)],
                 work,
-                score_n, score_f, slot_parts, first_slot,
+                score_n, score_f, slot_parts, slot_logs,
             )
             lot_parts = exchange(out, LOT_GROUPS)
-    (partial,) = call(
-        final_kernel,
-        [shape(n, width, dtype=jnp.bfloat16)],
-        [(wide_g, f32)] + [((n // CHUNKS, m), jnp.bfloat16)] * CHUNKS + [((n // CHUNKS, LANES), f32)] * CHUNKS,
-        work,
-        score_n, score_f, slot_parts, first_slot, f, near, far, slots_a, slots_b,
-    )
-    shares = exchange(partial, LOT_GROUPS).astype(f32)
-    return jnp.sum(shares.reshape(LOT_SHARE, own_rows, width), axis=0)
+    parts = {}
+    for score, lots, at in ((score_f, far, LOT_SHARE // 2), (score_n, near, 0)):
+        steps = STEPS[at : at + LOT_SHARE // 2]
+        outs = call(
+            final_kernel,
+            [shape(own_rows, width, dtype=jnp.bfloat16 if d else f32) for d in steps],
+            [(wide_g, f32)] + [((n // 2 // CHUNKS, m), jnp.bfloat16)] * CHUNKS + [((n // 2 // CHUNKS, LANES), f32)] * CHUNKS,
+            work // 2,
+            score, slot_parts, slot_logs, f_halves[at // (LOT_SHARE // 2)], lots, slots_a, slots_b,
+        )
+        parts.update(zip(steps, outs, strict=True))
+    arrived = [to_place(parts[d], d) for d in ORDER]
+    return parts[0] + sum(part.astype(f32) for part in arrived)
 
 
 def solution(mesh):

time: 129 us -> 127 us (0.984)
  blocking collectives: 79.3 us -> 61.9 us
  starting transfers between devices: 14.4 us -> 24.4 us
  waiting for transfers between devices: 10.6 us -> 16.1 us
    all_to_all x7 -> x6, blocking collectives: 79.3 us -> 61.9 us  [exchange(): lax.all_to_all(values, ALL, 0, 0, tiled=True, axis_index_groups=members)]
    ppermute x7 -> x14, starting transfers between devices: 3.7 us -> 12.4 us  [to_place(): lax.ppermute(values, ALL, [(group[i], group[i ^ d]) for group in LOT_GROU...]
    ppermute x7 -> x14, waiting for transfers between devices: 7.43 us -> 14.2 us  [to_place(): lax.ppermute(values, ALL, [(group[i], group[i ^ d]) for group in LOT_GROU...]
    pallas_call x9 -> x10, Pallas kernels: 18.5 us -> 17.7 us  [call(): pl.pallas_call(kernel, out_shape=outs, in_specs=[near] * len(args), out_s...]
  transfers between devices with their start and end apart: 9 -> 17, of which waited for: 7 -> 11; matrix products, arithmetic and copies ran while one was open for 0% -> 0% of each run, Pallas kernels for 2% -> 3%
where the time goes in v4:
time: 127 us; the launch traced here: 125 us
  blocking collectives  61.9 us (49%)
  starting transfers between devices  24.4 us (19%)
  Pallas kernels  17.7 us (14%)
  waiting for transfers between devices  16.1 us (13%)
  local copies, waits for them, and re-layouts  4.3 us (3%)
    all_to_all x6, blocking collectives, exchange(): lax.all_to_all(values, ALL, 0, 0, tiled=True, axis_index_groups=members)  61.9 us
    pallas_call x10, Pallas kernels, call(): pl.pallas_call(kernel, out_shape=outs, in_specs=[near] * len(args), out_s...  17.7 us
    ppermute x14, waiting for transfers between devices, to_place(): lax.ppermute(values, ALL, [(group[i], group[i ^ d]) for group in LOT_GROU...  14.2 us
    ppermute x14, starting transfers between devices, to_place(): lax.ppermute(values, ALL, [(group[i], group[i ^ d]) for group in LOT_GROU...  12.4 us
    all_to_all x1, starting transfers between devices, exchange(): lax.all_to_all(values, ALL, 0, 0, tiled=True, axis_index_groups=members)  8.77 us
  transfers between devices with their start and end apart: 17, of which 11 were waited for; matrix products, arithmetic and copies ran while one was open for 0% of the time, Pallas kernels for 3%

profile of v4, /device:TPU:1, one launch (start us, length us, event | category | flops | bytes accessed | tf_op | source)
XLA Modules:
  0.0 125.4 jit_solution(3349978885298289515)
XLA Ops:
  0.0 2.0 %tile.2 = bf16[8,128,512]{2,1,0:T(8,128)(2,1)} broadcast(bf16[128,512]{1,0:T(8,128)(2,1)} %param.5), dimensions={1,2} | broadcast | bytes 1179648 | tf_op jit(solution)/shard_map/tile | solution.py:339
  2.0 8.8 %all-to-all-start = ((bf16[8,128,512]{2,1,0:T(8,128)(2,1)}), bf16[8,128,512]{2,1,0:T(8,128)(2,1)S(1)}, u32[]{:S(2)}, u32[]{:S(2)}) async-start(bf16[8,128,512]{2,1,0:T(8,128)(2,1)} %tile.2), calls=%async_computation | async-start | bytes 2097152 | tf_op jit(solution)/shard_map/all_to_all | solution.py:327
  10.8 2.7 %collective-permute-start.1 = (bf16[128,512]{1,0:T(8,128)(2,1)}, bf16[128,512]{1,0:T(8,128)(2,1)S(1)}, u32[]{:S(2)}, u32[]{:S(2)}) collective-permute-start(bf16[128,512]{1,0:T(8,128)(2,1)} %lots.1), channel_id=1, source_target_pairs={{0,8},{1,9},{4,12},{5,13},{8,0},{9,1},{12,4},{13,5},{16,24},{17,25... | collective-permute-start | bytes 393224 | tf_op jit(solution)/shard_map/ppermute | solution.py:331
  13.5 0.3 collective-permute-start
  13.8 0.6 collective-permute-start.2
  14.4 0.0 collective-permute-start.3
  14.4 2.2 %collective-permute-done.1.refs_2_ = bf16[128,512]{1,0:T(8,128)(2,1)S(1)} collective-permute-done((bf16[128,512]{1,0:T(8,128)(2,1)}, bf16[128,512]{1,0:T(8,128)(2,1)S(1)}, u32[]{:S(2)}, u32[]{:S(2)}) %collective-permute-start.1) | collective-permute-done | bytes 131104 | tf_op jit(solution)/shard_map/ppermute | solution.py:331
  16.6 2.5 %collective-permute-done.refs_1_ = bf16[128,512]{1,0:T(8,128)(2,1)S(1)} collective-permute-done((bf16[128,512]{1,0:T(8,128)(2,1)}, bf16[128,512]{1,0:T(8,128)(2,1)S(1)}, u32[]{:S(2)}, u32[]{:S(2)}) %collective-permute-start) | collective-permute-done | bytes 131104 | tf_op jit(solution)/shard_map/ppermute | solution.py:331
  19.1 0.0 collective-permute-start.4
  19.1 0.9 copy-done
  20.1 0.7 copy-done.1
  20.8 0.7 copy-done.2
  21.4 0.1 shard_map.46
  21.6 0.3 collective-permute-done.5.refs_2_
  21.9 2.0 %collective-permute-done.4.refs_1_ = bf16[128,512]{1,0:T(8,128)(2,1)S(1)} collective-permute-done((bf16[128,512]{1,0:T(8,128)(2,1)S(1)}, bf16[128,512]{1,0:T(8,128)(2,1)S(1)}, u32[]{:S(2)}, u32[]{:S(2)}) %collective-permute-start.4) | collective-permute-done | bytes 131104 | tf_op jit(solution)/shard_map/ppermute | solution.py:331
  23.9 0.9 all-to-all-done
  24.8 2.0 %collective-permute-start.6 = (bf16[1024,512]{1,0:T(8,128)(2,1)S(1)}, bf16[1024,512]{1,0:T(8,128)(2,1)S(1)}, u32[]{:S(2)}, u32[]{:S(2)}) collective-permute-start(bf16[1024,512]{1,0:T(8,128)(2,1)S(1)} %bitcast.15), channel_id=1, source_target_pairs={{0,16},{16,0},{1,17},{17,1},{2,18},{18,2},{3,19},{19,3},{4,20},{20... | collective-permute-start | bytes 3145736 | tf_op jit(solution)/shard_map/ppermute | solution.py:359
  26.7 0.1 collective-permute-start.8
  26.8 1.2 collective-permute-start.7
  28.0 1.0 collective-permute-done.6.slots_b
  29.0 2.4 %shard_map.47 = (f32[512,2048]{1,0:T(8,128)S(1)}, bf16[512,512]{1,0:T(8,128)(2,1)S(1)}, f32[128,128]{1,0:T(8,128)S(1)}, f32[16,128]{1,0:T(8,128)S(1)}) custom-call(bf16[1024,512]{1,0:T(8,128)(2,1)S(1)} %bitcast.16, bf16[1024,512]{1,0:T(8,128)(2,1)S(1)} %collective-permute-done.6.slots_b, f32[8,128]{1,0:T(8,128)S(1)} %get-tuple-element.41.lot_rows, ...), custom_call_target="tpu_custom_call" | custom-call | flops 4194304 | tf_op jit(solution)/shard_map/pallas_call | solution.py:315
  31.5 0.4 collective-permute-done.8.refs_3_
  31.9 2.4 %shard_map.48 = (f32[512,2048]{1,0:T(8,128)S(1)}, bf16[512,512]{1,0:T(8,128)(2,1)S(1)}, f32[16,128]{1,0:T(8,128)S(1)}, f32[128,128]{1,0:T(8,128)S(1)}) custom-call(bf16[1024,512]{1,0:T(8,128)(2,1)S(1)} %bitcast.17, bf16[1024,512]{1,0:T(8,128)(2,1)S(1)} %collective-permute-done.6.slots_b, f32[8,128]{1,0:T(8,128)S(1)} %get-tuple-element.47.near_logs, ...), custom_call_target="tpu_custom_call" | custom-call | flops 4194304 | tf_op jit(solution)/shard_map/pallas_call | solution.py:315
  34.3 8.9 %all_to_all.75 = f32[8,16,128]{2,1,0:T(8,128)S(1)} all-to-all(f32[8,16,128]{2,1,0:T(8,128)S(1)} %bitcast.35), channel_id=1, replica_groups={{0,1,4,5,8,9,12,13},{16,17,20,21,24,25,28,29},{2,3,6,7,10,11,14,15},{18..., dimensions={0} | all-to-all | bytes 131072 | tf_op jit(solution)/shard_map/all_to_all | solution.py:327
  43.2 2.0 %shard_map.49 = f32[256,128]{1,0:T(8,128)S(1)} custom-call(f32[512,2048]{1,0:T(8,128)S(1)} %get-tuple-element.46.score_n.score, f32[512,2048]{1,0:T(8,128)S(1)} %get-tuple-element.53.score_f.score, f32[128,128]{1,0:T(8,128)S(1)} %bitcast.20, f32[128,128]{1,0:T(8,128)S(1)} %bitcast.21), custom_call_target="tpu_custom_call" | custom-call | flops 8388608 | tf_op jit(solution)/shard_map/pallas_call | solution.py:315
  45.1 13.6 %all_to_all.76 = f32[16,16,128]{2,1,0:T(8,128)S(1)} all-to-all(f32[16,16,128]{2,1,0:T(8,128)S(1)} %bitcast.29), channel_id=1, replica_groups={{1,2,33,34,65,66,97,98,17,18,49,50,81,82,113,114},{3,0,35,32,67,64,99,9..., dimensions={0} | all-to-all | bytes 262144 | tf_op jit(solution)/shard_map/all_to_all | solution.py:327
  58.8 2.0 %shard_map.50 = f32[64,128]{1,0:T(8,128)S(1)} custom-call(f32[512,2048]{1,0:T(8,128)S(1)} %get-tuple-element.46.score_n.score, f32[512,2048]{1,0:T(8,128)S(1)} %get-tuple-element.53.score_f.score, f32[256,128]{1,0:T(8,128)S(1)} %bitcast.26, f32[16,128]{1,0:T(8,128)S(1)} %get-tuple-element.55.slot_logs), custom_call_target="tpu_custom_call" | custom-call | flops 8388608 | tf_op jit(solution)/shard_map/pallas_call | solution.py:315
  60.8 7.4 %all_to_all.77 = f32[8,8,128]{2,1,0:T(8,128)S(1)} all-to-all(f32[8,8,128]{2,1,0:T(8,128)S(1)} %bitcast.31), channel_id=1, replica_groups={{0,1,4,5,8,9,12,13},{16,17,20,21,24,25,28,29},{2,3,6,7,10,11,14,15},{18..., dimensions={0} | all-to-all | bytes 65536 | tf_op jit(solution)/shard_map/all_to_all | solution.py:327
  68.3 2.0 %shard_map.51 = f32[256,128]{1,0:T(8,128)S(1)} custom-call(f32[512,2048]{1,0:T(8,128)S(1)} %get-tuple-element.46.score_n.score, f32[512,2048]{1,0:T(8,128)S(1)} %get-tuple-element.53.score_f.score, f32[64,128]{1,0:T(8,128)S(1)} %bitcast.32, f32[128,128]{1,0:T(8,128)S(1)} %bitcast.22), custom_call_target="tpu_custom_call" | custom-call | flops 8388608 | tf_op jit(solution)/shard_map/pallas_call | solution.py:315
  70.2 12.0 %all_to_all.78 = f32[16,16,128]{2,1,0:T(8,128)S(1)} all-to-all(f32[16,16,128]{2,1,0:T(8,128)S(1)} %bitcast.27), channel_id=1, replica_groups={{1,2,33,34,65,66,97,98,17,18,49,50,81,82,113,114},{3,0,35,32,67,64,99,9..., dimensions={0} | all-to-all | bytes 262144 | tf_op jit(solution)/shard_map/all_to_all | solution.py:327
  82.2 2.0 %shard_map.52 = f32[64,128]{1,0:T(8,128)S(1)} custom-call(f32[512,2048]{1,0:T(8,128)S(1)} %get-tuple-element.46.score_n.score, f32[512,2048]{1,0:T(8,128)S(1)} %get-tuple-element.53.score_f.score, f32[256,128]{1,0:T(8,128)S(1)} %bitcast.28, f32[16,128]{1,0:T(8,128)S(1)} %get-tuple-element.55.slot_logs), custom_call_target="tpu_custom_call" | custom-call | flops 8388608 | tf_op jit(solution)/shard_map/pallas_call | solution.py:315
  84.2 8.0 %all_to_all.79 = f32[8,8,128]{2,1,0:T(8,128)S(1)} all-to-all(f32[8,8,128]{2,1,0:T(8,128)S(1)} %bitcast.33), channel_id=1, replica_groups={{0,1,4,5,8,9,12,13},{16,17,20,21,24,25,28,29},{2,3,6,7,10,11,14,15},{18..., dimensions={0} | all-to-all | bytes 65536 | tf_op jit(solution)/shard_map/all_to_all | solution.py:327
  92.2 2.0 %shard_map.53 = (f32[256,128]{1,0:T(8,128)S(1)}, f32[512,128]{1,0:T(8,128)S(1)}, f32[512,128]{1,0:T(8,128)S(1)}) custom-call(f32[512,2048]{1,0:T(8,128)S(1)} %get-tuple-element.46.score_n.score, f32[512,2048]{1,0:T(8,128)S(1)} %get-tuple-element.53.score_f.score, f32[64,128]{1,0:T(8,128)S(1)} %bitcast.30, f32[128,128]{1,0:T(8,128)S(1)} %bitcast.23), custom_call_target="tpu_custom_call" | custom-call | flops 8388608 | tf_op jit(solution)/shard_map/pallas_call | solution.py:315
  94.1 12.0 %all_to_all.80 = f32[16,16,128]{2,1,0:T(8,128)S(1)} all-to-all(f32[16,16,128]{2,1,0:T(8,128)S(1)} %bitcast.34), channel_id=1, replica_groups={{1,2,33,34,65,66,97,98,17,18,49,50,81,82,113,114},{3,0,35,32,67,64,99,9..., dimensions={0} | all-to-all | bytes 262144 | tf_op jit(solution)/shard_map/all_to_all | solution.py:327
  106.2 1.4 %shard_map.55 = (bf16[128,512]{1,0:T(8,128)(2,1)S(1)}, bf16[128,512]{1,0:T(8,128)(2,1)S(1)}, bf16[128,512]{1,0:T(8,128)(2,1)S(1)}, bf16[128,512]{1,0:T(8,128)(2,1)S(1)}) custom-call(f32[512,2048]{1,0:T(8,128)S(1)} %get-tuple-element.53.score_f.score, f32[256,128]{1,0:T(8,128)S(1)} %bitcast.24, f32[16,128]{1,0:T(8,128)S(1)} %get-tuple-element.55.slot_logs, ...), custom_call_target="tpu_custom_call" | custom-call | flops 4194304 | tf_op jit(solution)/shard_map/pallas_call | solution.py:315
  107.6 0.4 collective-permute-start.9
  108.1 1.8 %collective-permute-start.10 = (bf16[128,512]{1,0:T(8,128)(2,1)S(1)}, bf16[128,512]{1,0:T(8,128)(2,1)S(1)}, u32[]{:S(2)}, u32[]{:S(2)}) collective-permute-start(bf16[128,512]{1,0:T(8,128)(2,1)S(1)} %get-tuple-element.63), channel_id=1, source_target_pairs={{0,9},{1,8},{4,13},{5,12},{8,1},{9,0},{12,5},{13,4},{16,25},{17,24... | collective-permute-start | bytes 393224 | tf_op jit(solution)/shard_map/ppermute | solution.py:331
  109.9 0.6 collective-permute-start.11
  110.4 2.6 %collective-permute-start.12 = (bf16[128,512]{1,0:T(8,128)(2,1)S(1)}, bf16[128,512]{1,0:T(8,128)(2,1)S(1)}, u32[]{:S(2)}, u32[]{:S(2)}) collective-permute-start(bf16[128,512]{1,0:T(8,128)(2,1)S(1)} %get-tuple-element.65), channel_id=1, source_target_pairs={{0,13},{1,12},{4,9},{5,8},{8,5},{9,4},{12,1},{13,0},{16,29},{17,28... | collective-permute-start | bytes 393224 | tf_op jit(solution)/shard_map/ppermute | solution.py:331
  113.0 1.5 %shard_map.54 = (f32[128,512]{1,0:T(8,128)S(1)}, bf16[128,512]{1,0:T(8,128)(2,1)S(1)}, bf16[128,512]{1,0:T(8,128)(2,1)S(1)}, bf16[128,512]{1,0:T(8,128)(2,1)S(1)}) custom-call(f32[512,2048]{1,0:T(8,128)S(1)} %get-tuple-element.46.score_n.score, f32[256,128]{1,0:T(8,128)S(1)} %bitcast.25, f32[16,128]{1,0:T(8,128)S(1)} %get-tuple-element.55.slot_logs, ...), custom_call_target="tpu_custom_call" | custom-call | flops 4194304 | tf_op jit(solution)/shard_map/pallas_call | solution.py:315
  114.5 1.1 collective-permute-start.13
  115.5 0.5 collective-permute-start.14
  116.0 1.8 %collective-permute-start.15 = (bf16[128,512]{1,0:T(8,128)(2,1)S(1)}, bf16[128,512]{1,0:T(8,128)(2,1)S(1)}, u32[]{:S(2)}, u32[]{:S(2)}) collective-permute-start(bf16[128,512]{1,0:T(8,128)(2,1)S(1)} %get-tuple-element.68), channel_id=1, source_target_pairs={{0,12},{1,13},{4,8},{5,9},{8,4},{9,5},{12,0},{13,1},{16,28},{17,29... | collective-permute-start | bytes 393224 | tf_op jit(solution)/shard_map/ppermute | solution.py:331
  117.8 2.6 %collective-permute-done.12 = bf16[128,512]{1,0:T(8,128)(2,1)S(1)} collective-permute-done((bf16[128,512]{1,0:T(8,128)(2,1)S(1)}, bf16[128,512]{1,0:T(8,128)(2,1)S(1)}, u32[]{:S(2)}, u32[]{:S(2)}) %collective-permute-start.12) | collective-permute-done | bytes 131104 | tf_op jit(solution)/shard_map/ppermute | solution.py:331
  120.4 0.3 collective-permute-done.13
  120.7 1.4 %collective-permute-done.14 = bf16[128,512]{1,0:T(8,128)(2,1)S(1)} collective-permute-done((bf16[128,512]{1,0:T(8,128)(2,1)S(1)}, bf16[128,512]{1,0:T(8,128)(2,1)S(1)}, u32[]{:S(2)}, u32[]{:S(2)}) %collective-permute-start.14) | collective-permute-done | bytes 131104 | tf_op jit(solution)/shard_map/ppermute | solution.py:331
  122.1 2.5 %collective-permute-done.15 = bf16[128,512]{1,0:T(8,128)(2,1)S(1)} collective-permute-done((bf16[128,512]{1,0:T(8,128)(2,1)S(1)}, bf16[128,512]{1,0:T(8,128)(2,1)S(1)}, u32[]{:S(2)}, u32[]{:S(2)}) %collective-permute-start.15) | collective-permute-done | bytes 131104 | tf_op jit(solution)/shard_map/ppermute | solution.py:331
  124.6 0.8 add_add_fusion
  (10 shorter events, 0.0 us)
Async XLA Ops:
  2.0 22.8 %all-to-all-start = ((bf16[8,128,512]{2,1,0:T(8,128)(2,1)}), bf16[8,128,512]{2,1,0:T(8,128)(2,1)S(1)}, u32[]{:S(2)}, u32[]{:S(2)}) async-start(bf16[8,128,512]{2,1,0:T(8,128)(2,1)} %tile.2), calls=%async_computation | async-start | bytes 2097152 | tf_op jit(solution)/shard_map/all_to_all | solution.py:327
  10.8 5.8 %collective-permute-start.1 = (bf16[128,512]{1,0:T(8,128)(2,1)}, bf16[128,512]{1,0:T(8,128)(2,1)S(1)}, u32[]{:S(2)}, u32[]{:S(2)}) collective-permute-start(bf16[128,512]{1,0:T(8,128)(2,1)} %lots.1), channel_id=1, source_target_pairs={{0,8},{1,9},{4,12},{5,13},{8,0},{9,1},{12,4},{13,5},{16,24},{17,25... | collective-permute-start | bytes 393224 | tf_op jit(solution)/shard_map/ppermute | solution.py:331
  13.5 5.6 %collective-permute-start = (bf16[128,512]{1,0:T(8,128)(2,1)}, bf16[128,512]{1,0:T(8,128)(2,1)S(1)}, u32[]{:S(2)}, u32[]{:S(2)}) collective-permute-start(bf16[128,512]{1,0:T(8,128)(2,1)} %lots.1), channel_id=1, source_target_pairs={{0,4},{1,5},{4,0},{5,1},{8,12},{9,13},{12,8},{13,9},{16,20},{17,21... | collective-permute-start | bytes 393224 | tf_op jit(solution)/shard_map/ppermute | solution.py:331
  13.8 7.7 %collective-permute-start.2 = (bf16[128,512]{1,0:T(8,128)(2,1)}, bf16[128,512]{1,0:T(8,128)(2,1)S(1)}, u32[]{:S(2)}, u32[]{:S(2)}) collective-permute-start(bf16[128,512]{1,0:T(8,128)(2,1)} %lots.1), channel_id=1, source_target_pairs={{0,12},{1,13},{4,8},{5,9},{8,4},{9,5},{12,0},{13,1},{16,28},{17,29... | collective-permute-start | bytes 393224 | tf_op jit(solution)/shard_map/ppermute | solution.py:331
  14.4 7.2 %collective-permute-start.3 = (bf16[128,512]{1,0:T(8,128)(2,1)}, bf16[128,512]{1,0:T(8,128)(2,1)S(1)}, u32[]{:S(2)}, u32[]{:S(2)}) collective-permute-start(bf16[128,512]{1,0:T(8,128)(2,1)} %lots.1), channel_id=1, source_target_pairs={{0,1},{1,0},{4,5},{5,4},{8,9},{9,8},{12,13},{13,12},{16,17},{17,16... | collective-permute-start | bytes 393224 | tf_op jit(solution)/shard_map/ppermute | solution.py:331
  16.6 5.3 %collective-permute-start.5 = (bf16[128,512]{1,0:T(8,128)(2,1)S(1)}, bf16[128,512]{1,0:T(8,128)(2,1)S(1)}, u32[]{:S(2)}, u32[]{:S(2)}) collective-permute-start(bf16[128,512]{1,0:T(8,128)(2,1)S(1)} %collective-permute-done.1.refs_2_), channel_id=1, source_target_pairs={{0,1},{1,0},{4,5},{5,4},{8,9},{9,8},{12,13},{13,12},{16,17},{17,16... | collective-permute-start | bytes 393224 | tf_op jit(solution)/shard_map/ppermute | solution.py:331
  19.1 4.7 %collective-permute-start.4 = (bf16[128,512]{1,0:T(8,128)(2,1)S(1)}, bf16[128,512]{1,0:T(8,128)(2,1)S(1)}, u32[]{:S(2)}, u32[]{:S(2)}) collective-permute-start(bf16[128,512]{1,0:T(8,128)(2,1)S(1)} %collective-permute-done.refs_1_), channel_id=1, source_target_pairs={{0,1},{1,0},{4,5},{5,4},{8,9},{9,8},{12,13},{13,12},{16,17},{17,16... | collective-permute-start | bytes 393224 | tf_op jit(solution)/shard_map/ppermute | solution.py:331
  19.1 0.9 copy-start
  20.1 0.7 copy-start.1
  20.8 0.7 copy-start.2
  24.8 4.2 %collective-permute-start.6 = (bf16[1024,512]{1,0:T(8,128)(2,1)S(1)}, bf16[1024,512]{1,0:T(8,128)(2,1)S(1)}, u32[]{:S(2)}, u32[]{:S(2)}) collective-permute-start(bf16[1024,512]{1,0:T(8,128)(2,1)S(1)} %bitcast.15), channel_id=1, source_target_pairs={{0,16},{16,0},{1,17},{17,1},{2,18},{18,2},{3,19},{19,3},{4,20},{20... | collective-permute-start | bytes 3145736 | tf_op jit(solution)/shard_map/ppermute | solution.py:359
  26.7 5.1 %collective-permute-start.8 = (bf16[128,512]{1,0:T(8,128)(2,1)S(1)}, bf16[128,512]{1,0:T(8,128)(2,1)S(1)}, u32[]{:S(2)}, u32[]{:S(2)}) collective-permute-start(bf16[128,512]{1,0:T(8,128)(2,1)S(1)} %collective-permute-done.2.refs_3_), channel_id=1, source_target_pairs={{0,1},{1,0},{4,5},{5,4},{8,9},{9,8},{12,13},{13,12},{16,17},{17,16... | collective-permute-start | bytes 393224 | tf_op jit(solution)/shard_map/ppermute | solution.py:331
  26.8 5.0 %collective-permute-start.7 = (f32[8,128]{1,0:T(8,128)S(1)}, f32[8,128]{1,0:T(8,128)S(1)}, u32[]{:S(2)}, u32[]{:S(2)}) collective-permute-start(f32[8,128]{1,0:T(8,128)S(1)} %get-tuple-element.47.near_logs), channel_id=1, source_target_pairs={{1,2},{2,1},{3,0},{0,3},{5,6},{6,5},{7,4},{4,7},{9,10},{10,9},{11,... | collective-permute-start | bytes 12296 | tf_op jit(solution)/shard_map/ppermute | solution.py:360
  107.6 7.9 %collective-permute-start.9 = (bf16[128,512]{1,0:T(8,128)(2,1)S(1)}, bf16[128,512]{1,0:T(8,128)(2,1)S(1)}, u32[]{:S(2)}, u32[]{:S(2)}) collective-permute-start(bf16[128,512]{1,0:T(8,128)(2,1)S(1)} %get-tuple-element.62), channel_id=1, source_target_pairs={{0,1},{1,0},{4,5},{5,4},{8,9},{9,8},{12,13},{13,12},{16,17},{17,16... | collective-permute-start | bytes 393224 | tf_op jit(solution)/shard_map/ppermute | solution.py:331
  108.1 8.0 %collective-permute-start.10 = (bf16[128,512]{1,0:T(8,128)(2,1)S(1)}, bf16[128,512]{1,0:T(8,128)(2,1)S(1)}, u32[]{:S(2)}, u32[]{:S(2)}) collective-permute-start(bf16[128,512]{1,0:T(8,128)(2,1)S(1)} %get-tuple-element.63), channel_id=1, source_target_pairs={{0,9},{1,8},{4,13},{5,12},{8,1},{9,0},{12,5},{13,4},{16,25},{17,24... | collective-permute-start | bytes 393224 | tf_op jit(solution)/shard_map/ppermute | solution.py:331
  109.9 8.0 %collective-permute-start.11 = (bf16[128,512]{1,0:T(8,128)(2,1)S(1)}, bf16[128,512]{1,0:T(8,128)(2,1)S(1)}, u32[]{:S(2)}, u32[]{:S(2)}) collective-permute-start(bf16[128,512]{1,0:T(8,128)(2,1)S(1)} %get-tuple-element.64), channel_id=1, source_target_pairs={{0,5},{1,4},{4,1},{5,0},{8,13},{9,12},{12,9},{13,8},{16,21},{17,20... | collective-permute-start | bytes 393224 | tf_op jit(solution)/shard_map/ppermute | solution.py:331
  110.4 10.0 %collective-permute-start.12 = (bf16[128,512]{1,0:T(8,128)(2,1)S(1)}, bf16[128,512]{1,0:T(8,128)(2,1)S(1)}, u32[]{:S(2)}, u32[]{:S(2)}) collective-permute-start(bf16[128,512]{1,0:T(8,128)(2,1)S(1)} %get-tuple-element.65), channel_id=1, source_target_pairs={{0,13},{1,12},{4,9},{5,8},{8,5},{9,4},{12,1},{13,0},{16,29},{17,28... | collective-permute-start | bytes 393224 | tf_op jit(solution)/shard_map/ppermute | solution.py:331
  114.5 6.2 %collective-permute-start.13 = (bf16[128,512]{1,0:T(8,128)(2,1)S(1)}, bf16[128,512]{1,0:T(8,128)(2,1)S(1)}, u32[]{:S(2)}, u32[]{:S(2)}) collective-permute-start(bf16[128,512]{1,0:T(8,128)(2,1)S(1)} %get-tuple-element.66), channel_id=1, source_target_pairs={{0,8},{1,9},{4,12},{5,13},{8,0},{9,1},{12,4},{13,5},{16,24},{17,25... | collective-permute-start | bytes 393224 | tf_op jit(solution)/shard_map/ppermute | solution.py:331
  115.5 6.6 %collective-permute-start.14 = (bf16[128,512]{1,0:T(8,128)(2,1)S(1)}, bf16[128,512]{1,0:T(8,128)(2,1)S(1)}, u32[]{:S(2)}, u32[]{:S(2)}) collective-permute-start(bf16[128,512]{1,0:T(8,128)(2,1)S(1)} %get-tuple-element.67), channel_id=1, source_target_pairs={{0,4},{1,5},{4,0},{5,1},{8,12},{9,13},{12,8},{13,9},{16,20},{17,21... | collective-permute-start | bytes 393224 | tf_op jit(solution)/shard_map/ppermute | solution.py:331
  116.0 8.5 %collective-permute-start.15 = (bf16[128,512]{1,0:T(8,128)(2,1)S(1)}, bf16[128,512]{1,0:T(8,128)(2,1)S(1)}, u32[]{:S(2)}, u32[]{:S(2)}) collective-permute-start(bf16[128,512]{1,0:T(8,128)(2,1)S(1)} %get-tuple-element.68), channel_id=1, source_target_pairs={{0,12},{1,13},{4,8},{5,9},{8,4},{9,5},{12,0},{13,1},{16,28},{17,29... | collective-permute-start | bytes 393224 | tf_op jit(solution)/shard_map/ppermute | solution.py:331

commit v5 on v4

--- a/solution.py
+++ b/solution.py
@@ -102,7 +102,7 @@
             total[pl.ds(first + row, 8), :] = whole
         return carry
 
-    lax.fori_loop(0, score.shape[0] // (8 * groups_of), step, 0)
+    lax.fori_loop(0, score.shape[0] // (8 * groups_of), step, 0, unroll=4)
 
 
 def row_result(peak, total):
@@ -135,7 +135,7 @@
             sums[pl.ds(i * tiles_of + k, 1), :] = high + jnp.log(whole) * LOG2E
         return carry
 
-    lax.fori_loop(0, sums.shape[0] // tiles_of, step, 0)
+    lax.fori_loop(0, sums.shape[0] // tiles_of, step, 0, unroll=2)
 
 
 def spread_rows(values, wide):

time: 127 us -> 126 us (level)
  no operation moved by 1% of the time
where the time goes in v5:
time: 126 us; the launch traced here: 125 us
  blocking collectives  61.9 us (49%)
  starting transfers between devices  24.4 us (19%)
  Pallas kernels  17.1 us (14%)
  waiting for transfers between devices  15.9 us (13%)
  local copies, waits for them, and re-layouts  4.3 us (3%)
    all_to_all x6, blocking collectives, exchange(): lax.all_to_all(values, ALL, 0, 0, tiled=True, axis_index_groups=members)  61.9 us
    pallas_call x10, Pallas kernels, call(): pl.pallas_call(kernel, out_shape=outs, in_specs=[near] * len(args), out_s...  17.1 us
    ppermute x14, waiting for transfers between devices, to_place(): lax.ppermute(values, ALL, [(group[i], group[i ^ d]) for group in LOT_GROU...  14 us
    ppermute x14, starting transfers between devices, to_place(): lax.ppermute(values, ALL, [(group[i], group[i ^ d]) for group in LOT_GROU...  12.4 us
    all_to_all x1, starting transfers between devices, exchange(): lax.all_to_all(values, ALL, 0, 0, tiled=True, axis_index_groups=members)  8.77 us
  transfers between devices with their start and end apart: 17, of which 11 were waited for; matrix products, arithmetic and copies ran while one was open for 0% of the time, Pallas kernels for 3%

profile of v5, /device:TPU:1, one launch (start us, length us, event | category | flops | bytes accessed | tf_op | source)
XLA Modules:
  0.0 124.6 jit_solution(9733597178058527618)
XLA Ops:
  0.0 2.0 %tile.2 = bf16[8,128,512]{2,1,0:T(8,128)(2,1)} broadcast(bf16[128,512]{1,0:T(8,128)(2,1)} %param.5), dimensions={1,2} | broadcast | bytes 1179648 | tf_op jit(solution)/shard_map/tile | solution.py:339
  2.0 8.8 %all-to-all-start = ((bf16[8,128,512]{2,1,0:T(8,128)(2,1)}), bf16[8,128,512]{2,1,0:T(8,128)(2,1)S(1)}, u32[]{:S(2)}, u32[]{:S(2)}) async-start(bf16[8,128,512]{2,1,0:T(8,128)(2,1)} %tile.2), calls=%async_computation | async-start | bytes 2097152 | tf_op jit(solution)/shard_map/all_to_all | solution.py:327
  10.8 2.7 %collective-permute-start.1 = (bf16[128,512]{1,0:T(8,128)(2,1)}, bf16[128,512]{1,0:T(8,128)(2,1)S(1)}, u32[]{:S(2)}, u32[]{:S(2)}) collective-permute-start(bf16[128,512]{1,0:T(8,128)(2,1)} %lots.1), channel_id=1, source_target_pairs={{0,8},{1,9},{4,12},{5,13},{8,0},{9,1},{12,4},{13,5},{16,24},{17,25... | collective-permute-start | bytes 393224 | tf_op jit(solution)/shard_map/ppermute | solution.py:331
  13.5 0.3 collective-permute-start
  13.8 0.6 collective-permute-start.2
  14.4 0.0 collective-permute-start.3
  14.4 2.2 %collective-permute-done.1.refs_2_ = bf16[128,512]{1,0:T(8,128)(2,1)S(1)} collective-permute-done((bf16[128,512]{1,0:T(8,128)(2,1)}, bf16[128,512]{1,0:T(8,128)(2,1)S(1)}, u32[]{:S(2)}, u32[]{:S(2)}) %collective-permute-start.1) | collective-permute-done | bytes 131104 | tf_op jit(solution)/shard_map/ppermute | solution.py:331
  16.6 2.5 %collective-permute-done.refs_1_ = bf16[128,512]{1,0:T(8,128)(2,1)S(1)} collective-permute-done((bf16[128,512]{1,0:T(8,128)(2,1)}, bf16[128,512]{1,0:T(8,128)(2,1)S(1)}, u32[]{:S(2)}, u32[]{:S(2)}) %collective-permute-start) | collective-permute-done | bytes 131104 | tf_op jit(solution)/shard_map/ppermute | solution.py:331
  19.1 0.0 collective-permute-start.4
  19.1 0.9 copy-done
  20.1 0.7 copy-done.1
  20.8 0.7 copy-done.2
  21.4 0.1 shard_map.46
  21.6 0.3 collective-permute-done.5.refs_2_
  21.9 2.0 %collective-permute-done.4.refs_1_ = bf16[128,512]{1,0:T(8,128)(2,1)S(1)} collective-permute-done((bf16[128,512]{1,0:T(8,128)(2,1)S(1)}, bf16[128,512]{1,0:T(8,128)(2,1)S(1)}, u32[]{:S(2)}, u32[]{:S(2)}) %collective-permute-start.4) | collective-permute-done | bytes 131104 | tf_op jit(solution)/shard_map/ppermute | solution.py:331
  23.9 0.9 all-to-all-done
  24.8 2.0 %collective-permute-start.6 = (bf16[1024,512]{1,0:T(8,128)(2,1)S(1)}, bf16[1024,512]{1,0:T(8,128)(2,1)S(1)}, u32[]{:S(2)}, u32[]{:S(2)}) collective-permute-start(bf16[1024,512]{1,0:T(8,128)(2,1)S(1)} %bitcast.15), channel_id=1, source_target_pairs={{0,16},{16,0},{1,17},{17,1},{2,18},{18,2},{3,19},{19,3},{4,20},{20... | collective-permute-start | bytes 3145736 | tf_op jit(solution)/shard_map/ppermute | solution.py:359
  26.7 0.1 collective-permute-start.8
  26.8 1.2 collective-permute-start.7
  28.0 1.0 collective-permute-done.6.slots_b
  29.0 2.3 %shard_map.47 = (f32[512,2048]{1,0:T(8,128)S(1)}, bf16[512,512]{1,0:T(8,128)(2,1)S(1)}, f32[128,128]{1,0:T(8,128)S(1)}, f32[16,128]{1,0:T(8,128)S(1)}) custom-call(bf16[1024,512]{1,0:T(8,128)(2,1)S(1)} %bitcast.16, bf16[1024,512]{1,0:T(8,128)(2,1)S(1)} %collective-permute-done.6.slots_b, f32[8,128]{1,0:T(8,128)S(1)} %get-tuple-element.41.lot_rows, ...), custom_call_target="tpu_custom_call" | custom-call | flops 4194304 | tf_op jit(solution)/shard_map/pallas_call | solution.py:315
  31.4 0.5 collective-permute-done.8.refs_3_
  31.9 2.3 %shard_map.48 = (f32[512,2048]{1,0:T(8,128)S(1)}, bf16[512,512]{1,0:T(8,128)(2,1)S(1)}, f32[16,128]{1,0:T(8,128)S(1)}, f32[128,128]{1,0:T(8,128)S(1)}) custom-call(bf16[1024,512]{1,0:T(8,128)(2,1)S(1)} %bitcast.17, bf16[1024,512]{1,0:T(8,128)(2,1)S(1)} %collective-permute-done.6.slots_b, f32[8,128]{1,0:T(8,128)S(1)} %get-tuple-element.47.near_logs, ...), custom_call_target="tpu_custom_call" | custom-call | flops 4194304 | tf_op jit(solution)/shard_map/pallas_call | solution.py:315
  34.2 8.9 %all_to_all.75 = f32[8,16,128]{2,1,0:T(8,128)S(1)} all-to-all(f32[8,16,128]{2,1,0:T(8,128)S(1)} %bitcast.35), channel_id=1, replica_groups={{0,1,4,5,8,9,12,13},{16,17,20,21,24,25,28,29},{2,3,6,7,10,11,14,15},{18..., dimensions={0} | all-to-all | bytes 131072 | tf_op jit(solution)/shard_map/all_to_all | solution.py:327
  43.1 1.9 %shard_map.49 = f32[256,128]{1,0:T(8,128)S(1)} custom-call(f32[512,2048]{1,0:T(8,128)S(1)} %get-tuple-element.46.score_n.score, f32[512,2048]{1,0:T(8,128)S(1)} %get-tuple-element.53.score_f.score, f32[128,128]{1,0:T(8,128)S(1)} %bitcast.20, f32[128,128]{1,0:T(8,128)S(1)} %bitcast.21), custom_call_target="tpu_custom_call" | custom-call | flops 8388608 | tf_op jit(solution)/shard_map/pallas_call | solution.py:315
  45.0 13.6 %all_to_all.76 = f32[16,16,128]{2,1,0:T(8,128)S(1)} all-to-all(f32[16,16,128]{2,1,0:T(8,128)S(1)} %bitcast.29), channel_id=1, replica_groups={{1,2,33,34,65,66,97,98,17,18,49,50,81,82,113,114},{3,0,35,32,67,64,99,9..., dimensions={0} | all-to-all | bytes 262144 | tf_op jit(solution)/shard_map/all_to_all | solution.py:327
  58.6 1.8 %shard_map.50 = f32[64,128]{1,0:T(8,128)S(1)} custom-call(f32[512,2048]{1,0:T(8,128)S(1)} %get-tuple-element.46.score_n.score, f32[512,2048]{1,0:T(8,128)S(1)} %get-tuple-element.53.score_f.score, f32[256,128]{1,0:T(8,128)S(1)} %bitcast.26, f32[16,128]{1,0:T(8,128)S(1)} %get-tuple-element.55.slot_logs), custom_call_target="tpu_custom_call" | custom-call | flops 8388608 | tf_op jit(solution)/shard_map/pallas_call | solution.py:315
  60.5 7.4 %all_to_all.77 = f32[8,8,128]{2,1,0:T(8,128)S(1)} all-to-all(f32[8,8,128]{2,1,0:T(8,128)S(1)} %bitcast.31), channel_id=1, replica_groups={{0,1,4,5,8,9,12,13},{16,17,20,21,24,25,28,29},{2,3,6,7,10,11,14,15},{18..., dimensions={0} | all-to-all | bytes 65536 | tf_op jit(solution)/shard_map/all_to_all | solution.py:327
  67.9 1.9 %shard_map.51 = f32[256,128]{1,0:T(8,128)S(1)} custom-call(f32[512,2048]{1,0:T(8,128)S(1)} %get-tuple-element.46.score_n.score, f32[512,2048]{1,0:T(8,128)S(1)} %get-tuple-element.53.score_f.score, f32[64,128]{1,0:T(8,128)S(1)} %bitcast.32, f32[128,128]{1,0:T(8,128)S(1)} %bitcast.22), custom_call_target="tpu_custom_call" | custom-call | flops 8388608 | tf_op jit(solution)/shard_map/pallas_call | solution.py:315
  69.9 12.1 %all_to_all.78 = f32[16,16,128]{2,1,0:T(8,128)S(1)} all-to-all(f32[16,16,128]{2,1,0:T(8,128)S(1)} %bitcast.27), channel_id=1, replica_groups={{1,2,33,34,65,66,97,98,17,18,49,50,81,82,113,114},{3,0,35,32,67,64,99,9..., dimensions={0} | all-to-all | bytes 262144 | tf_op jit(solution)/shard_map/all_to_all | solution.py:327
  82.0 1.8 %shard_map.52 = f32[64,128]{1,0:T(8,128)S(1)} custom-call(f32[512,2048]{1,0:T(8,128)S(1)} %get-tuple-element.46.score_n.score, f32[512,2048]{1,0:T(8,128)S(1)} %get-tuple-element.53.score_f.score, f32[256,128]{1,0:T(8,128)S(1)} %bitcast.28, f32[16,128]{1,0:T(8,128)S(1)} %get-tuple-element.55.slot_logs), custom_call_target="tpu_custom_call" | custom-call | flops 8388608 | tf_op jit(solution)/shard_map/pallas_call | solution.py:315
  83.9 7.8 %all_to_all.79 = f32[8,8,128]{2,1,0:T(8,128)S(1)} all-to-all(f32[8,8,128]{2,1,0:T(8,128)S(1)} %bitcast.33), channel_id=1, replica_groups={{0,1,4,5,8,9,12,13},{16,17,20,21,24,25,28,29},{2,3,6,7,10,11,14,15},{18..., dimensions={0} | all-to-all | bytes 65536 | tf_op jit(solution)/shard_map/all_to_all | solution.py:327
  91.7 2.0 %shard_map.53 = (f32[256,128]{1,0:T(8,128)S(1)}, f32[512,128]{1,0:T(8,128)S(1)}, f32[512,128]{1,0:T(8,128)S(1)}) custom-call(f32[512,2048]{1,0:T(8,128)S(1)} %get-tuple-element.46.score_n.score, f32[512,2048]{1,0:T(8,128)S(1)} %get-tuple-element.53.score_f.score, f32[64,128]{1,0:T(8,128)S(1)} %bitcast.30, f32[128,128]{1,0:T(8,128)S(1)} %bitcast.23), custom_call_target="tpu_custom_call" | custom-call | flops 8388608 | tf_op jit(solution)/shard_map/pallas_call | solution.py:315
  93.6 12.0 %all_to_all.80 = f32[16,16,128]{2,1,0:T(8,128)S(1)} all-to-all(f32[16,16,128]{2,1,0:T(8,128)S(1)} %bitcast.34), channel_id=1, replica_groups={{1,2,33,34,65,66,97,98,17,18,49,50,81,82,113,114},{3,0,35,32,67,64,99,9..., dimensions={0} | all-to-all | bytes 262144 | tf_op jit(solution)/shard_map/all_to_all | solution.py:327
  105.7 1.4 %shard_map.55 = (bf16[128,512]{1,0:T(8,128)(2,1)S(1)}, bf16[128,512]{1,0:T(8,128)(2,1)S(1)}, bf16[128,512]{1,0:T(8,128)(2,1)S(1)}, bf16[128,512]{1,0:T(8,128)(2,1)S(1)}) custom-call(f32[512,2048]{1,0:T(8,128)S(1)} %get-tuple-element.53.score_f.score, f32[256,128]{1,0:T(8,128)S(1)} %bitcast.24, f32[16,128]{1,0:T(8,128)S(1)} %get-tuple-element.55.slot_logs, ...), custom_call_target="tpu_custom_call" | custom-call | flops 4194304 | tf_op jit(solution)/shard_map/pallas_call | solution.py:315
  107.1 0.6 collective-permute-start.9
  107.7 1.6 %collective-permute-start.10 = (bf16[128,512]{1,0:T(8,128)(2,1)S(1)}, bf16[128,512]{1,0:T(8,128)(2,1)S(1)}, u32[]{:S(2)}, u32[]{:S(2)}) collective-permute-start(bf16[128,512]{1,0:T(8,128)(2,1)S(1)} %get-tuple-element.63), channel_id=1, source_target_pairs={{0,9},{1,8},{4,13},{5,12},{8,1},{9,0},{12,5},{13,4},{16,25},{17,24... | collective-permute-start | bytes 393224 | tf_op jit(solution)/shard_map/ppermute | solution.py:331
  109.3 0.8 collective-permute-start.11
  110.1 2.4 %collective-permute-start.12 = (bf16[128,512]{1,0:T(8,128)(2,1)S(1)}, bf16[128,512]{1,0:T(8,128)(2,1)S(1)}, u32[]{:S(2)}, u32[]{:S(2)}) collective-permute-start(bf16[128,512]{1,0:T(8,128)(2,1)S(1)} %get-tuple-element.65), channel_id=1, source_target_pairs={{0,13},{1,12},{4,9},{5,8},{8,5},{9,4},{12,1},{13,0},{16,29},{17,28... | collective-permute-start | bytes 393224 | tf_op jit(solution)/shard_map/ppermute | solution.py:331
  112.5 1.4 %shard_map.54 = (f32[128,512]{1,0:T(8,128)S(1)}, bf16[128,512]{1,0:T(8,128)(2,1)S(1)}, bf16[128,512]{1,0:T(8,128)(2,1)S(1)}, bf16[128,512]{1,0:T(8,128)(2,1)S(1)}) custom-call(f32[512,2048]{1,0:T(8,128)S(1)} %get-tuple-element.46.score_n.score, f32[256,128]{1,0:T(8,128)S(1)} %bitcast.25, f32[16,128]{1,0:T(8,128)S(1)} %get-tuple-element.55.slot_logs, ...), custom_call_target="tpu_custom_call" | custom-call | flops 4194304 | tf_op jit(solution)/shard_map/pallas_call | solution.py:315
  114.0 1.1 collective-permute-start.13
  115.0 0.5 collective-permute-start.14
  115.5 1.8 %collective-permute-start.15 = (bf16[128,512]{1,0:T(8,128)(2,1)S(1)}, bf16[128,512]{1,0:T(8,128)(2,1)S(1)}, u32[]{:S(2)}, u32[]{:S(2)}) collective-permute-start(bf16[128,512]{1,0:T(8,128)(2,1)S(1)} %get-tuple-element.68), channel_id=1, source_target_pairs={{0,12},{1,13},{4,8},{5,9},{8,4},{9,5},{12,0},{13,1},{16,28},{17,29... | collective-permute-start | bytes 393224 | tf_op jit(solution)/shard_map/ppermute | solution.py:331
  117.3 2.7 %collective-permute-done.12 = bf16[128,512]{1,0:T(8,128)(2,1)S(1)} collective-permute-done((bf16[128,512]{1,0:T(8,128)(2,1)S(1)}, bf16[128,512]{1,0:T(8,128)(2,1)S(1)}, u32[]{:S(2)}, u32[]{:S(2)}) %collective-permute-start.12) | collective-permute-done | bytes 131104 | tf_op jit(solution)/shard_map/ppermute | solution.py:331
  120.0 0.2 collective-permute-done.13
  120.2 1.4 %collective-permute-done.14 = bf16[128,512]{1,0:T(8,128)(2,1)S(1)} collective-permute-done((bf16[128,512]{1,0:T(8,128)(2,1)S(1)}, bf16[128,512]{1,0:T(8,128)(2,1)S(1)}, u32[]{:S(2)}, u32[]{:S(2)}) %collective-permute-start.14) | collective-permute-done | bytes 131104 | tf_op jit(solution)/shard_map/ppermute | solution.py:331
  121.6 2.2 %collective-permute-done.15 = bf16[128,512]{1,0:T(8,128)(2,1)S(1)} collective-permute-done((bf16[128,512]{1,0:T(8,128)(2,1)S(1)}, bf16[128,512]{1,0:T(8,128)(2,1)S(1)}, u32[]{:S(2)}, u32[]{:S(2)}) %collective-permute-start.15) | collective-permute-done | bytes 131104 | tf_op jit(solution)/shard_map/ppermute | solution.py:331
  123.8 0.8 add_add_fusion
  (10 shorter events, 0.0 us)
Async XLA Ops:
  2.0 22.8 %all-to-all-start = ((bf16[8,128,512]{2,1,0:T(8,128)(2,1)}), bf16[8,128,512]{2,1,0:T(8,128)(2,1)S(1)}, u32[]{:S(2)}, u32[]{:S(2)}) async-start(bf16[8,128,512]{2,1,0:T(8,128)(2,1)} %tile.2), calls=%async_computation | async-start | bytes 2097152 | tf_op jit(solution)/shard_map/all_to_all | solution.py:327
  10.8 5.8 %collective-permute-start.1 = (bf16[128,512]{1,0:T(8,128)(2,1)}, bf16[128,512]{1,0:T(8,128)(2,1)S(1)}, u32[]{:S(2)}, u32[]{:S(2)}) collective-permute-start(bf16[128,512]{1,0:T(8,128)(2,1)} %lots.1), channel_id=1, source_target_pairs={{0,8},{1,9},{4,12},{5,13},{8,0},{9,1},{12,4},{13,5},{16,24},{17,25... | collective-permute-start | bytes 393224 | tf_op jit(solution)/shard_map/ppermute | solution.py:331
  13.5 5.6 %collective-permute-start = (bf16[128,512]{1,0:T(8,128)(2,1)}, bf16[128,512]{1,0:T(8,128)(2,1)S(1)}, u32[]{:S(2)}, u32[]{:S(2)}) collective-permute-start(bf16[128,512]{1,0:T(8,128)(2,1)} %lots.1), channel_id=1, source_target_pairs={{0,4},{1,5},{4,0},{5,1},{8,12},{9,13},{12,8},{13,9},{16,20},{17,21... | collective-permute-start | bytes 393224 | tf_op jit(solution)/shard_map/ppermute | solution.py:331
  13.8 7.7 %collective-permute-start.2 = (bf16[128,512]{1,0:T(8,128)(2,1)}, bf16[128,512]{1,0:T(8,128)(2,1)S(1)}, u32[]{:S(2)}, u32[]{:S(2)}) collective-permute-start(bf16[128,512]{1,0:T(8,128)(2,1)} %lots.1), channel_id=1, source_target_pairs={{0,12},{1,13},{4,8},{5,9},{8,4},{9,5},{12,0},{13,1},{16,28},{17,29... | collective-permute-start | bytes 393224 | tf_op jit(solution)/shard_map/ppermute | solution.py:331
  14.4 7.2 %collective-permute-start.3 = (bf16[128,512]{1,0:T(8,128)(2,1)}, bf16[128,512]{1,0:T(8,128)(2,1)S(1)}, u32[]{:S(2)}, u32[]{:S(2)}) collective-permute-start(bf16[128,512]{1,0:T(8,128)(2,1)} %lots.1), channel_id=1, source_target_pairs={{0,1},{1,0},{4,5},{5,4},{8,9},{9,8},{12,13},{13,12},{16,17},{17,16... | collective-permute-start | bytes 393224 | tf_op jit(solution)/shard_map/ppermute | solution.py:331
  16.6 5.3 %collective-permute-start.5 = (bf16[128,512]{1,0:T(8,128)(2,1)S(1)}, bf16[128,512]{1,0:T(8,128)(2,1)S(1)}, u32[]{:S(2)}, u32[]{:S(2)}) collective-permute-start(bf16[128,512]{1,0:T(8,128)(2,1)S(1)} %collective-permute-done.1.refs_2_), channel_id=1, source_target_pairs={{0,1},{1,0},{4,5},{5,4},{8,9},{9,8},{12,13},{13,12},{16,17},{17,16... | collective-permute-start | bytes 393224 | tf_op jit(solution)/shard_map/ppermute | solution.py:331
  19.1 4.7 %collective-permute-start.4 = (bf16[128,512]{1,0:T(8,128)(2,1)S(1)}, bf16[128,512]{1,0:T(8,128)(2,1)S(1)}, u32[]{:S(2)}, u32[]{:S(2)}) collective-permute-start(bf16[128,512]{1,0:T(8,128)(2,1)S(1)} %collective-permute-done.refs_1_), channel_id=1, source_target_pairs={{0,1},{1,0},{4,5},{5,4},{8,9},{9,8},{12,13},{13,12},{16,17},{17,16... | collective-permute-start | bytes 393224 | tf_op jit(solution)/shard_map/ppermute | solution.py:331
  19.1 0.9 copy-start
  20.1 0.7 copy-start.1
  20.8 0.7 copy-start.2
  24.8 4.2 %collective-permute-start.6 = (bf16[1024,512]{1,0:T(8,128)(2,1)S(1)}, bf16[1024,512]{1,0:T(8,128)(2,1)S(1)}, u32[]{:S(2)}, u32[]{:S(2)}) collective-permute-start(bf16[1024,512]{1,0:T(8,128)(2,1)S(1)} %bitcast.15), channel_id=1, source_target_pairs={{0,16},{16,0},{1,17},{17,1},{2,18},{18,2},{3,19},{19,3},{4,20},{20... | collective-permute-start | bytes 3145736 | tf_op jit(solution)/shard_map/ppermute | solution.py:359
  26.7 5.1 %collective-permute-start.8 = (bf16[128,512]{1,0:T(8,128)(2,1)S(1)}, bf16[128,512]{1,0:T(8,128)(2,1)S(1)}, u32[]{:S(2)}, u32[]{:S(2)}) collective-permute-start(bf16[128,512]{1,0:T(8,128)(2,1)S(1)} %collective-permute-done.2.refs_3_), channel_id=1, source_target_pairs={{0,1},{1,0},{4,5},{5,4},{8,9},{9,8},{12,13},{13,12},{16,17},{17,16... | collective-permute-start | bytes 393224 | tf_op jit(solution)/shard_map/ppermute | solution.py:331
  26.8 5.0 %collective-permute-start.7 = (f32[8,128]{1,0:T(8,128)S(1)}, f32[8,128]{1,0:T(8,128)S(1)}, u32[]{:S(2)}, u32[]{:S(2)}) collective-permute-start(f32[8,128]{1,0:T(8,128)S(1)} %get-tuple-element.47.near_logs), channel_id=1, source_target_pairs={{1,2},{2,1},{3,0},{0,3},{5,6},{6,5},{7,4},{4,7},{9,10},{10,9},{11,... | collective-permute-start | bytes 12296 | tf_op jit(solution)/shard_map/ppermute | solution.py:360
  107.1 7.9 %collective-permute-start.9 = (bf16[128,512]{1,0:T(8,128)(2,1)S(1)}, bf16[128,512]{1,0:T(8,128)(2,1)S(1)}, u32[]{:S(2)}, u32[]{:S(2)}) collective-permute-start(bf16[128,512]{1,0:T(8,128)(2,1)S(1)} %get-tuple-element.62), channel_id=1, source_target_pairs={{0,1},{1,0},{4,5},{5,4},{8,9},{9,8},{12,13},{13,12},{16,17},{17,16... | collective-permute-start | bytes 393224 | tf_op jit(solution)/shard_map/ppermute | solution.py:331
  107.7 7.8 %collective-permute-start.10 = (bf16[128,512]{1,0:T(8,128)(2,1)S(1)}, bf16[128,512]{1,0:T(8,128)(2,1)S(1)}, u32[]{:S(2)}, u32[]{:S(2)}) collective-permute-start(bf16[128,512]{1,0:T(8,128)(2,1)S(1)} %get-tuple-element.63), channel_id=1, source_target_pairs={{0,9},{1,8},{4,13},{5,12},{8,1},{9,0},{12,5},{13,4},{16,25},{17,24... | collective-permute-start | bytes 393224 | tf_op jit(solution)/shard_map/ppermute | solution.py:331
  109.3 8.0 %collective-permute-start.11 = (bf16[128,512]{1,0:T(8,128)(2,1)S(1)}, bf16[128,512]{1,0:T(8,128)(2,1)S(1)}, u32[]{:S(2)}, u32[]{:S(2)}) collective-permute-start(bf16[128,512]{1,0:T(8,128)(2,1)S(1)} %get-tuple-element.64), channel_id=1, source_target_pairs={{0,5},{1,4},{4,1},{5,0},{8,13},{9,12},{12,9},{13,8},{16,21},{17,20... | collective-permute-start | bytes 393224 | tf_op jit(solution)/shard_map/ppermute | solution.py:331
  110.1 9.9 %collective-permute-start.12 = (bf16[128,512]{1,0:T(8,128)(2,1)S(1)}, bf16[128,512]{1,0:T(8,128)(2,1)S(1)}, u32[]{:S(2)}, u32[]{:S(2)}) collective-permute-start(bf16[128,512]{1,0:T(8,128)(2,1)S(1)} %get-tuple-element.65), channel_id=1, source_target_pairs={{0,13},{1,12},{4,9},{5,8},{8,5},{9,4},{12,1},{13,0},{16,29},{17,28... | collective-permute-start | bytes 393224 | tf_op jit(solution)/shard_map/ppermute | solution.py:331
  114.0 6.2 %collective-permute-start.13 = (bf16[128,512]{1,0:T(8,128)(2,1)S(1)}, bf16[128,512]{1,0:T(8,128)(2,1)S(1)}, u32[]{:S(2)}, u32[]{:S(2)}) collective-permute-start(bf16[128,512]{1,0:T(8,128)(2,1)S(1)} %get-tuple-element.66), channel_id=1, source_target_pairs={{0,8},{1,9},{4,12},{5,13},{8,0},{9,1},{12,4},{13,5},{16,24},{17,25... | collective-permute-start | bytes 393224 | tf_op jit(solution)/shard_map/ppermute | solution.py:331
  115.0 6.6 %collective-permute-start.14 = (bf16[128,512]{1,0:T(8,128)(2,1)S(1)}, bf16[128,512]{1,0:T(8,128)(2,1)S(1)}, u32[]{:S(2)}, u32[]{:S(2)}) collective-permute-start(bf16[128,512]{1,0:T(8,128)(2,1)S(1)} %get-tuple-element.67), channel_id=1, source_target_pairs={{0,4},{1,5},{4,0},{5,1},{8,12},{9,13},{12,8},{13,9},{16,20},{17,21... | collective-permute-start | bytes 393224 | tf_op jit(solution)/shard_map/ppermute | solution.py:331
  115.5 8.2 %collective-permute-start.15 = (bf16[128,512]{1,0:T(8,128)(2,1)S(1)}, bf16[128,512]{1,0:T(8,128)(2,1)S(1)}, u32[]{:S(2)}, u32[]{:S(2)}) collective-permute-start(bf16[128,512]{1,0:T(8,128)(2,1)S(1)} %get-tuple-element.68), channel_id=1, source_target_pairs={{0,12},{1,13},{4,8},{5,9},{8,4},{9,5},{12,0},{13,1},{16,28},{17,29... | collective-permute-start | bytes 393224 | tf_op jit(solution)/shard_map/ppermute | solution.py:331

commit v6 on v5

--- a/solution.py
+++ b/solution.py
@@ -410,7 +410,8 @@
         )
         parts.update(zip(steps, outs, strict=True))
     arrived = [to_place(parts[d], d) for d in ORDER]
-    return parts[0] + sum(part.astype(f32) for part in arrived)
+    early = lax.optimization_barrier(parts[0] + sum(part.astype(f32) for part in arrived[:4]))
+    return early + sum(part.astype(f32) for part in arrived[4:])
 
 
 def solution(mesh):

time: 126 us -> 126 us (level)
  no operation moved by 1% of the time
where the time goes in v6:
time: 126 us; the launch traced here: 125 us
  blocking collectives  61.9 us (49%)
  starting transfers between devices  24.4 us (19%)
  Pallas kernels  17.1 us (14%)
  waiting for transfers between devices  15.8 us (13%)
  local copies, waits for them, and re-layouts  4.3 us (3%)
    all_to_all x6, blocking collectives, exchange(): lax.all_to_all(values, ALL, 0, 0, tiled=True, axis_index_groups=members)  61.9 us
    pallas_call x10, Pallas kernels, call(): pl.pallas_call(kernel, out_shape=outs, in_specs=[near] * len(args), out_s...  17.1 us
    ppermute x14, waiting for transfers between devices, to_place(): lax.ppermute(values, ALL, [(group[i], group[i ^ d]) for group in LOT_GROU...  13.9 us
    ppermute x14, starting transfers between devices, to_place(): lax.ppermute(values, ALL, [(group[i], group[i ^ d]) for group in LOT_GROU...  12.4 us
    all_to_all x1, starting transfers between devices, exchange(): lax.all_to_all(values, ALL, 0, 0, tiled=True, axis_index_groups=members)  8.77 us
  transfers between devices with their start and end apart: 17, of which 11 were waited for; matrix products, arithmetic and copies ran while one was open for 0% of the time, Pallas kernels for 3%

profile of v6, /device:TPU:1, one launch (start us, length us, event | category | flops | bytes accessed | tf_op | source)
XLA Modules:
  0.0 124.6 jit_solution(7528037541421809780)
XLA Ops:
  0.0 2.0 %tile.2 = bf16[8,128,512]{2,1,0:T(8,128)(2,1)} broadcast(bf16[128,512]{1,0:T(8,128)(2,1)} %param.5), dimensions={1,2} | broadcast | bytes 1179648 | tf_op jit(solution)/shard_map/tile | solution.py:339
  2.0 8.8 %all-to-all-start = ((bf16[8,128,512]{2,1,0:T(8,128)(2,1)}), bf16[8,128,512]{2,1,0:T(8,128)(2,1)S(1)}, u32[]{:S(2)}, u32[]{:S(2)}) async-start(bf16[8,128,512]{2,1,0:T(8,128)(2,1)} %tile.2), calls=%async_computation | async-start | bytes 2097152 | tf_op jit(solution)/shard_map/all_to_all | solution.py:327
  10.8 2.7 %collective-permute-start.1 = (bf16[128,512]{1,0:T(8,128)(2,1)}, bf16[128,512]{1,0:T(8,128)(2,1)S(1)}, u32[]{:S(2)}, u32[]{:S(2)}) collective-permute-start(bf16[128,512]{1,0:T(8,128)(2,1)} %lots.1), channel_id=1, source_target_pairs={{0,8},{1,9},{4,12},{5,13},{8,0},{9,1},{12,4},{13,5},{16,24},{17,25... | collective-permute-start | bytes 393224 | tf_op jit(solution)/shard_map/ppermute | solution.py:331
  13.5 0.3 collective-permute-start
  13.8 0.6 collective-permute-start.2
  14.4 0.0 collective-permute-start.3
  14.4 2.2 %collective-permute-done.1.refs_2_ = bf16[128,512]{1,0:T(8,128)(2,1)S(1)} collective-permute-done((bf16[128,512]{1,0:T(8,128)(2,1)}, bf16[128,512]{1,0:T(8,128)(2,1)S(1)}, u32[]{:S(2)}, u32[]{:S(2)}) %collective-permute-start.1) | collective-permute-done | bytes 131104 | tf_op jit(solution)/shard_map/ppermute | solution.py:331
  16.6 2.5 %collective-permute-done.refs_1_ = bf16[128,512]{1,0:T(8,128)(2,1)S(1)} collective-permute-done((bf16[128,512]{1,0:T(8,128)(2,1)}, bf16[128,512]{1,0:T(8,128)(2,1)S(1)}, u32[]{:S(2)}, u32[]{:S(2)}) %collective-permute-start) | collective-permute-done | bytes 131104 | tf_op jit(solution)/shard_map/ppermute | solution.py:331
  19.1 0.9 copy-done
  20.1 0.7 copy-done.1
  20.8 0.7 copy-done.2
  21.4 0.1 shard_map.46
  21.6 0.3 collective-permute-done.5.refs_2_
  21.9 2.0 %collective-permute-done.4.refs_1_ = bf16[128,512]{1,0:T(8,128)(2,1)S(1)} collective-permute-done((bf16[128,512]{1,0:T(8,128)(2,1)S(1)}, bf16[128,512]{1,0:T(8,128)(2,1)S(1)}, u32[]{:S(2)}, u32[]{:S(2)}) %collective-permute-start.4) | collective-permute-done | bytes 131104 | tf_op jit(solution)/shard_map/ppermute | solution.py:331
  23.9 0.9 all-to-all-done
  24.8 2.0 %collective-permute-start.6 = (bf16[1024,512]{1,0:T(8,128)(2,1)S(1)}, bf16[1024,512]{1,0:T(8,128)(2,1)S(1)}, u32[]{:S(2)}, u32[]{:S(2)}) collective-permute-start(bf16[1024,512]{1,0:T(8,128)(2,1)S(1)} %bitcast.15), channel_id=1, source_target_pairs={{0,16},{16,0},{1,17},{17,1},{2,18},{18,2},{3,19},{19,3},{4,20},{20... | collective-permute-start | bytes 3145736 | tf_op jit(solution)/shard_map/ppermute | solution.py:359
  26.7 0.1 collective-permute-start.8
  26.8 1.2 collective-permute-start.7
  28.0 1.0 collective-permute-done.6.slots_b
  29.0 2.3 %shard_map.47 = (f32[512,2048]{1,0:T(8,128)S(1)}, bf16[512,512]{1,0:T(8,128)(2,1)S(1)}, f32[128,128]{1,0:T(8,128)S(1)}, f32[16,128]{1,0:T(8,128)S(1)}) custom-call(bf16[1024,512]{1,0:T(8,128)(2,1)S(1)} %bitcast.16, bf16[1024,512]{1,0:T(8,128)(2,1)S(1)} %collective-permute-done.6.slots_b, f32[8,128]{1,0:T(8,128)S(1)} %get-tuple-element.41.lot_rows, ...), custom_call_target="tpu_custom_call" | custom-call | flops 4194304 | tf_op jit(solution)/shard_map/pallas_call | solution.py:315
  31.4 0.5 collective-permute-done.8.refs_3_
  31.9 2.3 %shard_map.48 = (f32[512,2048]{1,0:T(8,128)S(1)}, bf16[512,512]{1,0:T(8,128)(2,1)S(1)}, f32[16,128]{1,0:T(8,128)S(1)}, f32[128,128]{1,0:T(8,128)S(1)}) custom-call(bf16[1024,512]{1,0:T(8,128)(2,1)S(1)} %bitcast.17, bf16[1024,512]{1,0:T(8,128)(2,1)S(1)} %collective-permute-done.6.slots_b, f32[8,128]{1,0:T(8,128)S(1)} %get-tuple-element.47.near_logs, ...), custom_call_target="tpu_custom_call" | custom-call | flops 4194304 | tf_op jit(solution)/shard_map/pallas_call | solution.py:315
  34.2 8.9 %all_to_all.75 = f32[8,16,128]{2,1,0:T(8,128)S(1)} all-to-all(f32[8,16,128]{2,1,0:T(8,128)S(1)} %bitcast.35), channel_id=1, replica_groups={{0,1,4,5,8,9,12,13},{16,17,20,21,24,25,28,29},{2,3,6,7,10,11,14,15},{18..., dimensions={0} | all-to-all | bytes 131072 | tf_op jit(solution)/shard_map/all_to_all | solution.py:327
  43.1 1.9 %shard_map.49 = f32[256,128]{1,0:T(8,128)S(1)} custom-call(f32[512,2048]{1,0:T(8,128)S(1)} %get-tuple-element.46.score_n.score, f32[512,2048]{1,0:T(8,128)S(1)} %get-tuple-element.53.score_f.score, f32[128,128]{1,0:T(8,128)S(1)} %bitcast.20, f32[128,128]{1,0:T(8,128)S(1)} %bitcast.21), custom_call_target="tpu_custom_call" | custom-call | flops 8388608 | tf_op jit(solution)/shard_map/pallas_call | solution.py:315
  45.0 13.6 %all_to_all.76 = f32[16,16,128]{2,1,0:T(8,128)S(1)} all-to-all(f32[16,16,128]{2,1,0:T(8,128)S(1)} %bitcast.29), channel_id=1, replica_groups={{1,2,33,34,65,66,97,98,17,18,49,50,81,82,113,114},{3,0,35,32,67,64,99,9..., dimensions={0} | all-to-all | bytes 262144 | tf_op jit(solution)/shard_map/all_to_all | solution.py:327
  58.6 1.8 %shard_map.50 = f32[64,128]{1,0:T(8,128)S(1)} custom-call(f32[512,2048]{1,0:T(8,128)S(1)} %get-tuple-element.46.score_n.score, f32[512,2048]{1,0:T(8,128)S(1)} %get-tuple-element.53.score_f.score, f32[256,128]{1,0:T(8,128)S(1)} %bitcast.26, f32[16,128]{1,0:T(8,128)S(1)} %get-tuple-element.55.slot_logs), custom_call_target="tpu_custom_call" | custom-call | flops 8388608 | tf_op jit(solution)/shard_map/pallas_call | solution.py:315
  60.5 7.4 %all_to_all.77 = f32[8,8,128]{2,1,0:T(8,128)S(1)} all-to-all(f32[8,8,128]{2,1,0:T(8,128)S(1)} %bitcast.31), channel_id=1, replica_groups={{0,1,4,5,8,9,12,13},{16,17,20,21,24,25,28,29},{2,3,6,7,10,11,14,15},{18..., dimensions={0} | all-to-all | bytes 65536 | tf_op jit(solution)/shard_map/all_to_all | solution.py:327
  67.9 1.9 %shard_map.51 = f32[256,128]{1,0:T(8,128)S(1)} custom-call(f32[512,2048]{1,0:T(8,128)S(1)} %get-tuple-element.46.score_n.score, f32[512,2048]{1,0:T(8,128)S(1)} %get-tuple-element.53.score_f.score, f32[64,128]{1,0:T(8,128)S(1)} %bitcast.32, f32[128,128]{1,0:T(8,128)S(1)} %bitcast.22), custom_call_target="tpu_custom_call" | custom-call | flops 8388608 | tf_op jit(solution)/shard_map/pallas_call | solution.py:315
  69.9 12.1 %all_to_all.78 = f32[16,16,128]{2,1,0:T(8,128)S(1)} all-to-all(f32[16,16,128]{2,1,0:T(8,128)S(1)} %bitcast.27), channel_id=1, replica_groups={{1,2,33,34,65,66,97,98,17,18,49,50,81,82,113,114},{3,0,35,32,67,64,99,9..., dimensions={0} | all-to-all | bytes 262144 | tf_op jit(solution)/shard_map/all_to_all | solution.py:327
  82.0 1.8 %shard_map.52 = f32[64,128]{1,0:T(8,128)S(1)} custom-call(f32[512,2048]{1,0:T(8,128)S(1)} %get-tuple-element.46.score_n.score, f32[512,2048]{1,0:T(8,128)S(1)} %get-tuple-element.53.score_f.score, f32[256,128]{1,0:T(8,128)S(1)} %bitcast.28, f32[16,128]{1,0:T(8,128)S(1)} %get-tuple-element.55.slot_logs), custom_call_target="tpu_custom_call" | custom-call | flops 8388608 | tf_op jit(solution)/shard_map/pallas_call | solution.py:315
  83.9 7.8 %all_to_all.79 = f32[8,8,128]{2,1,0:T(8,128)S(1)} all-to-all(f32[8,8,128]{2,1,0:T(8,128)S(1)} %bitcast.33), channel_id=1, replica_groups={{0,1,4,5,8,9,12,13},{16,17,20,21,24,25,28,29},{2,3,6,7,10,11,14,15},{18..., dimensions={0} | all-to-all | bytes 65536 | tf_op jit(solution)/shard_map/all_to_all | solution.py:327
  91.7 2.0 %shard_map.53 = (f32[256,128]{1,0:T(8,128)S(1)}, f32[512,128]{1,0:T(8,128)S(1)}, f32[512,128]{1,0:T(8,128)S(1)}) custom-call(f32[512,2048]{1,0:T(8,128)S(1)} %get-tuple-element.46.score_n.score, f32[512,2048]{1,0:T(8,128)S(1)} %get-tuple-element.53.score_f.score, f32[64,128]{1,0:T(8,128)S(1)} %bitcast.30, f32[128,128]{1,0:T(8,128)S(1)} %bitcast.23), custom_call_target="tpu_custom_call" | custom-call | flops 8388608 | tf_op jit(solution)/shard_map/pallas_call | solution.py:315
  93.6 12.0 %all_to_all.80 = f32[16,16,128]{2,1,0:T(8,128)S(1)} all-to-all(f32[16,16,128]{2,1,0:T(8,128)S(1)} %bitcast.34), channel_id=1, replica_groups={{1,2,33,34,65,66,97,98,17,18,49,50,81,82,113,114},{3,0,35,32,67,64,99,9..., dimensions={0} | all-to-all | bytes 262144 | tf_op jit(solution)/shard_map/all_to_all | solution.py:327
  105.7 1.4 %shard_map.55 = (bf16[128,512]{1,0:T(8,128)(2,1)S(1)}, bf16[128,512]{1,0:T(8,128)(2,1)S(1)}, bf16[128,512]{1,0:T(8,128)(2,1)S(1)}, bf16[128,512]{1,0:T(8,128)(2,1)S(1)}) custom-call(f32[512,2048]{1,0:T(8,128)S(1)} %get-tuple-element.53.score_f.score, f32[256,128]{1,0:T(8,128)S(1)} %bitcast.24, f32[16,128]{1,0:T(8,128)S(1)} %get-tuple-element.55.slot_logs, ...), custom_call_target="tpu_custom_call" | custom-call | flops 4194304 | tf_op jit(solution)/shard_map/pallas_call | solution.py:315
  107.1 0.6 collective-permute-start.9
  107.7 1.6 %collective-permute-start.10 = (bf16[128,512]{1,0:T(8,128)(2,1)S(1)}, bf16[128,512]{1,0:T(8,128)(2,1)S(1)}, u32[]{:S(2)}, u32[]{:S(2)}) collective-permute-start(bf16[128,512]{1,0:T(8,128)(2,1)S(1)} %get-tuple-element.63), channel_id=1, source_target_pairs={{0,9},{1,8},{4,13},{5,12},{8,1},{9,0},{12,5},{13,4},{16,25},{17,24... | collective-permute-start | bytes 393224 | tf_op jit(solution)/shard_map/ppermute | solution.py:331
  109.3 0.8 collective-permute-start.11
  110.1 2.4 %collective-permute-start.12 = (bf16[128,512]{1,0:T(8,128)(2,1)S(1)}, bf16[128,512]{1,0:T(8,128)(2,1)S(1)}, u32[]{:S(2)}, u32[]{:S(2)}) collective-permute-start(bf16[128,512]{1,0:T(8,128)(2,1)S(1)} %get-tuple-element.65), channel_id=1, source_target_pairs={{0,13},{1,12},{4,9},{5,8},{8,5},{9,4},{12,1},{13,0},{16,29},{17,28... | collective-permute-start | bytes 393224 | tf_op jit(solution)/shard_map/ppermute | solution.py:331
  112.5 1.4 %shard_map.54 = (f32[128,512]{1,0:T(8,128)S(1)}, bf16[128,512]{1,0:T(8,128)(2,1)S(1)}, bf16[128,512]{1,0:T(8,128)(2,1)S(1)}, bf16[128,512]{1,0:T(8,128)(2,1)S(1)}) custom-call(f32[512,2048]{1,0:T(8,128)S(1)} %get-tuple-element.46.score_n.score, f32[256,128]{1,0:T(8,128)S(1)} %bitcast.25, f32[16,128]{1,0:T(8,128)S(1)} %get-tuple-element.55.slot_logs, ...), custom_call_target="tpu_custom_call" | custom-call | flops 4194304 | tf_op jit(solution)/shard_map/pallas_call | solution.py:315
  114.0 1.1 collective-permute-start.13
  115.0 0.5 collective-permute-start.14
  115.5 1.8 %collective-permute-start.15 = (bf16[128,512]{1,0:T(8,128)(2,1)S(1)}, bf16[128,512]{1,0:T(8,128)(2,1)S(1)}, u32[]{:S(2)}, u32[]{:S(2)}) collective-permute-start(bf16[128,512]{1,0:T(8,128)(2,1)S(1)} %get-tuple-element.68), channel_id=1, source_target_pairs={{0,12},{1,13},{4,8},{5,9},{8,4},{9,5},{12,0},{13,1},{16,28},{17,29... | collective-permute-start | bytes 393224 | tf_op jit(solution)/shard_map/ppermute | solution.py:331
  117.3 2.7 %collective-permute-done.12 = bf16[128,512]{1,0:T(8,128)(2,1)S(1)} collective-permute-done((bf16[128,512]{1,0:T(8,128)(2,1)S(1)}, bf16[128,512]{1,0:T(8,128)(2,1)S(1)}, u32[]{:S(2)}, u32[]{:S(2)}) %collective-permute-start.12) | collective-permute-done | bytes 131104 | tf_op jit(solution)/shard_map/ppermute | solution.py:331
  120.0 0.1 add_add_fusion.1
  120.1 0.1 collective-permute-done.13
  120.2 1.4 %collective-permute-done.14 = bf16[128,512]{1,0:T(8,128)(2,1)S(1)} collective-permute-done((bf16[128,512]{1,0:T(8,128)(2,1)S(1)}, bf16[128,512]{1,0:T(8,128)(2,1)S(1)}, u32[]{:S(2)}, u32[]{:S(2)}) %collective-permute-start.14) | collective-permute-done | bytes 131104 | tf_op jit(solution)/shard_map/ppermute | solution.py:331
  121.6 2.2 %collective-permute-done.15 = bf16[128,512]{1,0:T(8,128)(2,1)S(1)} collective-permute-done((bf16[128,512]{1,0:T(8,128)(2,1)S(1)}, bf16[128,512]{1,0:T(8,128)(2,1)S(1)}, u32[]{:S(2)}, u32[]{:S(2)}) %collective-permute-start.15) | collective-permute-done | bytes 131104 | tf_op jit(solution)/shard_map/ppermute | solution.py:331
  123.8 0.8 add_add_fusion
  (11 shorter events, 0.0 us)
Async XLA Ops:
  2.0 22.8 %all-to-all-start = ((bf16[8,128,512]{2,1,0:T(8,128)(2,1)}), bf16[8,128,512]{2,1,0:T(8,128)(2,1)S(1)}, u32[]{:S(2)}, u32[]{:S(2)}) async-start(bf16[8,128,512]{2,1,0:T(8,128)(2,1)} %tile.2), calls=%async_computation | async-start | bytes 2097152 | tf_op jit(solution)/shard_map/all_to_all | solution.py:327
  10.8 5.8 %collective-permute-start.1 = (bf16[128,512]{1,0:T(8,128)(2,1)}, bf16[128,512]{1,0:T(8,128)(2,1)S(1)}, u32[]{:S(2)}, u32[]{:S(2)}) collective-permute-start(bf16[128,512]{1,0:T(8,128)(2,1)} %lots.1), channel_id=1, source_target_pairs={{0,8},{1,9},{4,12},{5,13},{8,0},{9,1},{12,4},{13,5},{16,24},{17,25... | collective-permute-start | bytes 393224 | tf_op jit(solution)/shard_map/ppermute | solution.py:331
  13.5 5.6 %collective-permute-start = (bf16[128,512]{1,0:T(8,128)(2,1)}, bf16[128,512]{1,0:T(8,128)(2,1)S(1)}, u32[]{:S(2)}, u32[]{:S(2)}) collective-permute-start(bf16[128,512]{1,0:T(8,128)(2,1)} %lots.1), channel_id=1, source_target_pairs={{0,4},{1,5},{4,0},{5,1},{8,12},{9,13},{12,8},{13,9},{16,20},{17,21... | collective-permute-start | bytes 393224 | tf_op jit(solution)/shard_map/ppermute | solution.py:331
  13.8 7.7 %collective-permute-start.2 = (bf16[128,512]{1,0:T(8,128)(2,1)}, bf16[128,512]{1,0:T(8,128)(2,1)S(1)}, u32[]{:S(2)}, u32[]{:S(2)}) collective-permute-start(bf16[128,512]{1,0:T(8,128)(2,1)} %lots.1), channel_id=1, source_target_pairs={{0,12},{1,13},{4,8},{5,9},{8,4},{9,5},{12,0},{13,1},{16,28},{17,29... | collective-permute-start | bytes 393224 | tf_op jit(solution)/shard_map/ppermute | solution.py:331
  14.4 7.2 %collective-permute-start.3 = (bf16[128,512]{1,0:T(8,128)(2,1)}, bf16[128,512]{1,0:T(8,128)(2,1)S(1)}, u32[]{:S(2)}, u32[]{:S(2)}) collective-permute-start(bf16[128,512]{1,0:T(8,128)(2,1)} %lots.1), channel_id=1, source_target_pairs={{0,1},{1,0},{4,5},{5,4},{8,9},{9,8},{12,13},{13,12},{16,17},{17,16... | collective-permute-start | bytes 393224 | tf_op jit(solution)/shard_map/ppermute | solution.py:331
  16.6 5.3 %collective-permute-start.5 = (bf16[128,512]{1,0:T(8,128)(2,1)S(1)}, bf16[128,512]{1,0:T(8,128)(2,1)S(1)}, u32[]{:S(2)}, u32[]{:S(2)}) collective-permute-start(bf16[128,512]{1,0:T(8,128)(2,1)S(1)} %collective-permute-done.1.refs_2_), channel_id=1, source_target_pairs={{0,1},{1,0},{4,5},{5,4},{8,9},{9,8},{12,13},{13,12},{16,17},{17,16... | collective-permute-start | bytes 393224 | tf_op jit(solution)/shard_map/ppermute | solution.py:331
  19.1 4.7 %collective-permute-start.4 = (bf16[128,512]{1,0:T(8,128)(2,1)S(1)}, bf16[128,512]{1,0:T(8,128)(2,1)S(1)}, u32[]{:S(2)}, u32[]{:S(2)}) collective-permute-start(bf16[128,512]{1,0:T(8,128)(2,1)S(1)} %collective-permute-done.refs_1_), channel_id=1, source_target_pairs={{0,1},{1,0},{4,5},{5,4},{8,9},{9,8},{12,13},{13,12},{16,17},{17,16... | collective-permute-start | bytes 393224 | tf_op jit(solution)/shard_map/ppermute | solution.py:331
  19.1 0.9 copy-start
  20.1 0.7 copy-start.1
  20.8 0.7 copy-start.2
  24.8 4.2 %collective-permute-start.6 = (bf16[1024,512]{1,0:T(8,128)(2,1)S(1)}, bf16[1024,512]{1,0:T(8,128)(2,1)S(1)}, u32[]{:S(2)}, u32[]{:S(2)}) collective-permute-start(bf16[1024,512]{1,0:T(8,128)(2,1)S(1)} %bitcast.15), channel_id=1, source_target_pairs={{0,16},{16,0},{1,17},{17,1},{2,18},{18,2},{3,19},{19,3},{4,20},{20... | collective-permute-start | bytes 3145736 | tf_op jit(solution)/shard_map/ppermute | solution.py:359
  26.7 5.1 %collective-permute-start.8 = (bf16[128,512]{1,0:T(8,128)(2,1)S(1)}, bf16[128,512]{1,0:T(8,128)(2,1)S(1)}, u32[]{:S(2)}, u32[]{:S(2)}) collective-permute-start(bf16[128,512]{1,0:T(8,128)(2,1)S(1)} %collective-permute-done.2.refs_3_), channel_id=1, source_target_pairs={{0,1},{1,0},{4,5},{5,4},{8,9},{9,8},{12,13},{13,12},{16,17},{17,16... | collective-permute-start | bytes 393224 | tf_op jit(solution)/shard_map/ppermute | solution.py:331
  26.8 5.0 %collective-permute-start.7 = (f32[8,128]{1,0:T(8,128)S(1)}, f32[8,128]{1,0:T(8,128)S(1)}, u32[]{:S(2)}, u32[]{:S(2)}) collective-permute-start(f32[8,128]{1,0:T(8,128)S(1)} %get-tuple-element.47.near_logs), channel_id=1, source_target_pairs={{1,2},{2,1},{3,0},{0,3},{5,6},{6,5},{7,4},{4,7},{9,10},{10,9},{11,... | collective-permute-start | bytes 12296 | tf_op jit(solution)/shard_map/ppermute | solution.py:360
  107.1 7.9 %collective-permute-start.9 = (bf16[128,512]{1,0:T(8,128)(2,1)S(1)}, bf16[128,512]{1,0:T(8,128)(2,1)S(1)}, u32[]{:S(2)}, u32[]{:S(2)}) collective-permute-start(bf16[128,512]{1,0:T(8,128)(2,1)S(1)} %get-tuple-element.62), channel_id=1, source_target_pairs={{0,1},{1,0},{4,5},{5,4},{8,9},{9,8},{12,13},{13,12},{16,17},{17,16... | collective-permute-start | bytes 393224 | tf_op jit(solution)/shard_map/ppermute | solution.py:331
  107.7 7.8 %collective-permute-start.10 = (bf16[128,512]{1,0:T(8,128)(2,1)S(1)}, bf16[128,512]{1,0:T(8,128)(2,1)S(1)}, u32[]{:S(2)}, u32[]{:S(2)}) collective-permute-start(bf16[128,512]{1,0:T(8,128)(2,1)S(1)} %get-tuple-element.63), channel_id=1, source_target_pairs={{0,9},{1,8},{4,13},{5,12},{8,1},{9,0},{12,5},{13,4},{16,25},{17,24... | collective-permute-start | bytes 393224 | tf_op jit(solution)/shard_map/ppermute | solution.py:331
  109.3 8.0 %collective-permute-start.11 = (bf16[128,512]{1,0:T(8,128)(2,1)S(1)}, bf16[128,512]{1,0:T(8,128)(2,1)S(1)}, u32[]{:S(2)}, u32[]{:S(2)}) collective-permute-start(bf16[128,512]{1,0:T(8,128)(2,1)S(1)} %get-tuple-element.64), channel_id=1, source_target_pairs={{0,5},{1,4},{4,1},{5,0},{8,13},{9,12},{12,9},{13,8},{16,21},{17,20... | collective-permute-start | bytes 393224 | tf_op jit(solution)/shard_map/ppermute | solution.py:331
  110.1 9.9 %collective-permute-start.12 = (bf16[128,512]{1,0:T(8,128)(2,1)S(1)}, bf16[128,512]{1,0:T(8,128)(2,1)S(1)}, u32[]{:S(2)}, u32[]{:S(2)}) collective-permute-start(bf16[128,512]{1,0:T(8,128)(2,1)S(1)} %get-tuple-element.65), channel_id=1, source_target_pairs={{0,13},{1,12},{4,9},{5,8},{8,5},{9,4},{12,1},{13,0},{16,29},{17,28... | collective-permute-start | bytes 393224 | tf_op jit(solution)/shard_map/ppermute | solution.py:331
  114.0 6.2 %collective-permute-start.13 = (bf16[128,512]{1,0:T(8,128)(2,1)S(1)}, bf16[128,512]{1,0:T(8,128)(2,1)S(1)}, u32[]{:S(2)}, u32[]{:S(2)}) collective-permute-start(bf16[128,512]{1,0:T(8,128)(2,1)S(1)} %get-tuple-element.66), channel_id=1, source_target_pairs={{0,8},{1,9},{4,12},{5,13},{8,0},{9,1},{12,4},{13,5},{16,24},{17,25... | collective-permute-start | bytes 393224 | tf_op jit(solution)/shard_map/ppermute | solution.py:331
  115.0 6.6 %collective-permute-start.14 = (bf16[128,512]{1,0:T(8,128)(2,1)S(1)}, bf16[128,512]{1,0:T(8,128)(2,1)S(1)}, u32[]{:S(2)}, u32[]{:S(2)}) collective-permute-start(bf16[128,512]{1,0:T(8,128)(2,1)S(1)} %get-tuple-element.67), channel_id=1, source_target_pairs={{0,4},{1,5},{4,0},{5,1},{8,12},{9,13},{12,8},{13,9},{16,20},{17,21... | collective-permute-start | bytes 393224 | tf_op jit(solution)/shard_map/ppermute | solution.py:331
  115.5 8.2 %collective-permute-start.15 = (bf16[128,512]{1,0:T(8,128)(2,1)S(1)}, bf16[128,512]{1,0:T(8,128)(2,1)S(1)}, u32[]{:S(2)}, u32[]{:S(2)}) collective-permute-start(bf16[128,512]{1,0:T(8,128)(2,1)S(1)} %get-tuple-element.68), channel_id=1, source_target_pairs={{0,12},{1,13},{4,8},{5,9},{8,4},{9,5},{12,0},{13,1},{16,28},{17,29... | collective-permute-start | bytes 393224 | tf_op jit(solution)/shard_map/ppermute | solution.py:331
